TPU v7x, 32 devices: a whole 2x2x4 slice. The times are simulated.
32 devices in a mesh: section: 2 (over core), tensor: 4 (over y, x), seq: 4 (over z).
Axes of the slice: x: 2, y: 2, z: 4, core: 2. Of those that a mesh axis runs over, the one named last changes fastest.
Arguments:
- tokens: bfloat16 [2, 4096, 768], P(None, 'seq'), may hold values from -6 to 6
- cotangent: bfloat16 [2, 4096, 768], P(None, 'seq'), may hold values from -6 to 6
- lengths: int32 [2, 3], replicated, may hold values from 1 to 3584, 4096 in all within a row
- selected: int32 [2, 2, 12, 64], P('section', None, 'tensor'), may hold values from -1 to 46, as said below
- input_weight: bfloat16 [2, 768, 3, 768], P('section', None, None, 'tensor'), may hold values from -0.21875 to 0.21875
- input_bias: bfloat16 [2, 2, 768], P('section', None, 'tensor'), may hold values from -3 to 3
- score_weight: bfloat16 [2, 768, 12], P('section', None, 'tensor'), may hold values from -0.21875 to 0.21875
- output_weight: bfloat16 [2, 768, 768], P('section', 'tensor'), may hold values from -0.625 to 0.625
- output_bias: bfloat16 [2, 768], P('section'), may hold values from -3 to 3
- up_weight: bfloat16 [2, 768, 3072], P('section', None, 'tensor'), may hold values from -0.21875 to 0.21875
- up_bias: bfloat16 [2, 3072], P('section', 'tensor'), may hold values from -3 to 3
- down_weight: bfloat16 [2, 3072, 768], P('section', 'tensor'), may hold values from -0.15625 to 0.15625
- down_bias: bfloat16 [2, 768], P('section'), may hold values from -3 to 3
- norm_gain: bfloat16 [2, 2, 768], P('section'), may hold values from 0.5 to 1.5
- norm_bias: bfloat16 [2, 2, 768], P('section'), may hold values from -2 to 2
Outputs:
- layer_out: bfloat16 [2, 2, 4096, 768], P('section', None, 'seq')
- input_grad: bfloat16 [2, 2, 4096, 768], P('section', None, 'seq')
- input_weight_grad: float32 [2, 768, 3, 768], P('section', 'seq', None, 'tensor')
- input_bias_grad: float32 [2, 2, 768], P('section', None, ('tensor', 'seq'))
- score_weight_grad: float32 [2, 768, 12], P('section', 'seq', 'tensor')
- output_weight_grad: float32 [2, 768, 768], P('section', 'tensor', 'seq')
- output_bias_grad: float32 [2, 768], P('section', 'seq')
- up_weight_grad: float32 [2, 768, 3072], P('section', 'seq', 'tensor')
- up_bias_grad: float32 [2, 3072], P('section', ('tensor', 'seq'))
- down_weight_grad: float32 [2, 3072, 768], P('section', 'tensor', 'seq')
- down_bias_grad: float32 [2, 768], P('section', 'seq')
- norm_gain_grad: float32 [2, 2, 768], P('section', None, 'seq')
- norm_bias_grad: float32 [2, 2, 768], P('section', None, 'seq')
Inputs may be any that keep to these rules, and one draw needn't show every extreme that they name: The lengths of the 3 documents packed into each micro-batch, in order; they sum to 4096. `selected`: entry [l, m, h, t] is -1 (no tile) or a key tile that lies on an earlier device along seq than query tile t (tile // 16 < t // 16), and is never the last tile of its device. Among the entries of one layer and micro-batch, of the 3 heads of one tensor index and of the 16 query tiles of one device, at most 16 name tiles of the same device.
All inputs are finite; a program needn't handle non-finite values.
Results may differ from a plain program's by a relative error of at most 0.033.
Values may be sent and summed in bfloat16 or wider, within the bound.
A program may use at most 192 MiB of HBM per device.

v0:
```python
import jax
import jax.numpy as jnp
from jax import lax
from jax.sharding import PartitionSpec as P

TILE = 64


MASKED = -1e30
EPSILON = 1e-05


def from_behind(value, axis, steps):
    count = lax.axis_size(axis)
    leading, last = (max(0, -steps), min(count, count - steps))
    return lax.ppermute(value, axis, [(source, source + steps) for source in range(leading, last)])


def layer_norm(vector, norm_gain, norm_shift):
    average = jnp.mean(vector, axis=-1, keepdims=True)
    centred = vector - average
    spread = jnp.mean(centred * centred, axis=-1, keepdims=True)
    return centred * lax.rsqrt(spread + EPSILON) * norm_gain + norm_shift


def gelu_tanh(vector):
    return jax.nn.gelu(vector, approximate=True)


def doc_index(position, doc_ends):
    return jnp.sum((position[..., None] >= doc_ends).astype(jnp.int32), axis=-1)


def to_tiles(matrix, head_count, tile_size):
    rows_total, columns = matrix.shape
    return matrix.reshape(
        rows_total // tile_size, tile_size, head_count, columns // head_count
    ).transpose(2, 0, 1, 3)


def from_tiles(blocks):
    head_count, tile_count, tile_size, head_size = blocks.shape
    return blocks.transpose(1, 2, 0, 3).reshape(tile_count * tile_size, head_count * head_size)


def own_rows(matrix):
    share = matrix.shape[0] // lax.axis_size("tensor")
    picked_rows = lax.dynamic_slice_in_dim(matrix, lax.axis_index("tensor") * share, share, 0)
    return picked_rows


def reduce_rows(partial_sum):
    total = lax.psum_scatter(
        partial_sum.astype(jnp.bfloat16), "tensor", scatter_dimension=0, tiled=True
    ).astype(jnp.float32)
    return total


def spread_rows(rows_low):
    whole = lax.all_gather(rows_low, "tensor", axis=0, tiled=True)
    return whole


def reduce_grads(partial_grad):
    total = lax.psum_scatter(
        partial_grad.astype(jnp.bfloat16), "tensor", scatter_dimension=0, tiled=True
    ).astype(jnp.float32)
    return total


def spread_grads(rows_low):
    whole = lax.all_gather(rows_low, "tensor", axis=0, tiled=True)
    return whole


def routing(chosen, seq_rank, seq_count, capacity):
    head_count, tiles_total = chosen.shape
    tiles_dev = tiles_total // seq_count
    slot_count = head_count * tiles_dev
    grouped = (
        chosen.reshape(head_count, seq_count, tiles_dev)
        .transpose(1, 0, 2)
        .reshape(seq_count, slot_count)
    )
    owners = jnp.where(grouped >= 0, grouped // tiles_dev, -1)
    mine_flag = (owners == seq_rank).astype(jnp.int32)
    mine_order = jnp.cumsum(mine_flag, axis=1) - 1
    places = lax.broadcasted_iota(jnp.int32, (seq_count, capacity, slot_count), 1)
    slot_ids = lax.broadcasted_iota(jnp.int32, (seq_count, capacity, slot_count), 2)
    matched = (mine_flag[:, None, :] == 1) & (mine_order[:, None, :] == places)
    present = jnp.any(matched, axis=2)
    picked_slot = jnp.sum(jnp.where(matched, slot_ids, 0), axis=2)
    wanted = jnp.take_along_axis(grouped, picked_slot, axis=1)
    source = picked_slot // tiles_dev * tiles_dev + wanted - seq_rank * tiles_dev
    source = jnp.where(present, source, 0)
    own_slots = lax.dynamic_index_in_dim(grouped, seq_rank, 0, keepdims=False)
    live_slots = own_slots >= 0
    target = jnp.where(live_slots, own_slots // tiles_dev, 0)
    peer_ids = lax.broadcasted_iota(jnp.int32, (slot_count, seq_count), 1)
    to_peer = ((target[:, None] == peer_ids) & live_slots[:, None]).astype(jnp.int32)
    place_in = jnp.sum((jnp.cumsum(to_peer, axis=0) - 1) * to_peer, axis=1)
    arrive = target * capacity + place_in
    return (
        source,
        present,
        arrive,
        live_slots.reshape(head_count, tiles_dev),
        own_slots.reshape(head_count, tiles_dev),
    )


def fetch_tiles(key_values, gate_tiles, source, present, arrive):
    head_count, tile_count, tile_size, pair_width = key_values.shape
    seq_count, capacity = source.shape
    pair_rows = key_values.reshape(head_count * tile_count, tile_size, pair_width)
    gate_rows = gate_tiles.reshape(head_count * tile_count, tile_size)
    sending = jnp.where(
        present[:, :, None, None], pair_rows[source], jnp.zeros((), key_values.dtype)
    )
    sending_gate = jnp.where(
        present[:, :, None], gate_rows[source], jnp.zeros((), gate_tiles.dtype)
    )
    arrived, arrived_gate = (
        lax.all_to_all(sending, "seq", split_axis=0, concat_axis=0, tiled=True),
        lax.all_to_all(sending_gate, "seq", split_axis=0, concat_axis=0, tiled=True),
    )
    picked = arrived.reshape(seq_count * capacity, tile_size, pair_width)[arrive]
    picked_gate = arrived_gate.reshape(seq_count * capacity, tile_size)[arrive]
    return (
        picked.reshape(head_count, tile_count, tile_size, pair_width),
        picked_gate.reshape(head_count, tile_count, tile_size),
    )


def gather_keys(key_values, gate_tiles, edge_pair, edge_gate, picked, picked_gate):
    before = jnp.concatenate([edge_pair[:, None], key_values[:, :-1]], axis=1)
    before_gate = jnp.concatenate([edge_gate[:, None], gate_tiles[:, :-1]], axis=1)
    return (
        jnp.concatenate([key_values, before, picked], axis=2),
        jnp.concatenate([gate_tiles, before_gate, picked_gate], axis=2),
    )


def key_masks(seq_rank, tile_count, tile_size, own_slots, live_slots, doc_ends):
    head_count = own_slots.shape[0]
    offsets = lax.broadcasted_iota(jnp.int32, (tile_count, tile_size), 1)
    tile_ids = lax.broadcasted_iota(jnp.int32, (tile_count, tile_size), 0)
    query_pos = seq_rank * tile_count * tile_size + tile_ids * tile_size + offsets
    before_pos = query_pos - tile_size
    query_doc = doc_index(query_pos, doc_ends)
    before_doc = doc_index(jnp.maximum(before_pos, 0), doc_ends)
    own_ok = (query_pos[:, :, None] >= query_pos[:, None, :]) & (
        query_doc[:, :, None] == query_doc[:, None, :]
    )
    before_ok = (
        (query_pos[:, :, None] - before_pos[:, None, :] < tile_size)
        & (before_pos[:, None, :] >= 0)
        & (query_doc[:, :, None] == before_doc[:, None, :])
    )
    chosen_pos = jnp.maximum(own_slots, 0)[:, :, None] * tile_size + offsets[None]
    chosen_doc = doc_index(chosen_pos, doc_ends)
    chosen_ok = live_slots[:, :, None, None] & (
        query_doc[None, :, :, None] == chosen_doc[:, :, None, :]
    )
    shape_all = (head_count, tile_count, tile_size, tile_size)
    return jnp.concatenate(
        [jnp.broadcast_to(own_ok, shape_all), jnp.broadcast_to(before_ok, shape_all), chosen_ok],
        axis=3,
    )


def attention_scores(query_tiles, key_set, gate_set, allowed, scale_factor):
    head_size = query_tiles.shape[3]
    raw_scores = jnp.einsum(
        "hutd,hukd->hutk", query_tiles, key_set[..., :head_size], preferred_element_type=jnp.float32
    )
    scored = scale_factor * raw_scores + gate_set.astype(jnp.float32)[:, :, None, :]
    return jnp.where(allowed, scored, MASKED)


def layer_forward(layer_in, params, chosen, doc_ends, capacity, tile_size):
    (
        input_weight,
        input_bias,
        score_weight,
        output_weight,
        output_bias,
        up_weight,
        up_bias,
        down_weight,
        down_bias,
        norm_gain,
        norm_bias,
    ) = params
    tok_count, model_width = layer_in.shape
    head_count = score_weight.shape[1]
    inner_width = input_weight.shape[2]
    head_size = inner_width // head_count
    tile_count = tok_count // tile_size
    seq_rank = lax.axis_index("seq")
    seq_count = lax.axis_size("seq")
    residual = layer_in.astype(jnp.float32)
    normed = layer_norm(
        residual, norm_gain[0].astype(jnp.float32), norm_bias[0].astype(jnp.float32)
    ).astype(jnp.bfloat16)
    projected = jnp.dot(
        normed,
        input_weight.reshape(model_width, 3 * inner_width),
        preferred_element_type=jnp.float32,
    ).reshape(tok_count, 3, inner_width)
    queries = (projected[:, 0] + input_bias[0].astype(jnp.float32)).astype(jnp.bfloat16)
    key_proj = projected[:, 1].astype(jnp.bfloat16)
    value_proj = (projected[:, 2] + input_bias[1].astype(jnp.float32)).astype(jnp.bfloat16)
    key_score = jnp.dot(normed, score_weight, preferred_element_type=jnp.float32)
    key_gate = jax.nn.log_sigmoid(key_score).astype(jnp.bfloat16)
    query_tiles = to_tiles(queries, head_count, tile_size)
    key_values = jnp.concatenate(
        [to_tiles(key_proj, head_count, tile_size), to_tiles(value_proj, head_count, tile_size)],
        axis=3,
    )
    gate_tiles = key_gate.reshape(tile_count, tile_size, head_count).transpose(2, 0, 1)
    edge_pair, edge_gate = from_behind((key_values[:, -1], gate_tiles[:, -1]), "seq", 1)
    source, present, arrive, live_slots, own_slots = routing(chosen, seq_rank, seq_count, capacity)
    picked, picked_gate = fetch_tiles(key_values, gate_tiles, source, present, arrive)
    key_set, gate_set = gather_keys(
        key_values, gate_tiles, edge_pair, edge_gate, picked, picked_gate
    )
    allowed = key_masks(seq_rank, tile_count, tile_size, own_slots, live_slots, doc_ends)
    scale_factor = head_size ** (-0.5)
    scores = attention_scores(query_tiles, key_set, gate_set, allowed, scale_factor)
    row_top = jnp.max(scores, axis=-1, keepdims=True)
    exponent = jnp.exp(scores - row_top)
    row_total = jnp.sum(exponent, axis=-1, keepdims=True)
    probability = (exponent / row_total).astype(jnp.bfloat16)
    mixed_out = jnp.einsum(
        "hutk,hukd->hutd", probability, key_set[..., head_size:], preferred_element_type=jnp.float32
    )
    attended = from_tiles(mixed_out.astype(jnp.bfloat16))
    middle = (
        own_rows(residual)
        + reduce_rows(jnp.dot(attended, output_weight, preferred_element_type=jnp.float32))
        + output_bias.astype(jnp.float32)
    )
    normed_two = spread_rows(
        layer_norm(
            middle, norm_gain[1].astype(jnp.float32), norm_bias[1].astype(jnp.float32)
        ).astype(jnp.bfloat16)
    )
    up_proj = jnp.dot(normed_two, up_weight, preferred_element_type=jnp.float32) + up_bias.astype(
        jnp.float32
    )
    active = gelu_tanh(up_proj).astype(jnp.bfloat16)
    result = (
        middle
        + reduce_rows(jnp.dot(active, down_weight, preferred_element_type=jnp.float32))
        + down_bias.astype(jnp.float32)
    )
    result_low = spread_rows(result.astype(jnp.bfloat16))
    stored = {
        "layer_in": layer_in,
        "normed": normed,
        "key_score": key_score,
        "query_tiles": query_tiles,
        "key_values": key_values,
        "gate_tiles": gate_tiles,
        "edge_pair": edge_pair,
        "edge_gate": edge_gate,
        "row_top": row_top,
        "row_total": row_total,
        "attended": attended,
        "middle": middle,
        "normed_two": normed_two,
        "up_proj": up_proj,
        "active": active,
        "chosen": chosen,
        "doc_ends": doc_ends,
    }
    return (result_low, stored)


def layer_backward(cotan_now, params, stored, capacity, tile_size):
    (
        input_weight,
        input_bias,
        score_weight,
        output_weight,
        output_bias,
        up_weight,
        up_bias,
        down_weight,
        down_bias,
        norm_gain,
        norm_bias,
    ) = params
    layer_in = stored["layer_in"]
    tok_count, model_width = layer_in.shape
    head_count = score_weight.shape[1]
    inner_width = input_weight.shape[2]
    head_size = inner_width // head_count
    tile_count = tok_count // tile_size
    seq_rank = lax.axis_index("seq")
    seq_count = lax.axis_size("seq")
    cotan_low = cotan_now.astype(jnp.bfloat16)
    down_bias_grad = jnp.sum(cotan_now, axis=0)
    down_weight_grad = jnp.einsum(
        "tf,td->fd", stored["active"], cotan_low, preferred_element_type=jnp.float32
    )
    grad_active = jnp.einsum(
        "td,fd->tf", cotan_low, down_weight, preferred_element_type=jnp.float32
    )
    _, gelu_pull = jax.vjp(gelu_tanh, stored["up_proj"])
    grad_up = gelu_pull(grad_active)[0].astype(jnp.bfloat16)
    up_bias_grad = jnp.sum(grad_up.astype(jnp.float32), axis=0)
    up_weight_grad = jnp.einsum(
        "td,tf->df", stored["normed_two"], grad_up, preferred_element_type=jnp.float32
    )
    grad_normed_two = reduce_grads(
        jnp.einsum("tf,df->td", grad_up, up_weight, preferred_element_type=jnp.float32)
    )
    _, norm_pull_two = jax.vjp(
        layer_norm,
        stored["middle"],
        norm_gain[1].astype(jnp.float32),
        norm_bias[1].astype(jnp.float32),
    )
    grad_middle, gain_grad_one, shift_grad_one = norm_pull_two(grad_normed_two)
    grad_middle = own_rows(cotan_now) + grad_middle
    output_bias_grad = jnp.sum(grad_middle, axis=0)
    branch_low = spread_grads(grad_middle.astype(jnp.bfloat16))
    output_weight_grad = jnp.einsum(
        "th,td->hd", stored["attended"], branch_low, preferred_element_type=jnp.float32
    )
    grad_attended = jnp.einsum(
        "td,hd->th", branch_low, output_weight, preferred_element_type=jnp.float32
    ).astype(jnp.bfloat16)
    grad_tiles = to_tiles(grad_attended, head_count, tile_size)
    source, present, arrive, live_slots, own_slots = routing(
        stored["chosen"], seq_rank, seq_count, capacity
    )
    picked, picked_gate = fetch_tiles(
        stored["key_values"], stored["gate_tiles"], source, present, arrive
    )
    key_set, gate_set = gather_keys(
        stored["key_values"],
        stored["gate_tiles"],
        stored["edge_pair"],
        stored["edge_gate"],
        picked,
        picked_gate,
    )
    allowed = key_masks(seq_rank, tile_count, tile_size, own_slots, live_slots, stored["doc_ends"])
    scale_factor = head_size ** (-0.5)
    scores = attention_scores(stored["query_tiles"], key_set, gate_set, allowed, scale_factor)
    probs_full = jnp.exp(scores - stored["row_top"]) / stored["row_total"]
    grad_probs = jnp.einsum(
        "hutd,hukd->hutk", grad_tiles, key_set[..., head_size:], preferred_element_type=jnp.float32
    )
    row_dot = jnp.sum(probs_full * grad_probs, axis=-1, keepdims=True)
    grad_scores = (probs_full * (grad_probs - row_dot)).astype(jnp.bfloat16)
    grad_query = (
        scale_factor
        * jnp.einsum(
            "hutk,hukd->hutd",
            grad_scores,
            key_set[..., :head_size],
            preferred_element_type=jnp.float32,
        )
    ).astype(jnp.bfloat16)
    grad_keys = scale_factor * jnp.einsum(
        "hutk,hutd->hukd", grad_scores, stored["query_tiles"], preferred_element_type=jnp.float32
    )
    grad_values = jnp.einsum(
        "hutk,hutd->hukd",
        probs_full.astype(jnp.bfloat16),
        grad_tiles,
        preferred_element_type=jnp.float32,
    )
    grad_set = jnp.concatenate([grad_keys, grad_values], axis=3)
    grad_gates = jnp.sum(grad_scores.astype(jnp.float32), axis=2)
    own_grad = grad_set[:, :, :tile_size]
    before_grad = grad_set[:, :, tile_size : 2 * tile_size]
    chosen_grad = grad_set[:, :, 2 * tile_size :]
    own_gate_grad = grad_gates[:, :, :tile_size]
    before_gate_grad = grad_gates[:, :, tile_size : 2 * tile_size]
    chosen_gate_grad = grad_gates[:, :, 2 * tile_size :]
    edge_grad, edge_gate_grad = (
        from_behind(before_grad[:, 0].astype(jnp.bfloat16), "seq", -1).astype(jnp.float32),
        from_behind(before_gate_grad[:, 0].astype(jnp.bfloat16), "seq", -1).astype(jnp.float32),
    )
    local_grad = own_grad + jnp.concatenate([before_grad[:, 1:], edge_grad[:, None]], axis=1)
    local_gate_grad = own_gate_grad + jnp.concatenate(
        [before_gate_grad[:, 1:], edge_gate_grad[:, None]], axis=1
    )
    slot_count = head_count * tile_count
    pair_width = 2 * head_size
    live_flat = live_slots.reshape(slot_count)
    chosen_flat = jnp.where(
        live_flat[:, None, None], chosen_grad.reshape(slot_count, tile_size, pair_width), 0.0
    )
    chosen_gate_flat = jnp.where(
        live_flat[:, None], chosen_gate_grad.reshape(slot_count, tile_size), 0.0
    )
    outgoing = (
        jnp.zeros((seq_count * capacity, tile_size, pair_width), jnp.float32)
        .at[arrive]
        .add(chosen_flat)
    )
    outgoing_gate = (
        jnp.zeros((seq_count * capacity, tile_size), jnp.float32).at[arrive].add(chosen_gate_flat)
    )
    returned, returned_gate = (
        lax.all_to_all(
            outgoing.reshape(seq_count, capacity, tile_size, pair_width).astype(jnp.bfloat16),
            "seq",
            split_axis=0,
            concat_axis=0,
            tiled=True,
        ).astype(jnp.float32),
        lax.all_to_all(
            outgoing_gate.reshape(seq_count, capacity, tile_size).astype(jnp.bfloat16),
            "seq",
            split_axis=0,
            concat_axis=0,
            tiled=True,
        ).astype(jnp.float32),
    )
    returned = jnp.where(present[:, :, None, None], returned, 0.0).reshape(
        seq_count * capacity, tile_size, pair_width
    )
    returned_gate = jnp.where(present[:, :, None], returned_gate, 0.0).reshape(
        seq_count * capacity, tile_size
    )
    rows_flat = source.reshape(seq_count * capacity)
    pair_grad = local_grad.reshape(slot_count, tile_size, pair_width).at[rows_flat].add(returned)
    pair_grad = pair_grad.reshape(head_count, tile_count, tile_size, pair_width)
    gate_grad = local_gate_grad.reshape(slot_count, tile_size).at[rows_flat].add(returned_gate)
    gate_grad = gate_grad.reshape(head_count, tile_count, tile_size)
    grad_key = from_tiles(pair_grad[..., :head_size]).astype(jnp.bfloat16)
    grad_value = from_tiles(pair_grad[..., head_size:]).astype(jnp.bfloat16)
    grad_query_rows = from_tiles(grad_query)
    grad_gate_rows = gate_grad.transpose(1, 2, 0).reshape(tok_count, head_count)
    _, sigmoid_pull = jax.vjp(jax.nn.log_sigmoid, stored["key_score"])
    grad_score = sigmoid_pull(grad_gate_rows)[0].astype(jnp.bfloat16)
    grad_projected = jnp.stack([grad_query_rows, grad_key, grad_value], axis=1)
    input_weight_grad = jnp.einsum(
        "td,tcf->dcf", stored["normed"], grad_projected, preferred_element_type=jnp.float32
    )
    input_bias_grad = jnp.stack(
        [
            jnp.sum(grad_query_rows.astype(jnp.float32), axis=0),
            jnp.sum(grad_value.astype(jnp.float32), axis=0),
        ]
    )
    score_weight_grad = jnp.einsum(
        "td,th->dh", stored["normed"], grad_score, preferred_element_type=jnp.float32
    )
    grad_normed = jnp.einsum(
        "tcf,dcf->td", grad_projected, input_weight, preferred_element_type=jnp.float32
    ) + jnp.einsum("th,dh->td", grad_score, score_weight, preferred_element_type=jnp.float32)
    grad_normed = reduce_grads(grad_normed)
    _, norm_pull_one = jax.vjp(
        layer_norm,
        own_rows(layer_in.astype(jnp.float32)),
        norm_gain[0].astype(jnp.float32),
        norm_bias[0].astype(jnp.float32),
    )
    grad_residual, gain_grad_zero, shift_grad_zero = norm_pull_one(grad_normed)
    grad_input = grad_middle + grad_residual
    grad_low = spread_grads(grad_input.astype(jnp.bfloat16))
    layer_grads = (
        input_weight_grad,
        input_bias_grad,
        score_weight_grad,
        output_weight_grad,
        output_bias_grad,
        up_weight_grad,
        up_bias_grad,
        down_weight_grad,
        down_bias_grad,
        jnp.stack([gain_grad_zero, gain_grad_one]),
        jnp.stack([shift_grad_zero, shift_grad_one]),
    )
    return (grad_low, layer_grads)


def body(
    tokens,
    cotangent,
    lengths,
    selected,
    input_weight,
    input_bias,
    score_weight,
    output_weight,
    output_bias,
    up_weight,
    up_bias,
    down_weight,
    down_bias,
    norm_gain,
    norm_bias,
):
    micro_count, tok_count, model_width = tokens.shape
    section_count = lax.axis_size("section")
    section_rank = lax.axis_index("section")
    seq_count = lax.axis_size("seq")
    head_count = score_weight.shape[2]
    tile_count = tok_count // TILE
    reach = seq_count - 1
    capacity = (head_count * tile_count + reach - 1) // reach
    params = (
        input_weight[0],
        input_bias[0],
        score_weight[0],
        output_weight[0],
        output_bias[0],
        up_weight[0],
        up_bias[0],
        down_weight[0],
        down_bias[0],
        norm_gain[0],
        norm_bias[0],
    )
    chosen_all = selected[0]
    step_count = micro_count + section_count - 1
    incoming = jnp.zeros((tok_count, model_width), jnp.bfloat16)
    layer_out = jnp.zeros((micro_count, tok_count, model_width), jnp.bfloat16)
    kept_steps = []
    for step_index in range(step_count):
        micro_index = step_index - section_rank
        active_step = (micro_index >= 0) & (micro_index < micro_count)
        safe_index = jnp.clip(micro_index, 0, micro_count - 1)
        first_in = lax.dynamic_index_in_dim(tokens, safe_index, 0, keepdims=False)
        layer_in = jnp.where(section_rank == 0, first_in, incoming)
        chosen = lax.dynamic_index_in_dim(chosen_all, safe_index, 0, keepdims=False)
        doc_ends = jnp.cumsum(lax.dynamic_index_in_dim(lengths, safe_index, 0, keepdims=False))[:-1]
        result, stored = layer_forward(layer_in, params, chosen, doc_ends, capacity, TILE)
        kept_steps.append(stored)
        updated = lax.dynamic_update_index_in_dim(layer_out, result, safe_index, 0)
        layer_out = jnp.where(active_step, updated, layer_out)
        if step_index + 1 < step_count:
            incoming = from_behind(result, "section", 1)
    grad_totals = tuple((jnp.zeros(weight_arg.shape, jnp.float32) for weight_arg in params))
    input_grad = jnp.zeros((micro_count, tok_count, model_width), jnp.bfloat16)
    returning = jnp.zeros((tok_count, model_width), jnp.bfloat16)
    for step_index in range(step_count):
        micro_index = micro_count - 1 - step_index + (section_count - 1 - section_rank)
        active_step = (micro_index >= 0) & (micro_index < micro_count)
        safe_index = jnp.clip(micro_index, 0, micro_count - 1)
        last_cotan = lax.dynamic_index_in_dim(cotangent, safe_index, 0, keepdims=False)
        cotan_now = jnp.where(section_rank == section_count - 1, last_cotan, returning).astype(
            jnp.float32
        )
        cotan_now = jnp.where(active_step, cotan_now, 0.0)
        grad_low, layer_grads = layer_backward(
            cotan_now, params, kept_steps[step_count - 1 - step_index], capacity, TILE
        )
        grad_totals = tuple(
            (total_now + grad_now for total_now, grad_now in zip(grad_totals, layer_grads))
        )
        updated = lax.dynamic_update_index_in_dim(input_grad, grad_low, safe_index, 0)
        input_grad = jnp.where(active_step, updated, input_grad)
        if step_index + 1 < step_count:
            returning = from_behind(grad_low, "section", -1)
    stat_sums = lax.psum((grad_totals[4], grad_totals[9], grad_totals[10]), "tensor")
    merged = (
        grad_totals[0],
        grad_totals[1],
        grad_totals[2],
        grad_totals[3],
        stat_sums[0],
        grad_totals[5],
        grad_totals[6],
        grad_totals[7],
        grad_totals[8],
        stat_sums[1],
        stat_sums[2],
    )
    reduced = (
        lax.psum_scatter(
            merged[0].astype(jnp.bfloat16), "seq", scatter_dimension=0, tiled=True
        ).astype(jnp.float32),
        lax.psum_scatter(
            merged[1].astype(jnp.bfloat16), "seq", scatter_dimension=1, tiled=True
        ).astype(jnp.float32),
        lax.psum_scatter(
            merged[2].astype(jnp.bfloat16), "seq", scatter_dimension=0, tiled=True
        ).astype(jnp.float32),
        lax.psum_scatter(
            merged[3].astype(jnp.bfloat16), "seq", scatter_dimension=1, tiled=True
        ).astype(jnp.float32),
        lax.psum_scatter(
            merged[4].astype(jnp.bfloat16), "seq", scatter_dimension=0, tiled=True
        ).astype(jnp.float32),
        lax.psum_scatter(
            merged[5].astype(jnp.bfloat16), "seq", scatter_dimension=0, tiled=True
        ).astype(jnp.float32),
        lax.psum_scatter(
            merged[6].astype(jnp.bfloat16), "seq", scatter_dimension=0, tiled=True
        ).astype(jnp.float32),
        lax.psum_scatter(
            merged[7].astype(jnp.bfloat16), "seq", scatter_dimension=1, tiled=True
        ).astype(jnp.float32),
        lax.psum_scatter(
            merged[8].astype(jnp.bfloat16), "seq", scatter_dimension=0, tiled=True
        ).astype(jnp.float32),
        lax.psum_scatter(
            merged[9].astype(jnp.bfloat16), "seq", scatter_dimension=1, tiled=True
        ).astype(jnp.float32),
        lax.psum_scatter(
            merged[10].astype(jnp.bfloat16), "seq", scatter_dimension=1, tiled=True
        ).astype(jnp.float32),
    )
    return (
        layer_out[None],
        input_grad[None],
        reduced[0][None],
        reduced[1][None],
        reduced[2][None],
        reduced[3][None],
        reduced[4][None],
        reduced[5][None],
        reduced[6][None],
        reduced[7][None],
        reduced[8][None],
        reduced[9][None],
        reduced[10][None],
    )


def solution(mesh):
    return jax.shard_map(
        body,
        mesh=mesh,
        in_specs=(
            P(None, "seq", None),
            P(None, "seq", None),
            P(),
            P("section", None, "tensor", None),
            P("section", None, None, "tensor"),
            P("section", None, "tensor"),
            P("section", None, "tensor"),
            P("section", "tensor", None),
            P("section", None),
            P("section", None, "tensor"),
            P("section", "tensor"),
            P("section", "tensor", None),
            P("section", None),
            P("section", None, None),
            P("section", None, None),
        ),
        out_specs=(
            P("section", None, "seq", None),
            P("section", None, "seq", None),
            P("section", "seq", None, "tensor"),
            P("section", None, ("tensor", "seq")),
            P("section", "seq", "tensor"),
            P("section", "tensor", "seq"),
            P("section", "seq"),
            P("section", "seq", "tensor"),
            P("section", ("tensor", "seq")),
            P("section", "tensor", "seq"),
            P("section", "seq"),
            P("section", None, "seq"),
            P("section", None, "seq"),
        ),
        check_vma=False,
    )
```

profile of v0, /device:TPU:0, one launch (start us, length us, event | category | flops | bytes accessed | tf_op | source)
XLA Modules:
  0.0 1719.1 jit_solution(7740180637249171521)
XLA Ops:
  104.3 7.8 all-to-all-done
  123.9 8.8 fusion.82
  139.1 26.8 %reduce-scatter.31.cloned.1.call-done = bf16[256,768]{1,0:T(8,128)(2,1)} async-done(((bf16[1024,768]{1,0:T(8,128)(2,1)}), bf16[256,768]{1,0:T(8,128)(2,1)}) %reduce-scatter.31.cloned.1.call-update) | async-done | bytes 393232 | tf_op jit(solution)/shard_map/reduce_scatter | solution.py:53
  169.0 30.6 %all-gather.13.cloned.1.call-done = bf16[1024,768]{1,0:T(8,128)(2,1)} async-done(((bf16[256,768]{1,0:T(8,128)(2,1)}), bf16[1024,768]{1,0:T(8,128)(2,1)}) %all-gather.13.cloned.1.call-update) | async-done | bytes 1572880 | tf_op jit(solution)/shard_map/all_gather | solution.py:60
  207.7 31.0 %reduce-scatter.33.cloned.1.call-done = bf16[256,768]{1,0:T(8,128)(2,1)} async-done(((bf16[1024,768]{1,0:T(8,128)(2,1)}), bf16[256,768]{1,0:T(8,128)(2,1)}) %reduce-scatter.33.cloned.1.call-update) | async-done | bytes 393232 | tf_op jit(solution)/shard_map/reduce_scatter | solution.py:53
  242.6 29.4 %all-gather.15.cloned.1.call-done = bf16[1024,768]{1,0:T(8,128)(2,1)} async-done(((bf16[256,768]{1,0:T(8,128)(2,1)}), bf16[1024,768]{1,0:T(8,128)(2,1)}) %all-gather.15.cloned.1.call-update) | async-done | bytes 1572880 | tf_op jit(solution)/shard_map/all_gather | solution.py:60
  357.1 9.0 fusion.85
  369.2 28.6 %reduce-scatter.35.cloned.1.call-done = bf16[256,768]{1,0:T(8,128)(2,1)} async-done(((bf16[1024,768]{1,0:T(8,128)(2,1)}), bf16[256,768]{1,0:T(8,128)(2,1)}) %reduce-scatter.35.cloned.1.call-update) | async-done | bytes 393232 | tf_op jit(solution)/shard_map/reduce_scatter | solution.py:53
  401.3 30.8 %all-gather.17.cloned.1.call-done = bf16[1024,768]{1,0:T(8,128)(2,1)} async-done(((bf16[256,768]{1,0:T(8,128)(2,1)}), bf16[1024,768]{1,0:T(8,128)(2,1)}) %all-gather.17.cloned.1.call-update) | async-done | bytes 1572880 | tf_op jit(solution)/shard_map/all_gather | solution.py:60
  439.9 31.0 %reduce-scatter.37.cloned.1.call-done = bf16[256,768]{1,0:T(8,128)(2,1)} async-done(((bf16[1024,768]{1,0:T(8,128)(2,1)}), bf16[256,768]{1,0:T(8,128)(2,1)}) %reduce-scatter.37.cloned.1.call-update) | async-done | bytes 393232 | tf_op jit(solution)/shard_map/reduce_scatter | solution.py:53
  472.8 31.6 %all-gather.19.cloned.1.call-done = bf16[1024,768]{1,0:T(8,128)(2,1)} async-done(((bf16[256,768]{1,0:T(8,128)(2,1)}), bf16[1024,768]{1,0:T(8,128)(2,1)}) %all-gather.19.cloned.1.call-update) | async-done | bytes 1572880 | tf_op jit(solution)/shard_map/all_gather | solution.py:60
  599.1 9.7 fusion.88
  613.0 28.6 %reduce-scatter.39.cloned.1.call-done = bf16[256,768]{1,0:T(8,128)(2,1)} async-done(((bf16[1024,768]{1,0:T(8,128)(2,1)}), bf16[256,768]{1,0:T(8,128)(2,1)}) %reduce-scatter.39.cloned.1.call-update) | async-done | bytes 393232 | tf_op jit(solution)/shard_map/reduce_scatter | solution.py:53
  644.9 31.1 %all-gather.21.cloned.1.call-done = bf16[1024,768]{1,0:T(8,128)(2,1)} async-done(((bf16[256,768]{1,0:T(8,128)(2,1)}), bf16[1024,768]{1,0:T(8,128)(2,1)}) %all-gather.21.cloned.1.call-update) | async-done | bytes 1572880 | tf_op jit(solution)/shard_map/all_gather | solution.py:60
  696.6 21.4 %reduce-scatter.43.cloned.1.call-done = bf16[256,768]{1,0:T(8,128)(2,1)} async-done(((bf16[1024,768]{1,0:T(8,128)(2,1)}), bf16[256,768]{1,0:T(8,128)(2,1)}) %reduce-scatter.43.cloned.1.call-update) | async-done | bytes 393232 | tf_op jit(solution)/shard_map/reduce_scatter | solution.py:65
  722.0 29.8 %reduce-scatter.41.cloned.1.call-done = bf16[256,768]{1,0:T(8,128)(2,1)} async-done(((bf16[1024,768]{1,0:T(8,128)(2,1)}), bf16[256,768]{1,0:T(8,128)(2,1)}) %reduce-scatter.41.cloned.1.call-update) | async-done | bytes 393232 | tf_op jit(solution)/shard_map/reduce_scatter | solution.py:53
  756.5 31.1 %all-gather.25.cloned.1.call-done = bf16[1024,768]{1,0:T(8,128)(2,1)} async-done(((bf16[256,768]{1,0:T(8,128)(2,1)}), bf16[1024,768]{1,0:T(8,128)(2,1)}) %all-gather.25.cloned.1.call-update) | async-done | bytes 1572880 | tf_op jit(solution)/shard_map/all_gather | solution.py:72
  790.2 10.0 fusion.178
  814.7 6.5 all-to-all-start.7
  821.2 6.3 pad_maximum_fusion.2
  833.8 8.0 scatter_fusion
  861.7 12.5 all-to-all-done.6
  876.9 7.0 scatter_fusion.1
  905.3 28.0 %reduce-scatter.45.cloned.1.call-done = bf16[256,768]{1,0:T(8,128)(2,1)} async-done(((bf16[1024,768]{1,0:T(8,128)(2,1)}), bf16[256,768]{1,0:T(8,128)(2,1)}) %reduce-scatter.45.cloned.1.call-update) | async-done | bytes 393232 | tf_op jit(solution)/shard_map/reduce_scatter | solution.py:65
  940.4 31.1 %all-gather.27.cloned.1.call-done = bf16[1024,768]{1,0:T(8,128)(2,1)} async-done(((bf16[256,768]{1,0:T(8,128)(2,1)}), bf16[1024,768]{1,0:T(8,128)(2,1)}) %all-gather.27.cloned.1.call-update) | async-done | bytes 1572880 | tf_op jit(solution)/shard_map/all_gather | solution.py:72
  987.7 31.0 %reduce-scatter.47.cloned.1.call-done = bf16[256,768]{1,0:T(8,128)(2,1)} async-done(((bf16[1024,768]{1,0:T(8,128)(2,1)}), bf16[256,768]{1,0:T(8,128)(2,1)}) %reduce-scatter.47.cloned.1.call-update) | async-done | bytes 393232 | tf_op jit(solution)/shard_map/reduce_scatter | solution.py:65
  1027.3 31.1 %all-gather.29.cloned.1.call-done = bf16[1024,768]{1,0:T(8,128)(2,1)} async-done(((bf16[256,768]{1,0:T(8,128)(2,1)}), bf16[1024,768]{1,0:T(8,128)(2,1)}) %all-gather.29.cloned.1.call-update) | async-done | bytes 1572880 | tf_op jit(solution)/shard_map/all_gather | solution.py:72
  1063.0 10.1 fusion.175
  1086.9 6.5 all-to-all-start.9
  1107.3 9.1 scatter_fusion.3
  1137.7 11.0 all-to-all-done.8
  1151.4 10.3 scatter_fusion.4
  1181.4 28.0 %reduce-scatter.49.cloned.1.call-done = bf16[256,768]{1,0:T(8,128)(2,1)} async-done(((bf16[1024,768]{1,0:T(8,128)(2,1)}), bf16[256,768]{1,0:T(8,128)(2,1)}) %reduce-scatter.49.cloned.1.call-update) | async-done | bytes 393232 | tf_op jit(solution)/shard_map/reduce_scatter | solution.py:65
  1216.2 31.1 %all-gather.31.cloned.1.call-done = bf16[1024,768]{1,0:T(8,128)(2,1)} async-done(((bf16[256,768]{1,0:T(8,128)(2,1)}), bf16[1024,768]{1,0:T(8,128)(2,1)}) %all-gather.31.cloned.1.call-update) | async-done | bytes 1572880 | tf_op jit(solution)/shard_map/all_gather | solution.py:72
  1263.7 31.0 %reduce-scatter.51.cloned.1.call-done = bf16[256,768]{1,0:T(8,128)(2,1)} async-done(((bf16[1024,768]{1,0:T(8,128)(2,1)}), bf16[256,768]{1,0:T(8,128)(2,1)}) %reduce-scatter.51.cloned.1.call-update) | async-done | bytes 393232 | tf_op jit(solution)/shard_map/reduce_scatter | solution.py:65
  1303.2 31.1 %all-gather.33.cloned.1.call-done = bf16[1024,768]{1,0:T(8,128)(2,1)} async-done(((bf16[256,768]{1,0:T(8,128)(2,1)}), bf16[1024,768]{1,0:T(8,128)(2,1)}) %all-gather.33.cloned.1.call-update) | async-done | bytes 1572880 | tf_op jit(solution)/shard_map/all_gather | solution.py:72
  1338.8 10.0 fusion.172
  1382.9 8.2 scatter_fusion.6
  1413.7 9.7 all-to-all-done.10
  1426.2 10.4 scatter_fusion.7
  1532.2 27.4 %all-reduce.3 = (bf16[768]{0:T(1024)(128)(2,1)S(1)}, bf16[2,768]{1,0:T(2,128)(2,1)S(1)}, bf16[2,768]{1,0:T(2,128)(2,1)S(1)}) all-reduce(f32[768]{0:T(1024)S(1)} %add_add_fusion.10, f32[2,768]{1,0:T(2,128)S(1)} %fusion.265, f32[2,768]{1,0:T(2,128)S(1)} %fusion.266), channel_id=1, replica_groups=mesh['section'=2,'tensor'=4,'seq'=4] {'tensor'}, use_global_device_ids=true, to_apply=%region_106.109 | all-reduce | flops 3840 | bytes 23040 | tf_op jit(solution)/shard_map/psum | solution.py:565
  1568.9 19.2 %reduce-scatter.65.cloned.1.call-done = bf16[192,192]{1,0:T(8,128)(2,1)} async-done(((bf16[768,192]{1,0:T(8,128)(2,1)}), bf16[192,192]{1,0:T(8,128)(2,1)}) %reduce-scatter.65.cloned.1.call-update) | async-done | bytes 73744
  1589.8 17.8 %reduce-scatter.61.cloned.1.call-done = bf16[48,2]{1,0:T(8,128)(2,1)} async-done(((bf16[192,2]{1,0:T(8,128)(2,1)}), bf16[48,2]{1,0:T(8,128)(2,1)}) %reduce-scatter.61.cloned.1.call-update) | async-done | bytes 208
  1609.0 28.4 %reduce-scatter.55.cloned.1.call-done = bf16[192,3,192]{2,0,1:T(8,128)(2,1)} async-done(((bf16[768,3,192]{2,0,1:T(8,128)(2,1)}), bf16[192,3,192]{2,0,1:T(8,128)(2,1)}) %reduce-scatter.55.cloned.1.call-update) | async-done | bytes 221200 | tf_op jit(solution)/shard_map/reduce_scatter | solution.py:580
  1639.2 9.6 all-reduce.4
  1650.7 7.0 reduce-scatter.67.cloned.1.call-done
  1658.6 19.0 %reduce-scatter.69.cloned.1.call-done = bf16[192,2]{1,0:T(8,128)(2,1)} async-done(((bf16[768,2]{1,0:T(8,128)(2,1)}), bf16[192,2]{1,0:T(8,128)(2,1)}) %reduce-scatter.69.cloned.1.call-update) | async-done | bytes 784
  1679.7 29.1 %all-gather.35.cloned.1.call-done = bf16[1024,768]{1,0:T(8,128)(2,1)} async-done(((bf16[256,768]{1,0:T(8,128)(2,1)}), bf16[1024,768]{1,0:T(8,128)(2,1)}) %all-gather.35.cloned.1.call-update) | async-done | bytes 1572880 | tf_op jit(solution)/shard_map/all_gather | solution.py:72
  (1065 shorter events, 748.0 us)
Async XLA Ops:
  22.1 93.6 %collective-permute-start = (bf16[3,64,128]{1,2,0:T(8,128)(2,1)}, bf16[3,64,128]{1,2,0:T(8,128)(2,1)}, u32[]{:S(2)}, u32[]{:S(2)}) collective-permute-start(bf16[3,64,128]{1,2,0:T(8,128)(2,1)} %fusion.223), channel_id=1, source_target_pairs={{0,1},{1,2},{2,3},{4,5},{5,6},{6,7},{8,9},{9,10},{10,11},{12,13},{... | collective-permute-start | bytes 147464 | tf_op jit(solution)/shard_map/ppermute | solution.py:16
  50.4 32.2 %all-to-all-start.1 = ((bf16[4,2,512]{2,1,0:T(2,128)(2,1)}), bf16[4,2,512]{2,1,0:T(2,128)(2,1)}, u32[]{:S(2)}, u32[]{:S(2)}) async-start(bf16[4,2,512]{2,1,0:T(2,128)(2,1)} %reshape.2159), calls=%async_computation.1 | async-start | bytes 16384 | tf_op jit(solution)/shard_map/all_to_all | solution.py:125
  54.9 46.6 %collective-permute-start.1 = (bf16[3,64]{1,0:T(4,128)(2,1)}, bf16[3,64]{1,0:T(4,128)(2,1)}, u32[]{:S(2)}, u32[]{:S(2)}) collective-permute-start(bf16[3,64]{1,0:T(4,128)(2,1)} %bitcast.688), channel_id=1, source_target_pairs={{0,1},{1,2},{2,3},{4,5},{5,6},{6,7},{8,9},{9,10},{10,11},{12,13},{... | collective-permute-start | bytes 1160 | tf_op jit(solution)/shard_map/ppermute | solution.py:16
  82.6 29.5 %all-to-all-start = ((bf16[4,16,64,128]{3,2,1,0:T(8,128)(2,1)}), bf16[4,16,64,128]{3,2,1,0:T(8,128)(2,1)}, u32[]{:S(2)}, u32[]{:S(2)}) async-start(bf16[4,16,64,128]{3,2,1,0:T(8,128)(2,1)} %broadcast_select_fusion.2), calls=%async_computation | async-start | bytes 2097152 | tf_op jit(solution)/shard_map/all_to_all | solution.py:124
  86.9 78.9 %reduce-scatter.31.cloned.1.call-start = ((), (), s32[]{:S(2)}) async-start(), calls=%async_computation.32 | async-start | bytes 1966080 | tf_op jit(solution)/shard_map/reduce_scatter | solution.py:53
  135.7 64.0 %all-gather.13.cloned.1.call-start = ((), (), s32[]{:S(2)}) async-start(), calls=%async_computation.33 | async-start | bytes 1966080 | tf_op jit(solution)/shard_map/all_gather | solution.py:60
  168.6 70.1 %reduce-scatter.33.cloned.1.call-start = ((), (), s32[]{:S(2)}) async-start(), calls=%async_computation.34 | async-start | bytes 1966080 | tf_op jit(solution)/shard_map/reduce_scatter | solution.py:53
  207.6 64.4 %all-gather.15.cloned.1.call-start = ((), (), s32[]{:S(2)}) async-start(), calls=%async_computation.35 | async-start | bytes 1966080 | tf_op jit(solution)/shard_map/all_gather | solution.py:60
  312.9 32.4 %all-to-all-start.2 = ((bf16[4,16,64,128]{3,2,1,0:T(8,128)(2,1)}), bf16[4,16,64,128]{3,2,1,0:T(8,128)(2,1)}, u32[]{:S(2)}, u32[]{:S(2)}) async-start(bf16[4,16,64,128]{3,2,1,0:T(8,128)(2,1)} %broadcast_select_fusion.1), calls=%async_computation.4 | async-start | bytes 2097152 | tf_op jit(solution)/shard_map/all_to_all | solution.py:124
  317.2 80.5 %reduce-scatter.35.cloned.1.call-start = ((), (), s32[]{:S(2)}) async-start(), calls=%async_computation.36 | async-start | bytes 1966080 | tf_op jit(solution)/shard_map/reduce_scatter | solution.py:53
  330.6 11.8 collective-permute-start.4
  337.3 11.7 collective-permute-start.3
  369.1 63.0 %all-gather.17.cloned.1.call-start = ((), (), s32[]{:S(2)}) async-start(), calls=%async_computation.37 | async-start | bytes 1966080 | tf_op jit(solution)/shard_map/all_gather | solution.py:60
  401.0 70.0 %reduce-scatter.37.cloned.1.call-start = ((), (), s32[]{:S(2)}) async-start(), calls=%async_computation.38 | async-start | bytes 1966080 | tf_op jit(solution)/shard_map/reduce_scatter | solution.py:53
  439.9 64.5 %all-gather.19.cloned.1.call-start = ((), (), s32[]{:S(2)}) async-start(), calls=%async_computation.39 | async-start | bytes 1966080 | tf_op jit(solution)/shard_map/all_gather | solution.py:60
  548.9 36.7 %all-to-all-start.4 = ((bf16[4,16,64,128]{3,2,1,0:T(8,128)(2,1)}), bf16[4,16,64,128]{3,2,1,0:T(8,128)(2,1)}, u32[]{:S(2)}, u32[]{:S(2)}) async-start(bf16[4,16,64,128]{3,2,1,0:T(8,128)(2,1)} %broadcast_select_fusion), calls=%async_computation.8 | async-start | bytes 2097152 | tf_op jit(solution)/shard_map/all_to_all | solution.py:124
  553.2 88.3 %reduce-scatter.39.cloned.1.call-start = ((), (), s32[]{:S(2)}) async-start(), calls=%async_computation.40 | async-start | bytes 1966080 | tf_op jit(solution)/shard_map/reduce_scatter | solution.py:53
  566.4 13.1 collective-permute-start.7
  573.0 18.0 %collective-permute-start.6 = (bf16[3,64,128]{1,2,0:T(8,128)(2,1)}, bf16[3,64,128]{1,2,0:T(8,128)(2,1)}, u32[]{:S(2)}, u32[]{:S(2)}) collective-permute-start(bf16[3,64,128]{1,2,0:T(8,128)(2,1)} %fusion.225), channel_id=1, source_target_pairs={{0,1},{1,2},{2,3},{4,5},{5,6},{6,7},{8,9},{9,10},{10,11},{12,13},{... | collective-permute-start | bytes 147464 | tf_op jit(solution)/shard_map/ppermute | solution.py:16
  612.9 63.0 %all-gather.21.cloned.1.call-start = ((), (), s32[]{:S(2)}) async-start(), calls=%async_computation.41 | async-start | bytes 1966080 | tf_op jit(solution)/shard_map/all_gather | solution.py:60
  644.8 73.2 %reduce-scatter.43.cloned.1.call-start = ((), (), s32[]{:S(2)}) async-start(), calls=%async_computation.44 | async-start | bytes 1966080 | tf_op jit(solution)/shard_map/reduce_scatter | solution.py:65
  687.0 64.9 %reduce-scatter.41.cloned.1.call-start = ((), (), s32[]{:S(2)}) async-start(), calls=%async_computation.42 | async-start | bytes 1966080 | tf_op jit(solution)/shard_map/reduce_scatter | solution.py:53
  692.2 95.5 %all-gather.25.cloned.1.call-start = ((), (), s32[]{:S(2)}) async-start(), calls=%async_computation.45 | async-start | bytes 1966080 | tf_op jit(solution)/shard_map/all_gather | solution.py:72
  814.7 30.0 %all-to-all-start.7 = ((bf16[4,2,512]{2,1,0:T(2,128)(2,1)}), bf16[4,2,512]{2,1,0:T(2,128)(2,1)S(1)}, u32[]{:S(2)}, u32[]{:S(2)}) async-start(bf16[4,2,512]{2,1,0:T(2,128)(2,1)} %reshape.2165), calls=%async_computation.14 | async-start | bytes 16384 | tf_op jit(solution)/shard_map/all_to_all | solution.py:419
  844.7 29.5 %all-to-all-start.6 = ((bf16[4,16,64,128]{3,2,1,0:T(8,128)(2,1)}), bf16[4,16,64,128]{3,2,1,0:T(8,128)(2,1)}, u32[]{:S(2)}, u32[]{:S(2)}) async-start(bf16[4,16,64,128]{3,2,1,0:T(8,128)(2,1)} %bitcast.731), calls=%async_computation.13 | async-start | bytes 2097152 | tf_op jit(solution)/shard_map/all_to_all | solution.py:412
  848.9 84.3 %reduce-scatter.45.cloned.1.call-start = ((), (), s32[]{:S(2)}) async-start(), calls=%async_computation.46 | async-start | bytes 1966080 | tf_op jit(solution)/shard_map/reduce_scatter | solution.py:65
  904.0 67.5 %all-gather.27.cloned.1.call-start = ((), (), s32[]{:S(2)}) async-start(), calls=%async_computation.47 | async-start | bytes 1966080 | tf_op jit(solution)/shard_map/all_gather | solution.py:72
  940.3 78.5 %reduce-scatter.47.cloned.1.call-start = ((), (), s32[]{:S(2)}) async-start(), calls=%async_computation.48 | async-start | bytes 1966080 | tf_op jit(solution)/shard_map/reduce_scatter | solution.py:65
  987.7 70.8 %all-gather.29.cloned.1.call-start = ((), (), s32[]{:S(2)}) async-start(), calls=%async_computation.49 | async-start | bytes 1966080 | tf_op jit(solution)/shard_map/all_gather | solution.py:72
  1086.9 32.3 %all-to-all-start.9 = ((bf16[4,2,512]{2,1,0:T(2,128)(2,1)}), bf16[4,2,512]{2,1,0:T(2,128)(2,1)S(1)}, u32[]{:S(2)}, u32[]{:S(2)}) async-start(bf16[4,2,512]{2,1,0:T(2,128)(2,1)} %reshape.2167), calls=%async_computation.18 | async-start | bytes 16384 | tf_op jit(solution)/shard_map/all_to_all | solution.py:419
  1119.2 29.5 %all-to-all-start.8 = ((bf16[4,16,64,128]{3,2,1,0:T(8,128)(2,1)}), bf16[4,16,64,128]{3,2,1,0:T(8,128)(2,1)}, u32[]{:S(2)}, u32[]{:S(2)}) async-start(bf16[4,16,64,128]{3,2,1,0:T(8,128)(2,1)} %bitcast.730), calls=%async_computation.17 | async-start | bytes 2097152 | tf_op jit(solution)/shard_map/all_to_all | solution.py:412
  1123.5 85.9 %reduce-scatter.49.cloned.1.call-start = ((), (), s32[]{:S(2)}) async-start(), calls=%async_computation.50 | async-start | bytes 1966080 | tf_op jit(solution)/shard_map/reduce_scatter | solution.py:65
  1179.7 67.6 %all-gather.31.cloned.1.call-start = ((), (), s32[]{:S(2)}) async-start(), calls=%async_computation.51 | async-start | bytes 1966080 | tf_op jit(solution)/shard_map/all_gather | solution.py:72
  1216.2 78.5 %reduce-scatter.51.cloned.1.call-start = ((), (), s32[]{:S(2)}) async-start(), calls=%async_computation.52 | async-start | bytes 1966080 | tf_op jit(solution)/shard_map/reduce_scatter | solution.py:65
  1263.6 70.7 %all-gather.33.cloned.1.call-start = ((), (), s32[]{:S(2)}) async-start(), calls=%async_computation.53 | async-start | bytes 1966080 | tf_op jit(solution)/shard_map/all_gather | solution.py:72
  1362.8 31.1 %all-to-all-start.11 = ((bf16[4,2,512]{2,1,0:T(2,128)(2,1)}), bf16[4,2,512]{2,1,0:T(2,128)(2,1)S(1)}, u32[]{:S(2)}, u32[]{:S(2)}) async-start(bf16[4,2,512]{2,1,0:T(2,128)(2,1)} %reshape.2169), calls=%async_computation.22 | async-start | bytes 16384 | tf_op jit(solution)/shard_map/all_to_all | solution.py:419
  1393.9 29.5 %all-to-all-start.10 = ((bf16[4,16,64,128]{3,2,1,0:T(8,128)(2,1)}), bf16[4,16,64,128]{3,2,1,0:T(8,128)(2,1)}, u32[]{:S(2)}, u32[]{:S(2)}) async-start(bf16[4,16,64,128]{3,2,1,0:T(8,128)(2,1)} %bitcast.729), calls=%async_computation.21 | async-start | bytes 2097152 | tf_op jit(solution)/shard_map/all_to_all | solution.py:412
  1398.7 121.5 %all-gather.23.cloned.1.call-start = ((), (), s32[]{:S(2)}) async-start(), calls=%async_computation.43 | async-start | bytes 1966080 | tf_op jit(solution)/shard_map/all_gather | solution.py:60
  1399.4 129.2 %reduce-scatter.53.cloned.1.call-start = ((), (), s32[]{:S(2)}) async-start(), calls=%async_computation.54 | async-start | bytes 1966080 | tf_op jit(solution)/shard_map/reduce_scatter | solution.py:65
  1454.6 109.2 %reduce-scatter.57.cloned.1.call-start = ((), (), s32[]{:S(2)}) async-start(), calls=%async_computation.57 | async-start | bytes 1474560 | tf_op jit(solution)/shard_map/reduce_scatter | solution.py:595
  1465.4 100.2 %reduce-scatter.59.cloned.1.call-start = ((), (), s32[]{:S(2)}) async-start(), calls=%async_computation.58 | async-start | bytes 1474560 | tf_op jit(solution)/shard_map/reduce_scatter | solution.py:601
  1479.5 87.9 %reduce-scatter.63.cloned.1.call-start = ((), (), s32[]{:S(2)}) async-start(), calls=%async_computation.60 | async-start | bytes 245760
  1505.1 82.9 %reduce-scatter.65.cloned.1.call-start = ((), (), s32[]{:S(2)}) async-start(), calls=%async_computation.61 | async-start | bytes 491520
  1508.3 99.3 %reduce-scatter.61.cloned.1.call-start = ((), (), s32[]{:S(2)}) async-start(), calls=%async_computation.59 | async-start | bytes 61440
  1514.8 122.6 %reduce-scatter.55.cloned.1.call-start = ((), (), s32[]{:S(2)}) async-start(), calls=%async_computation.56 | async-start | bytes 1474560 | tf_op jit(solution)/shard_map/reduce_scatter | solution.py:580
  1520.1 137.6 %reduce-scatter.67.cloned.1.call-start = ((), (), s32[]{:S(2)}) async-start(), calls=%async_computation.62 | async-start | bytes 245760
  1560.4 117.2 %reduce-scatter.69.cloned.1.call-start = ((), (), s32[]{:S(2)}) async-start(), calls=%async_computation.63 | async-start | bytes 245760
  1561.3 147.4 %all-gather.35.cloned.1.call-start = ((), (), s32[]{:S(2)}) async-start(), calls=%async_computation.55 | async-start | bytes 1966080 | tf_op jit(solution)/shard_map/all_gather | solution.py:72
  (235 other events, 2555.6 us)
Sparse Core Ops, SparseCore 0:
  135.8 30.0 reduce-scatter.30
  168.7 30.9 all-gather.12
  207.7 30.9 reduce-scatter.32
  241.0 30.9 all-gather.14
  369.2 28.4 reduce-scatter.34
  401.1 30.9 all-gather.16
  440.0 30.9 reduce-scatter.36
  473.4 30.9 all-gather.18
  613.1 28.4 reduce-scatter.38
  644.9 30.9 all-gather.20
  687.1 30.8 reduce-scatter.42
  720.9 30.8 reduce-scatter.40
  756.7 30.9 all-gather.24
  904.1 29.1 reduce-scatter.44
  940.4 30.9 all-gather.26
  987.8 30.9 reduce-scatter.46
  1027.5 30.9 all-gather.28
  1179.8 29.4 reduce-scatter.48
  1216.3 30.9 all-gather.30
  1263.7 30.8 reduce-scatter.50
  1303.3 30.9 all-gather.32
  1401.9 31.4 all-gather.22
  1454.7 29.2 reduce-scatter.52
  1486.2 29.1 reduce-scatter.56
  1517.7 27.9 reduce-scatter.58
  1548.3 18.0 reduce-scatter.62
  1569.2 18.7 reduce-scatter.64
  1590.3 17.2 reduce-scatter.60
  1610.0 27.3 reduce-scatter.54
  1639.6 18.1 reduce-scatter.66
  1660.0 17.5 reduce-scatter.68
  1679.6 29.1 all-gather.34
where the time goes:
time: 1730 us; the launch traced here: 1720 us
  waiting for transfers between devices  802 us (46%)
  other arithmetic  324 us (19%)
  local copies, waits for them, and re-layouts  226 us (13%)
  matrix products  208 us (12%)
  starting transfers between devices  103 us (6%)
  blocking collectives  37 us (2%)
  between operations  18.6 us (1%)
    all_gather x6, waiting for transfers between devices, spread_grads(): whole = lax.all_gather(rows_low, 'tensor', axis=0, tiled=True)  185 us
    reduce_scatter x6, waiting for transfers between devices, reduce_rows(): lax.psum_scatter(partial_sum.astype(jnp.bfloat16), 'tensor', scatter_dime...  176 us
    all_gather x6, waiting for transfers between devices, spread_rows(): whole = lax.all_gather(rows_low, 'tensor', axis=0, tiled=True)  153 us
    reduce_scatter x6, waiting for transfers between devices, reduce_grads(): lax.psum_scatter(partial_grad.astype(jnp.bfloat16), 'tensor', scatter_dim...  139 us
    unnamed x37, waiting for transfers between devices  64.2 us
    unnamed x484, local copies, waits for them, and re-layouts  53.1 us
    ppermute x16, starting transfers between devices, from_behind(): lax.ppermute(value, axis, [(source, source + steps) for source in range(l...  41.5 us
  transfers between devices with their start and end apart: 60, of which 36 were waited for; matrix products, arithmetic and copies ran while one was open for 23% of the time, Pallas kernels for 0%

commit v1 on v0

v1 whole, which is shorter than its diff:
```python
import functools
import math

import jax
import jax.numpy as jnp
from jax import lax
from jax.experimental import pallas as pl
from jax.experimental.pallas import tpu as pltpu
from jax.sharding import PartitionSpec as P

TILE = 64
LANES = 128
MASKED = -1e30
EPSILON = 1e-05
FAR = -(1 << 20)
MESH = pl.DeviceIdType.MESH
BF = jnp.bfloat16
F32 = jnp.float32
GELU_A = 0.044715
GELU_K = math.sqrt(2.0 / math.pi)
LIMIT = 60 * 1024 * 1024


class Sizes:
    def __init__(self, mesh_tensor, mesh_seq, rows, width, heads, hidden):
        self.T, self.S = mesh_tensor, mesh_seq
        self.rows, self.width, self.heads, self.hidden = rows, width, heads, hidden
        self.tiles = rows // TILE
        self.slots = heads * self.tiles
        self.cap = -(-self.slots // (mesh_seq - 1))
        self.capg = -(-self.cap // 8) * 8
        self.n = mesh_seq * self.cap
        self.block = rows // mesh_tensor
        self.pad = heads * LANES
        self.SEND, self.INV, self.ORD, self.CONT = 0, self.n, 2 * self.n, 3 * self.n
        self.ARR = 4 * self.n
        self.POS = self.ARR + self.slots
        self.LAST = self.POS + self.slots
        self.ENDS = self.LAST + self.slots
        self.route = self.ENDS + 2


def nn(a, b):
    return jnp.dot(a, b, preferred_element_type=F32)


def nt(a, b):
    return lax.dot_general(a, b, (((1,), (1,)), ((), ())), preferred_element_type=F32)


def tn(a, b):
    return lax.dot_general(a, b, (((0,), (0,)), ((), ())), preferred_element_type=F32)


def normed(x):
    centred = x - jnp.mean(x, axis=-1, keepdims=True)
    spread = lax.rsqrt(jnp.mean(centred * centred, axis=-1, keepdims=True) + EPSILON)
    return centred * spread, spread


def norm_back(grad, gain, y, spread):
    scaled = grad * gain
    return spread * (
        scaled
        - jnp.mean(scaled, axis=-1, keepdims=True)
        - y * jnp.mean(scaled * y, axis=-1, keepdims=True)
    )


def partner(me, step):
    return (me // 2 + step // 2) % 2 * 2 + (me % 2 + step % 2) % 2


def column_sum(x):
    return jnp.sum(x, axis=0, keepdims=True)


def routing_kernel(z, sel_ref, ends_ref, rt0_ref, rt1_ref, key_ref, count_ref):
    me = lax.axis_index("seq")
    for layer, rt in enumerate((rt0_ref, rt1_ref)):

        def clear(i, _):
            rt[z.SEND + i] = 1
            rt[z.INV + i] = 0
            key_ref[i] = z.slots
            return 0

        lax.fori_loop(0, z.n, clear, 0)

        def zero(i, _):
            count_ref[i] = 0
            return 0

        lax.fori_loop(0, z.S, zero, 0)

        def source(d, _):
            def slot(u, count):
                h, t = u // z.tiles, u % z.tiles
                v = sel_ref[layer, h, d * z.tiles + t]
                mine = lax.shift_right_arithmetic(v, z.tiles.bit_length() - 1) == me

                @pl.when(mine)
                def _():
                    inner = v - me * z.tiles
                    rt[z.SEND + d * z.cap + count] = h * (z.tiles + 1) + inner + 1
                    key_ref[d * z.cap + count] = h * z.tiles + inner

                return count + mine.astype(jnp.int32)

            lax.fori_loop(0, z.slots, slot, jnp.int32(0))
            return 0

        lax.fori_loop(me + 1, z.S, source, 0)

        def arrival(u, _):
            h, t = u // z.tiles, u % z.tiles
            v = sel_ref[layer, h, me * z.tiles + t]
            live = v >= 0
            owner = jnp.where(live, v // z.tiles, 0)
            place = count_ref[owner]
            rt[z.ARR + u] = jnp.where(live, owner * z.cap + place, me * z.cap)
            rt[z.POS + u] = jnp.where(live, v * TILE, FAR)

            @pl.when(live)
            def _():
                rt[z.INV + owner * z.cap + place] = u
                count_ref[owner] = place + 1

            return 0

        lax.fori_loop(0, z.slots, arrival, 0)
        lax.fori_loop(0, z.slots + 1, zero, 0)

        def tally(i, _):
            count_ref[key_ref[i]] = count_ref[key_ref[i]] + 1
            return 0

        lax.fori_loop(0, z.n, tally, 0)

        def prefix(tile, begin):
            count = count_ref[tile]
            count_ref[tile] = begin

            @pl.when(tile < z.slots)
            def _():
                rt[z.LAST + tile] = jnp.where(count > 0, begin + count - 1, z.n)

            return begin + count

        lax.fori_loop(0, z.slots + 1, prefix, jnp.int32(0))

        def place_in(i, _):
            tile = key_ref[i]
            at = count_ref[tile]
            rt[z.ORD + at] = i
            count_ref[tile] = at + 1
            return 0

        lax.fori_loop(0, z.n, place_in, 0)

        def follow(k, before):
            tile = key_ref[rt[z.ORD + k]]
            rt[z.CONT + k] = (tile == before).astype(jnp.int32)
            return tile

        lax.fori_loop(0, z.n, follow, jnp.int32(-1))
        rt[z.ENDS] = ends_ref[0]
        rt[z.ENDS + 1] = ends_ref[1]


def smem():
    return pl.BlockSpec(memory_space=pltpu.SMEM)


def vmem():
    return pl.BlockSpec(memory_space=pltpu.VMEM)


def routing(z, sel, ends):
    shape = jax.ShapeDtypeStruct((z.route,), jnp.int32)
    return pl.pallas_call(
        functools.partial(routing_kernel, z),
        out_shape=(shape, shape),
        in_specs=[smem(), smem()],
        out_specs=(smem(), smem()),
        scratch_shapes=[
            pltpu.SMEM((z.n,), jnp.int32),
            pltpu.SMEM((max(z.slots + 1, z.S),), jnp.int32),
        ],
        name="routing",
    )(sel, ends)


def to_tensor(step, me):
    return {"tensor": partner(me, step)}


def remote(src, dst, send, recv, target):
    return pltpu.make_async_remote_copy(
        src_ref=src, dst_ref=dst, send_sem=send, recv_sem=recv, device_id=target, device_id_type=MESH
    )


def forward_kernel(
    z,
    rt,
    r_ref,
    vec_ref,
    w1_ref,
    swt_ref,
    wo_ref,
    wup_ref,
    wdn_ref,
    n1_ref,
    q_ref,
    kvt_ref,
    st_ref,
    p_ref,
    ckv_ref,
    o_ref,
    mid_ref,
    n2_ref,
    u_ref,
    act_ref,
    res_ref,
    gt_ref,
    gate_ref,
    edge_ref,
    edge_gate_ref,
    send_kv,
    send_gate,
    got_gate,
    far_gate_ref,
    wo_all,
    o_all,
    part_send,
    part_got,
    own_part,
    kv_ss,
    kv_rs,
    gate_ss,
    gate_rs,
    edge_ss,
    edge_rs,
    wo_ss,
    wo_rs,
    o_ss,
    o_rs,
    part_ss,
    part_rs,
    res_ss,
    res_rs,
):
    me, at = lax.axis_index("tensor"), lax.axis_index("seq")
    last = z.S - 1
    first_row = at * z.rows
    barrier = pltpu.get_barrier_semaphore()
    ckv_ref[at * z.cap] = jnp.zeros((TILE, LANES), BF)
    for step in range(1, z.T):
        pl.semaphore_signal(barrier, inc=1, device_id=to_tensor(step, me), device_id_type=MESH)

    def greet(d, _):
        pl.semaphore_signal(barrier, inc=1, device_id={"seq": d}, device_id_type=MESH)
        return 0

    lax.fori_loop(0, at, greet, 0)
    pl.semaphore_wait(barrier, z.T - 1 + last - at)

    def wo_copy(step):
        return remote(
            wo_ref, wo_all.at[me], wo_ss.at[step], wo_rs.at[step], to_tensor(step, me)
        )

    for step in range(1, z.T):
        wo_copy(step).start()
    wo_all[me] = wo_ref[...]

    per_block = z.block // TILE

    def project(b, _):
        rows = pl.ds(b * z.block, z.block)
        y, _ = normed(r_ref[rows, :].astype(F32))
        n1 = (y * vec_ref[0:1, :] + vec_ref[1:2, :]).astype(BF)
        n1_ref[rows, :] = n1
        qkv = (nn(n1, w1_ref[...]) + vec_ref[2:3, :]).astype(BF)
        q_ref[rows, :] = qkv[:, : z.pad]
        for h in range(z.heads):
            pairs = qkv[:, z.pad + h * LANES : z.pad + (h + 1) * LANES]
            kvt_ref[pl.ds(h * (z.tiles + 1) + 1 + b * per_block, per_block)] = pairs.reshape(
                per_block, TILE, LANES
            )
        return 0

    lax.fori_loop(0, z.T, project, 0)
    score = nt(swt_ref[...], n1_ref[...])[0:8]
    st_ref[...] = score
    gate = jnp.minimum(score, 0.0) - jnp.log1p(jnp.exp(-jnp.abs(score)))
    gt_ref[:, 0:LANES] = jnp.zeros((8, LANES), F32)
    gt_ref[:, LANES : LANES + z.rows] = gate.astype(BF).astype(F32)
    gt_ref[:, LANES + z.rows :] = jnp.zeros((8, LANES), F32)
    for t in range(z.tiles + 1):
        for h in range(z.heads):
            gate_ref[h * (z.tiles + 1) + t, 0:1, :] = gt_ref[
                h : h + 1, TILE + t * TILE : TILE + t * TILE + LANES
            ]

    def edge_copies():
        after = {"seq": jnp.minimum(at + 1, last)}
        return [
            remote(
                kvt_ref.at[h * (z.tiles + 1) + z.tiles],
                edge_ref.at[h],
                edge_ss.at[h],
                edge_rs.at[h],
                after,
            )
            for h in range(z.heads)
        ] + [
            remote(
                gt_ref.at[:, pl.ds(z.rows, LANES)],
                edge_gate_ref,
                edge_ss.at[z.heads],
                edge_rs.at[z.heads],
                after,
            )
        ]

    @pl.when(at < last)
    def _():
        for copy in edge_copies():
            copy.start()

    def tile_copies(d, source):
        return (
            remote(
                send_kv.at[d],
                ckv_ref.at[pl.ds(source * z.cap, z.cap)],
                kv_ss.at[d],
                kv_rs.at[source],
                {"seq": d},
            ),
            remote(send_gate.at[d], got_gate.at[source], gate_ss.at[d], gate_rs.at[source], {"seq": d}),
        )

    def pack(d, _):
        def slot(s, _):
            u = rt[z.SEND + d * z.cap + s]
            send_kv[d, s] = kvt_ref[u]
            send_gate[d, pl.ds(s, 1), :] = gate_ref[u][0:1]
            return 0

        lax.fori_loop(0, z.cap, slot, 0)
        for copy in tile_copies(d, at):
            copy.start()
        return 0

    lax.fori_loop(at + 1, z.S, pack, 0)

    def landed(source, _):
        for copy in tile_copies(last, source):
            copy.wait_recv()
        for s in range(z.cap):
            far_gate_ref[source * z.cap + s, 0:1, :] = got_gate[source, s : s + 1, :]
        return 0

    lax.fori_loop(0, at, landed, 0)
    lane = lax.broadcasted_iota(jnp.int32, (TILE, LANES), 1)
    row = lax.broadcasted_iota(jnp.int32, (TILE, LANES), 0)

    for h in range(z.heads):
        kvt_ref[h * (z.tiles + 1)] = jnp.zeros((TILE, LANES), BF)

    @pl.when(at > 0)
    def _():
        for copy in edge_copies():
            copy.wait_recv()
        for h in range(z.heads):
            kvt_ref[h * (z.tiles + 1)] = edge_ref[h]
            gate_ref[h * (z.tiles + 1), 0:1, :] = jnp.where(
                lane[0:1] < TILE,
                pltpu.roll(edge_gate_ref[...], TILE, 1)[h : h + 1],
                gate_ref[h * (z.tiles + 1), 0:1, :],
            )

    def attend(t):
        base = pl.multiple_of(t * TILE, TILE)
        query = first_row + base + row
        begin = jnp.where(
            query >= rt[z.ENDS + 1],
            rt[z.ENDS + 1],
            jnp.where(query >= rt[z.ENDS], rt[z.ENDS], 0),
        )
        key = first_row + base - TILE + lane
        near_ok = (key <= query) & (key > query - TILE) & (key >= begin)
        mixed = []
        for h in range(z.heads):
            cols = slice(h * LANES, (h + 1) * LANES)
            u = h * z.tiles + t
            arrived = rt[z.ARR + u]
            query_tile = q_ref[pl.ds(base, TILE), cols]
            near = kvt_ref[pl.ds(h * (z.tiles + 1) + t, 2)].reshape(2 * TILE, LANES)
            far = ckv_ref[arrived]
            near_score = nt(query_tile, near) + gate_ref[h * (z.tiles + 1) + t, 0:1, :]
            far_score = nt(query_tile, jnp.concatenate([far, far], axis=0)) + far_gate_ref[arrived][0:1]
            far_ok = (rt[z.POS + u] + lane >= begin) & (lane < TILE)
            near_score = jnp.where(near_ok, near_score, MASKED)
            far_score = jnp.where(far_ok, far_score, MASKED)
            top = jnp.max(jnp.maximum(near_score, far_score), axis=-1, keepdims=True)
            near_exp = jnp.exp(near_score - top)
            far_exp = jnp.exp(far_score - top)
            scale = 1.0 / jnp.sum(near_exp + far_exp, axis=-1, keepdims=True)
            near_p = (near_exp * scale).astype(BF)
            far_p = (far_exp * scale).astype(BF)
            p_ref[t * z.heads + h, :, 0:LANES] = near_p
            p_ref[t * z.heads + h, :, LANES:] = far_p
            mixed.append(nn(near_p, near) + nn(far_p[:, :TILE], far))
        pair = jnp.where(lane < TILE, pltpu.roll(mixed[0], TILE, 1), mixed[1]).astype(BF)
        single = pltpu.roll(mixed[2], TILE, 1).astype(BF)
        o_ref[pl.ds(base, TILE), 0:LANES] = pair
        o_ref[pl.ds(base, TILE), LANES:] = single

    def o_copy(step, b):
        rows = pl.ds(b * z.block, z.block)
        return remote(
            o_ref.at[rows, :],
            o_all.at[me, rows, :],
            o_ss.at[step * z.T + b],
            o_rs.at[step * z.T + b],
            to_tensor(step, me),
        )

    def attend_block(b, _):
        def pair(i, _):
            attend(b * per_block + 2 * i)
            attend(b * per_block + 2 * i + 1)
            return 0

        lax.fori_loop(0, per_block // 2, pair, 0)
        for step in range(1, z.T):
            o_copy(step, b).start()
        rows = pl.ds(b * z.block, z.block)
        o_all[me, rows, :] = o_ref[rows, :]
        return 0

    lax.fori_loop(0, z.T, attend_block, 0)
    for step in range(1, z.T):
        wo_copy(step).wait()

    def part_copy(step):
        return remote(
            part_send.at[step - 1],
            part_got.at[step - 1],
            part_ss.at[step - 1],
            part_rs.at[step - 1],
            to_tensor(step, me),
        )

    def feed(k, _):
        step = (k + 1) % z.T
        block = partner(me, step)
        rows = pl.ds(pl.multiple_of(block * z.block, z.block), z.block)
        for other in range(1, z.T):
            o_copy(other, block).wait_recv()
        mixed = nn(o_all[0, rows, :], wo_all[0])
        for other in range(1, z.T):
            mixed += nn(o_all[other, rows, :], wo_all[other])
        middle = r_ref[rows, :].astype(F32) + mixed + vec_ref[3:4, :]
        mid_ref[...] = middle
        y, _ = normed(middle)
        n2 = (y * vec_ref[4:5, :] + vec_ref[5:6, :]).astype(BF)
        n2_ref[rows, :] = n2
        u = nn(n2, wup_ref[...]) + vec_ref[6:7, :]
        u_ref[rows, :] = u.astype(BF)
        act = (0.5 * u * (1.0 + jnp.tanh(GELU_K * (u + GELU_A * u * u * u)))).astype(BF)
        act_ref[rows, :] = act
        own_part[...] = nn(act, wdn_ref[...])

        @pl.when(step > 0)
        def _():
            part_send[step - 1] = own_part[...].astype(BF)
            part_copy(step).start()

        return 0

    lax.fori_loop(0, z.T, feed, 0)
    total = mid_ref[...] + own_part[...] + vec_ref[7:8, :]
    for step in range(1, z.T):
        part_copy(step).wait_recv()
        total += part_got[step - 1].astype(F32)
    own_rows = pl.ds(pl.multiple_of(me * z.block, z.block), z.block)
    res_ref[own_rows, :] = total.astype(BF)

    def res_copy(step):
        return remote(
            res_ref.at[own_rows, :],
            res_ref.at[own_rows, :],
            res_ss.at[step],
            res_rs.at[step],
            to_tensor(step, me),
        )

    for step in range(1, z.T):
        res_copy(step).start()
    for step in range(1, z.T):
        part_copy(step).wait_send()
        for b in range(z.T):
            o_copy(step, b).wait_send()

    def sent(d, _):
        for copy in tile_copies(d, at):
            copy.wait_send()
        return 0

    lax.fori_loop(at + 1, z.S, sent, 0)

    @pl.when(at < last)
    def _():
        for copy in edge_copies():
            copy.wait_send()

    for step in range(1, z.T):
        res_copy(step).wait()


def forward(z, ident, route, r, w):
    rows, width, heads = z.rows, z.width, z.heads
    shapes = dict(
        n1=((rows, width), BF),
        q=((rows, z.pad), BF),
        kvt=((heads * (z.tiles + 1), TILE, LANES), BF),
        st=((8, rows), F32),
        p=((z.slots, TILE, 2 * LANES), BF),
        ckv=((z.n, TILE, LANES), BF),
        o=((rows, 2 * LANES), BF),
        mid=((z.block, width), F32),
        n2=((rows, width), BF),
        u=((rows, z.hidden), BF),
        act=((rows, z.hidden), BF),
        res=((rows, width), BF),
    )
    dma = pltpu.SemaphoreType.DMA
    outs = pl.pallas_call(
        functools.partial(forward_kernel, z),
        out_shape=tuple(jax.ShapeDtypeStruct(*s) for s in shapes.values()),
        in_specs=[smem()] + [vmem()] * 7,
        out_specs=tuple(vmem() for _ in shapes),
        scratch_shapes=[
            pltpu.VMEM((8, rows + 2 * LANES), F32),
            pltpu.VMEM((heads * (z.tiles + 1), 8, LANES), F32),
            pltpu.VMEM((heads, TILE, LANES), BF),
            pltpu.VMEM((8, LANES), F32),
            pltpu.VMEM((z.S, z.cap, TILE, LANES), BF),
            pltpu.VMEM((z.S, z.capg, LANES), F32),
            pltpu.VMEM((z.S, z.capg, LANES), F32),
            pltpu.VMEM((z.n, 8, LANES), F32),
            pltpu.VMEM((z.T, 2 * LANES, width), BF),
            pltpu.VMEM((z.T, rows, 2 * LANES), BF),
            pltpu.VMEM((z.T - 1, z.block, width), BF),
            pltpu.VMEM((z.T - 1, z.block, width), BF),
            pltpu.VMEM((z.block, width), F32),
            dma((z.S,)),
            dma((z.S,)),
            dma((z.S,)),
            dma((z.S,)),
            dma((heads + 1,)),
            dma((heads + 1,)),
            dma((z.T,)),
            dma((z.T,)),
            dma((z.T * z.T,)),
            dma((z.T * z.T,)),
            dma((z.T,)),
            dma((z.T,)),
            dma((z.T,)),
            dma((z.T,)),
        ],
        compiler_params=pltpu.CompilerParams(
            collective_id=ident, has_side_effects=True, vmem_limit_bytes=LIMIT
        ),
        name=f"forward{ident}",
    )(route, r, w["vec"], w["w1"], w["swt"], w["wo"], w["wup"], w["wdn"])
    return dict(zip(shapes, outs))


def backward_kernel(
    z,
    rt,
    c_ref,
    r_ref,
    vec_ref,
    w1_ref,
    swt_ref,
    wop_ref,
    wup_ref,
    wdn_ref,
    n1_ref,
    q_ref,
    kvt_ref,
    st_ref,
    p_ref,
    ckv_ref,
    o_ref,
    mid_ref,
    n2_ref,
    u_ref,
    act_ref,
    grad_ref,
    g_ref,
    ib_ref,
    du_ref,
    part_send,
    part_got,
    own_part,
    dr2_ref,
    ob_ref,
    dout_ref,
    dqkv_ref,
    dkvx_ref,
    dgate_ref,
    far_ref,
    far_gate_ref,
    send_kv,
    send_gate,
    got_kv,
    got_gate,
    got_gate_ref,
    edge_send,
    edge_got,
    edge_gate_got,
    sum_ref,
    gate_sum_ref,
    tile_gate_ref,
    ds_ref,
    stat_ref,
    stat_got,
    kv_ss,
    kv_rs,
    gate_ss,
    gate_rs,
    edge_ss,
    edge_rs,
    part_ss,
    part_rs,
    ob_ss,
    ob_rs,
    grad_ss,
    grad_rs,
    stat_ss,
    stat_rs,
):
    me, at = lax.axis_index("tensor"), lax.axis_index("seq")
    last = z.S - 1
    barrier = pltpu.get_barrier_semaphore()
    for step in range(1, z.T):
        pl.semaphore_signal(barrier, inc=1, device_id=to_tensor(step, me), device_id_type=MESH)

    def greet(d, _):
        pl.semaphore_signal(barrier, inc=1, device_id={"seq": d}, device_id_type=MESH)
        return 0

    lax.fori_loop(at + 1, z.S, greet, 0)
    pl.semaphore_wait(barrier, z.T - 1 + at)
    own_rows = pl.ds(pl.multiple_of(me * z.block, z.block), z.block)
    W, FFD = z.width, z.hidden
    C_O = 2 * z.pad
    C_U = C_O + 2 * LANES
    C_D = C_U + FFD
    C_S = C_D + FFD

    def part_copy(step, phase):
        return remote(
            part_send.at[phase, step - 1],
            part_got.at[phase, step - 1],
            part_ss.at[phase, step],
            part_rs.at[phase, step],
            to_tensor(step, me),
        )

    def ff_back(k, _):
        step = (k + 1) % z.T
        rows = pl.ds(pl.multiple_of(partner(me, step) * z.block, z.block), z.block)
        u = u_ref[rows, :].astype(F32)
        squared = u * u
        bent = jnp.tanh(GELU_K * (u + GELU_A * squared * u))
        slope = 0.5 * (1.0 + bent) + 0.5 * u * (1.0 - bent * bent) * (
            GELU_K * (1.0 + 3.0 * GELU_A * squared)
        )
        du = (nt(c_ref[rows, :], wdn_ref[...]) * slope).astype(BF)
        du_ref[rows, :] = du
        own_part[...] = nt(du, wup_ref[...])

        @pl.when(step > 0)
        def _():
            part_send[0, step - 1] = own_part[...].astype(BF)
            part_copy(step, 0).start()

        return 0

    lax.fori_loop(0, z.T, ff_back, 0)
    ones = jnp.ones((16, z.rows), BF)
    stat_ref[...] = jnp.zeros((24, W), F32)
    g_ref[:, C_D:C_S] = tn(c_ref[...], act_ref[...]).astype(BF)
    g_ref[:, C_U:C_D] = tn(n2_ref[...], du_ref[...]).astype(BF)
    stat_ref[8:9, :] = nn(ones, du_ref[...])[0:1]
    stat_ref[9:10, :] = nn(ones, c_ref[...])[0:1]
    grad = own_part[...]
    for step in range(1, z.T):
        part_copy(step, 0).wait_recv()
        grad += part_got[0, step - 1].astype(F32)
    y, spread = normed(mid_ref[...])
    dr2 = c_ref[own_rows, :].astype(F32) + norm_back(grad, vec_ref[4:5, :], y, spread)
    dr2_ref[...] = dr2
    stat_ref[0:1, :] = column_sum(dr2)
    stat_ref[1:2, :] = column_sum(grad * y)
    stat_ref[2:3, :] = column_sum(grad)
    ob_ref[own_rows, :] = dr2.astype(BF)

    def rows_copy(ref, sends, recvs, step):
        return remote(
            ref.at[own_rows, :], ref.at[own_rows, :], sends.at[step], recvs.at[step], to_tensor(step, me)
        )

    for step in range(1, z.T):
        rows_copy(ob_ref, ob_ss, ob_rs, step).start()
    dkvx_ref[...] = jnp.zeros((z.rows + TILE, z.pad), F32)

    def out_back(step, _):
        @pl.when(step > 0)
        def _():
            rows_copy(ob_ref, ob_ss, ob_rs, step).wait_recv()

        rows = pl.ds(pl.multiple_of(partner(me, step) * z.block, z.block), z.block)
        dout_ref[rows, :] = nt(ob_ref[rows, :], wop_ref[...]).astype(BF)
        return 0

    lax.fori_loop(0, z.T, out_back, 0)

    def attend_back(t):
        base = pl.multiple_of(t * TILE, TILE)
        for h in range(z.heads):
            cols = slice(h * LANES, (h + 1) * LANES)
            u = h * z.tiles + t
            arrived = rt[z.ARR + u]
            near = kvt_ref[pl.ds(h * (z.tiles + 1) + t, 2)].reshape(2 * TILE, LANES)
            far = ckv_ref[arrived]
            query = q_ref[pl.ds(base, TILE), cols]
            dout = dout_ref[pl.ds(base, TILE), cols]
            near_p = p_ref[t * z.heads + h, :, 0:LANES]
            far_p = p_ref[t * z.heads + h, :, LANES : LANES + TILE]
            near_pf, far_pf = near_p.astype(F32), far_p.astype(F32)
            near_dp, far_dp = nt(dout, near), nt(dout, far)
            total = jnp.sum(near_pf * near_dp, axis=-1, keepdims=True) + jnp.sum(
                far_pf * far_dp, axis=-1, keepdims=True
            )
            near_dz = (near_pf * (near_dp - total)).astype(BF)
            far_dz = (far_pf * (far_dp - total)).astype(BF)
            dqkv_ref[pl.ds(base, TILE), cols] = (nn(near_dz, near) + nn(far_dz, far)).astype(BF)
            dkvx_ref[pl.ds(base, 2 * TILE), cols] += tn(near_dz, query) + tn(near_p, dout)
            far_ref[u] = (tn(far_dz, query) + tn(far_p, dout)).astype(BF)
            dgate_ref[t, h : h + 1, :] = column_sum(near_dz.astype(F32))
            far_gate_ref[u, 0:1, 0:TILE] = column_sum(far_dz.astype(F32))

    def attend_back_pair(i, _):
        attend_back(2 * i)
        attend_back(2 * i + 1)
        return 0

    lax.fori_loop(0, z.tiles // 2, attend_back_pair, 0)
    dgate_ref[z.tiles] = jnp.zeros((8, LANES), F32)

    def edge_copies():
        return (
            remote(
                edge_send, edge_got, edge_ss.at[0], edge_rs.at[0], {"seq": jnp.maximum(at - 1, 0)}
            ),
            remote(
                dgate_ref.at[0],
                edge_gate_got,
                edge_ss.at[1],
                edge_rs.at[1],
                {"seq": jnp.maximum(at - 1, 0)},
            ),
        )

    @pl.when(at > 0)
    def _():
        edge_send[...] = dkvx_ref[0:TILE, :].astype(BF)
        for copy in edge_copies():
            copy.start()

    def tile_copies(d, source):
        return (
            remote(send_kv.at[d], got_kv.at[pl.ds(source * z.cap, z.cap)], kv_ss.at[d], kv_rs.at[source], {"seq": d}),
            remote(send_gate.at[d], got_gate.at[source], gate_ss.at[d], gate_rs.at[source], {"seq": d}),
        )

    def pack(d, _):
        def slot(s, _):
            u = rt[z.INV + d * z.cap + s]
            send_kv[d, s] = far_ref[u]
            send_gate[d, pl.ds(s, 1), :] = far_gate_ref[u][0:1]
            return 0

        lax.fori_loop(0, z.cap, slot, 0)
        for copy in tile_copies(d, at):
            copy.start()
        return 0

    lax.fori_loop(0, at, pack, 0)
    g_ref[:, C_O:C_U] = tn(ob_ref[...], o_ref[...]).astype(BF)
    sum_ref[z.n] = jnp.zeros((TILE, LANES), F32)
    gate_sum_ref[z.n] = jnp.zeros((8, LANES), F32)

    @pl.when(at < last)
    def _():
        for copy in edge_copies():
            copy.wait_recv()
        dkvx_ref[pl.ds(z.rows, TILE), :] += edge_got[...].astype(F32)
        dgate_ref[z.tiles] = edge_gate_got[...]

    def landed(source, _):
        for copy in tile_copies(0, source):
            copy.wait_recv()
        for s in range(z.cap):
            got_gate_ref[source * z.cap + s, 0:1, :] = got_gate[source, s : s + 1, :]
        return 0

    lax.fori_loop(at + 1, z.S, landed, 0)

    def gather(k, carry):
        running, gates = carry
        index = rt[z.ORD + k]
        joined = rt[z.CONT + k].astype(F32)
        running = running * joined + got_kv[index].astype(F32)
        gates = gates * joined + got_gate_ref[index]
        sum_ref[k] = running
        gate_sum_ref[k] = gates
        return running, gates

    lax.fori_loop(0, z.n, gather, (jnp.zeros((TILE, LANES), F32), jnp.zeros((8, LANES), F32)))

    def settle(t, _):
        base = pl.multiple_of((t + 1) * TILE, TILE)
        for h in range(z.heads):
            cols = slice(h * LANES, (h + 1) * LANES)
            index = rt[z.LAST + h * z.tiles + t]
            dqkv_ref[pl.ds(pl.multiple_of(t * TILE, TILE), TILE), slice(z.pad + h * LANES, z.pad + (h + 1) * LANES)] = (
                dkvx_ref[pl.ds(base, TILE), cols] + sum_ref[index]
            ).astype(BF)
            tile_gate_ref[t, h : h + 1, :] = gate_sum_ref[index][0:1]
        return 0

    lax.fori_loop(0, z.tiles, settle, 0)
    lane = lax.broadcasted_iota(jnp.int32, (8, LANES), 1)
    head_row = lax.broadcasted_iota(jnp.int32, (8, LANES), 0)
    for k in range(z.tiles // 2):
        halves = []
        for t in (2 * k, 2 * k + 1):
            halves.append(pltpu.roll(dgate_ref[t], TILE, 1) + dgate_ref[t + 1] + tile_gate_ref[t])
        both = jnp.where(lane < TILE, halves[0], pltpu.roll(halves[1], TILE, 1))
        score = st_ref[:, k * LANES : (k + 1) * LANES]
        grads = jnp.where(head_row < z.heads, both / (1.0 + jnp.exp(score)), 0.0)
        ds_ref[0:8, k * LANES : (k + 1) * LANES] = grads
        ds_ref[8:16, k * LANES : (k + 1) * LANES] = jnp.zeros((8, LANES), F32)

    def in_back(k, _):
        step = (k + 1) % z.T
        begin = pl.multiple_of(partner(me, step) * z.block, z.block)
        rows = pl.ds(begin, z.block)
        own_part[...] = nt(dqkv_ref[rows, :], w1_ref[...]) + tn(
            ds_ref[:, rows].astype(BF), swt_ref[...]
        )

        @pl.when(step > 0)
        def _():
            part_send[1, step - 1] = own_part[...].astype(BF)
            part_copy(step, 1).start()

        return 0

    lax.fori_loop(0, z.T, in_back, 0)
    g_ref[:, 0:C_O] = tn(n1_ref[...], dqkv_ref[...]).astype(BF)
    stat_ref[10:13, :] = nn(ds_ref[...].astype(BF), n1_ref[...])[0:3]
    ib_ref[...] = nn(ones, dqkv_ref[...])[0:8]
    grad = own_part[...]
    for step in range(1, z.T):
        part_copy(step, 1).wait_recv()
        grad += part_got[1, step - 1].astype(F32)
    y, spread = normed(r_ref[own_rows, :].astype(F32))
    dr = dr2_ref[...] + norm_back(grad, vec_ref[0:1, :], y, spread)
    grad_ref[own_rows, :] = dr.astype(BF)
    for step in range(1, z.T):
        rows_copy(grad_ref, grad_ss, grad_rs, step).start()
    stat_ref[3:4, :] = column_sum(grad * y)
    stat_ref[4:5, :] = column_sum(grad)

    def stat_copy(step):
        return remote(
            stat_ref.at[pl.ds(0, 8), :],
            stat_got.at[step - 1],
            stat_ss.at[step],
            stat_rs.at[step],
            to_tensor(step, me),
        )

    for step in range(1, z.T):
        stat_copy(step).start()
    shared = stat_ref[0:8, :]
    for step in range(1, z.T):
        stat_copy(step).wait()
        shared += stat_got[step - 1]
    stats = jnp.concatenate([shared, stat_ref[8:16, :]], axis=0).astype(BF)
    unit = (
        lax.broadcasted_iota(jnp.int32, (16, LANES), 0)
        == lax.broadcasted_iota(jnp.int32, (16, LANES), 1)
    ).astype(F32).astype(BF)
    g_ref[:, C_S:] = tn(stats, unit).astype(BF)
    for step in range(1, z.T):
        for phase in range(2):
            part_copy(step, phase).wait_send()
        rows_copy(ob_ref, ob_ss, ob_rs, step).wait_send()

    def sent(d, _):
        for copy in tile_copies(d, at):
            copy.wait_send()
        return 0

    lax.fori_loop(0, at, sent, 0)

    @pl.when(at > 0)
    def _():
        for copy in edge_copies():
            copy.wait_send()

    for step in range(1, z.T):
        rows_copy(grad_ref, grad_ss, grad_rs, step).wait()


def backward(z, ident, route, c, r, w, kept):
    rows, width = z.rows, z.width
    columns = 2 * z.pad + 2 * LANES + 2 * z.hidden + LANES
    dma = pltpu.SemaphoreType.DMA
    names = ("n1", "q", "kvt", "st", "p", "ckv", "o", "mid", "n2", "u", "act")
    return pl.pallas_call(
        functools.partial(backward_kernel, z),
        out_shape=(
            jax.ShapeDtypeStruct((rows, width), BF),
            jax.ShapeDtypeStruct((width, columns), BF),
            jax.ShapeDtypeStruct((8, 2 * z.pad), F32),
        ),
        in_specs=[smem()] + [vmem()] * 19,
        out_specs=(vmem(), vmem(), vmem()),
        scratch_shapes=[
            pltpu.VMEM((rows, z.hidden), BF),
            pltpu.VMEM((2, z.T - 1, z.block, width), BF),
            pltpu.VMEM((2, z.T - 1, z.block, width), BF),
            pltpu.VMEM((z.block, width), F32),
            pltpu.VMEM((z.block, width), F32),
            pltpu.VMEM((rows, width), BF),
            pltpu.VMEM((rows, z.pad), BF),
            pltpu.VMEM((rows, 2 * z.pad), BF),
            pltpu.VMEM((rows + TILE, z.pad), F32),
            pltpu.VMEM((z.tiles + 1, 8, LANES), F32),
            pltpu.VMEM((z.slots, TILE, LANES), BF),
            pltpu.VMEM((z.slots, 8, LANES), F32),
            pltpu.VMEM((z.S, z.cap, TILE, LANES), BF),
            pltpu.VMEM((z.S, z.capg, LANES), F32),
            pltpu.VMEM((z.n, TILE, LANES), BF),
            pltpu.VMEM((z.S, z.capg, LANES), F32),
            pltpu.VMEM((z.n, 8, LANES), F32),
            pltpu.VMEM((TILE, z.pad), BF),
            pltpu.VMEM((TILE, z.pad), BF),
            pltpu.VMEM((8, LANES), F32),
            pltpu.VMEM((z.n + 1, TILE, LANES), F32),
            pltpu.VMEM((z.n + 1, 8, LANES), F32),
            pltpu.VMEM((z.tiles, 8, LANES), F32),
            pltpu.VMEM((16, rows), F32),
            pltpu.VMEM((24, width), F32),
            pltpu.VMEM((z.T - 1, 8, width), F32),
            dma((z.S,)),
            dma((z.S,)),
            dma((z.S,)),
            dma((z.S,)),
            dma((2,)),
            dma((2,)),
            dma((2, z.T)),
            dma((2, z.T)),
            dma((z.T,)),
            dma((z.T,)),
            dma((z.T,)),
            dma((z.T,)),
            dma((z.T,)),
            dma((z.T,)),
        ],
        compiler_params=pltpu.CompilerParams(
            collective_id=ident, has_side_effects=True, vmem_limit_bytes=LIMIT
        ),
        name=f"backward{ident}",
    )(
        route,
        c,
        r,
        w["vec"],
        w["w1"],
        w["swt"],
        w["wop"],
        w["wup"],
        w["wdn"],
        *(kept[name] for name in names),
    )


def swapped(value):
    return lax.ppermute(value, "section", [(0, 1), (1, 0)])


def body(
    tokens,
    cotangent,
    lengths,
    selected,
    input_weight,
    input_bias,
    score_weight,
    output_weight,
    output_bias,
    up_weight,
    up_bias,
    down_weight,
    down_bias,
    norm_gain,
    norm_bias,
):
    core = lax.axis_index("section")
    _, rows, width = tokens.shape
    heads, hidden = score_weight.shape[2], up_weight.shape[2]
    head = input_weight.shape[3] // heads
    inner = heads * head
    z = Sizes(lax.axis_size("tensor"), lax.axis_size("seq"), rows, width, heads, hidden)
    scale = head**-0.5
    split = input_weight[0].reshape(width, 3, heads, head)
    w1 = jnp.concatenate(
        [
            jnp.concatenate([split[:, 0] * BF(scale), jnp.zeros_like(split[:, 0])], axis=-1).reshape(
                width, z.pad
            ),
            jnp.concatenate([split[:, 1], split[:, 2]], axis=-1).reshape(width, z.pad),
        ],
        axis=1,
    )
    shift = input_bias[0].astype(F32).reshape(2, heads, head)
    nothing = jnp.zeros((heads, head), F32)
    b1 = jnp.concatenate(
        [
            jnp.concatenate([shift[0] * scale, nothing], axis=-1).reshape(1, z.pad),
            jnp.concatenate([nothing, shift[1]], axis=-1).reshape(1, z.pad),
        ],
        axis=1,
    )
    vec = jnp.concatenate(
        [
            norm_gain[0, 0:1].astype(F32),
            norm_bias[0, 0:1].astype(F32),
            b1,
            output_bias.astype(F32),
            norm_gain[0, 1:2].astype(F32),
            norm_bias[0, 1:2].astype(F32),
            up_bias.astype(F32),
            down_bias.astype(F32),
        ],
        axis=0,
    )
    swt = jnp.pad(score_weight[0].T, ((0, 16 - heads), (0, 0)))
    wo = jnp.pad(output_weight[0], ((0, 2 * LANES - inner), (0, 0)))
    wop = jnp.pad(output_weight[0].reshape(heads, head, width), ((0, 0), (LANES - head, 0), (0, 0))).reshape(
        z.pad, width
    )
    mine = dict(vec=vec, w1=w1, swt=swt, wo=wo, wop=wop, wup=up_weight[0], wdn=down_weight[0])
    theirs = {name: swapped(value) for name, value in mine.items()}
    layers = [
        {name: jnp.where(core == layer, mine[name], theirs[name]) for name in mine} for layer in range(2)
    ]
    given = lax.dynamic_index_in_dim(selected[0], 1 - core, 0, keepdims=False)
    kept_choice = lax.dynamic_index_in_dim(selected[0], core, 0, keepdims=False)
    got_choice = swapped(given)
    choice = jnp.where(
        core == 0, jnp.stack([kept_choice, got_choice]), jnp.stack([got_choice, kept_choice])
    )
    length = lax.dynamic_index_in_dim(lengths, core, 0, keepdims=False)
    ends = jnp.stack([length[0], length[0] + length[1]])
    routes = routing(z, choice, ends)
    first = lax.dynamic_index_in_dim(tokens, core, 0, keepdims=False)
    cotan = lax.dynamic_index_in_dim(cotangent, core, 0, keepdims=False)
    zero = forward(z, 0, routes[0], first, layers[0])
    one = forward(z, 1, routes[1], zero["res"], layers[1])
    grad1, g1, ib1 = backward(z, 2, routes[1], cotan, zero["res"], layers[1], one)
    grad0, g0, ib0 = backward(z, 3, routes[0], grad1, first, layers[0], zero)

    def both(layer0, layer1):
        own = jnp.where(core == 0, layer0, layer1)
        other = swapped(jnp.where(core == 0, layer1, layer0))
        return jnp.where(core == 0, jnp.stack([own, other]), jnp.stack([other, own]))[None]

    def added(layer0, layer1):
        own = jnp.where(core == 0, layer0, layer1).astype(F32)
        other = swapped(jnp.where(core == 0, layer1, layer0)).astype(F32)
        return own + other

    layer_out = both(zero["res"], one["res"])
    input_grad = both(grad0, grad1)
    total = lax.psum_scatter(
        added(g0, g1).astype(BF), "seq", scatter_dimension=0, tiled=True
    ).astype(F32)
    bias = added(ib0, ib1)[0]
    bias = jnp.stack(
        [
            scale * bias[: z.pad].reshape(heads, LANES)[:, :head].reshape(inner),
            bias[z.pad :].reshape(heads, LANES)[:, head:].reshape(inner),
        ]
    )
    bias = lax.psum_scatter(bias.astype(BF), "seq", scatter_dimension=1, tiled=True).astype(F32)
    share = total.shape[0]
    c_o = 2 * z.pad
    c_u = c_o + 2 * LANES
    c_d = c_u + hidden
    c_s = c_d + hidden
    queries = total[:, : z.pad].reshape(share, heads, LANES)
    pairs = total[:, z.pad : c_o].reshape(share, heads, LANES)
    input_weight_grad = jnp.stack(
        [
            scale * queries[:, :, :head].reshape(share, inner),
            pairs[:, :, :head].reshape(share, inner),
            pairs[:, :, head:].reshape(share, inner),
        ],
        axis=1,
    )
    stats = total[:, c_s : c_s + 16].T
    return (
        layer_out,
        input_grad,
        input_weight_grad[None],
        bias[None],
        total[:, c_s + 10 : c_s + 10 + heads][None],
        total[:, c_o : c_o + inner].T[None],
        stats[0][None],
        total[:, c_u:c_d][None],
        stats[8][None],
        total[:, c_d:c_s].T[None],
        stats[9][None],
        jnp.stack([stats[3], stats[1]])[None],
        jnp.stack([stats[4], stats[2]])[None],
    )


def solution(mesh):
    return jax.shard_map(
        body,
        mesh=mesh,
        in_specs=(
            P(None, "seq", None),
            P(None, "seq", None),
            P(),
            P("section", None, "tensor", None),
            P("section", None, None, "tensor"),
            P("section", None, "tensor"),
            P("section", None, "tensor"),
            P("section", "tensor", None),
            P("section", None),
            P("section", None, "tensor"),
            P("section", "tensor"),
            P("section", "tensor", None),
            P("section", None),
            P("section", None, None),
            P("section", None, None),
        ),
        out_specs=(
            P("section", None, "seq", None),
            P("section", None, "seq", None),
            P("section", "seq", None, "tensor"),
            P("section", None, ("tensor", "seq")),
            P("section", "seq", "tensor"),
            P("section", "tensor", "seq"),
            P("section", "seq"),
            P("section", "seq", "tensor"),
            P("section", ("tensor", "seq")),
            P("section", "tensor", "seq"),
            P("section", "seq"),
            P("section", None, "seq"),
            P("section", None, "seq"),
        ),
        check_vma=False,
    )
```

time: 1730 us -> 618 us (0.36)
  waiting for transfers between devices: 802 us -> 78.6 us
  Pallas kernels: 0 us -> 438 us
  other arithmetic: 324 us -> 51.7 us
  matrix products: 208 us -> 0 us
  local copies, waits for them, and re-layouts: 226 us -> 29.8 us
  starting transfers between devices: 103 us -> 3.7 us
  blocking collectives: 37 us -> 0 us
    pallas_call x0 -> x5, Pallas kernels: none -> 438 us  [the longest x2 230 us: backward(): pl.pallas_call(functools.partial(backward_kernel, z), out_shape=(jax.Shap...]
    all_gather x12 -> x0, waiting for transfers between devices: 338 us -> none  [the longest x6 185 us: spread_grads(): whole = lax.all_gather(rows_low, 'tensor', axis=0, tiled=True)]
    reduce_scatter x15 -> x1, waiting for transfers between devices: 344 us -> 67.3 us  [body(): lax.psum_scatter(added(g0, g1).astype(BF), 'seq', scatter_dimension=0, ti...]
    dot_general x63 -> x0, matrix products: 208 us -> none  [the longest x3 30.1 us: layer_backward(): jnp.einsum('hutk,hutd->hukd', probs_full.astype(jnp.bfloat16), grad_tiles...]
    reduce_sum x47 -> x0, other arithmetic: 68.1 us -> none  [the longest x9 18.1 us: layer_norm(): return centred * lax.rsqrt(spread + EPSILON) * norm_gain + norm_shift]
    unnamed x37 -> x3, waiting for transfers between devices: 64.2 us -> 5.1 us
    scatter-add x12 -> x0, other arithmetic: 58.8 us -> none  [the longest x3 27.8 us: layer_backward(): local_grad.reshape(slot_count, tile_size, pair_width).at[rows_flat]]
    all_to_all x12 -> x0, starting transfers between devices: 58.2 us -> none  [the longest x3 19.2 us: layer_backward(): lax.all_to_all(outgoing_gate.reshape(seq_count, capacity, tile_size).asty...]
  transfers between devices with their start and end apart: 60 -> 14, of which waited for: 36 -> 3; matrix products, arithmetic and copies ran while one was open for 23% -> 9% of each run, Pallas kernels for 0% -> 2%
where the time goes in v1:
time: 618 us; the launch traced here: 617 us
  Pallas kernels  438 us (71%)
  waiting for transfers between devices  78.6 us (13%)
  other arithmetic  51.7 us (8%)
  local copies, waits for them, and re-layouts  29.8 us (5%)
  between operations  15.6 us (3%)
    pallas_call x2, Pallas kernels, backward(): pl.pallas_call(functools.partial(backward_kernel, z), out_shape=(jax.Shap...  230 us
    pallas_call x2, Pallas kernels, forward(): pl.pallas_call(functools.partial(forward_kernel, z), out_shape=tuple((jax...  193 us
    reduce_scatter x1, waiting for transfers between devices, body(): lax.psum_scatter(added(g0, g1).astype(BF), 'seq', scatter_dimension=0, ti...  67.3 us
    pallas_call x1, Pallas kernels, routing(): pl.pallas_call(functools.partial(routing_kernel, z), out_shape=(shape, sh...  15.1 us
    select_n x7, other arithmetic, body(): jnp.where(core == layer, mine[name], theirs[name])  13.8 us
  transfers between devices with their start and end apart: 14, of which 3 were waited for; matrix products, arithmetic and copies ran while one was open for 9% of the time, Pallas kernels for 2%

profile of v1, /device:TPU:0, one launch (start us, length us, event | category | flops | bytes accessed | tf_op | source)
XLA Modules:
  0.0 617.5 jit_solution(17766785742613222497)
XLA Ops:
  7.2 0.9 dynamic-slice_bitcast_fusion.2
  8.6 0.7 pad.15
  9.4 0.7 convert_element_type.93
  10.4 0.8 bitcast_convert_fusion
  11.1 0.8 concatenate.52
  12.4 1.7 pad.16
  14.2 1.9 fusion
  16.1 0.9 concatenate.53
  17.0 2.1 copy.72
  19.1 1.8 pad_maximum_fusion.1
  20.9 2.1 copy.73
  23.0 2.4 pad_maximum_fusion
  26.4 1.2 dynamic-slice_bitcast_fusion.1.r_ref
  27.7 1.2 copy-done.11
  28.9 1.2 dynamic-slice_bitcast_fusion.c_ref
  31.4 1.2 pad_add_fusion.ends_ref
  33.4 15.1 %routing.1 = (s32[402]{0:T(512)}, s32[402]{0:T(512)}) custom-call(s32[2,3,64]{2,1,0:T(4,128)} %add_select_fusion.sel_ref, s32[2]{0:T(128)} %pad_add_fusion.ends_ref), custom_call_target="tpu_custom_call" | custom-call | tf_op jit(solution)/shard_map/routing/pallas_call | solution.py:181
  50.4 2.1 broadcast_select_fusion.11
  52.6 1.2 broadcast_select_fusion.9
  53.8 3.1 broadcast_select_fusion.5
  56.9 3.0 broadcast_select_fusion.3
  59.9 3.1 broadcast_select_fusion.4
  63.0 91.8 %forward0.1 = (bf16[1024,768]{1,0:T(8,128)(2,1)}, bf16[1024,384]{1,0:T(8,128)(2,1)}, bf16[51,64,128]{2,1,0:T(8,128)(2,1)}, f32[8,1024]{1,0:T(8,128)}, bf16[48,64...) custom-call(s32[402]{0:T(512)} %get-tuple-element.45.rt, ...), custom_call_target="tpu_custom_call" | custom-call | tf_op jit(solution)/shard_map/forward0/pallas_call | solution.py:542
  154.8 100.9 %forward1.1 = (bf16[1024,768]{1,0:T(8,128)(2,1)}, bf16[1024,384]{1,0:T(8,128)(2,1)}, bf16[51,64,128]{2,1,0:T(8,128)(2,1)}, f32[8,1024]{1,0:T(8,128)}, bf16[48,64...) custom-call(s32[402]{0:T(512)} %get-tuple-element.47.rt, ...), custom_call_target="tpu_custom_call" | custom-call | tf_op jit(solution)/shard_map/forward1/pallas_call | solution.py:542
  255.8 120.1 %backward2.1 = (bf16[1024,768]{1,0:T(8,128)(2,1)}, bf16[768,2688]{1,0:T(8,128)(2,1)}, f32[8,768]{1,0:T(8,128)}) custom-call(s32[402]{0:T(512)} %get-tuple-element.47.rt, bf16[1024,768]{1,0:T(8,128)(2,1)} %dynamic-slice_bitcast_fusion.c_ref, bf16[1024,768]{1,0:T(8,128)(2,1)} %get-tuple-element.46.r_ref, f32[8,768]{1,0:T(8,128)} %get-tuple-element.161.vec_ref, ...), custom_call_target="tpu_custom_call" | custom-call | tf_op jit(solution)/shard_map/backward2/pallas_call | solution.py:943
  375.9 110.1 %backward3.1 = (bf16[1024,768]{1,0:T(8,128)(2,1)}, bf16[768,2688]{1,0:T(8,128)(2,1)}, f32[8,768]{1,0:T(8,128)}) custom-call(s32[402]{0:T(512)} %get-tuple-element.45.rt, bf16[1024,768]{1,0:T(8,128)(2,1)} %get-tuple-element.60.c_ref, bf16[1024,768]{1,0:T(8,128)(2,1)} %dynamic-slice_bitcast_fusion.1.r_ref, f32[8,768]{1,0:T(8,128)} %get-tuple-element.162.vec_ref, ...), custom_call_target="tpu_custom_call" | custom-call | tf_op jit(solution)/shard_map/backward3/pallas_call | solution.py:943
  486.0 4.6 broadcast_select_fusion
  491.2 6.1 collective-permute-done.11
  497.7 0.8 copy.87
  498.8 6.9 %add_convert_fusion = bf16[768,2688]{1,0:T(8,128)(2,1)} fusion(bf16[768,2688]{1,0:T(8,128)(2,1)} %collective-permute-done.10, bf16[768,2688]{1,0:T(8,128)(2,1)} %get-tuple-element.73, bf16[768,2688]{1,0:T(8,128)(2,1)} %get-tuple-element.74, pred[]{:T(512)S(6)} %eq.4), kind=kLoop, calls=%fused_computation | loop fusion | flops 10321920 | bytes 16515073 | tf_op jit(solution)/shard_map/convert_element_type | solution.py:1111
  505.7 1.4 copy-done.2
  507.1 3.4 select_bitcast_fusion.1
  510.9 1.9 select_bitcast_fusion
  513.0 5.1 reduce-scatter.7.cloned.1.call-done
  518.0 0.8 copy.88
  519.4 3.8 maximum_select_fusion
  523.2 3.8 maximum_select_fusion.1
  527.1 67.3 %reduce-scatter.5.cloned.1.call-done = bf16[192,2688]{1,0:T(8,128)(2,1)} async-done(((bf16[768,2688]{1,0:T(8,128)(2,1)}), bf16[192,2688]{1,0:T(8,128)(2,1)}) %reduce-scatter.5.cloned.1.call-update) | async-done | bytes 1032208 | tf_op jit(solution)/shard_map/reduce_scatter | solution.py:1110
  594.4 1.4 convert_element_type.104
  595.8 1.1 slice_bitcast_fusion
  598.1 0.9 maximum_bitcast_fusion
  599.0 2.3 copy.81
  601.9 0.8 copy.83
  602.7 0.9 fusion.5
  603.6 1.0 copy.79
  604.6 1.0 copy.80
  605.6 1.0 copy.78
  606.6 1.0 copy.77
  (98 shorter events, 12.5 us)
Async XLA Ops:
  7.2 19.2 %copy-start = (bf16[2,1024,768]{2,1,0:T(8,128)(2,1)S(1)}, bf16[2,1024,768]{2,1,0:T(8,128)(2,1)}, u32[]{:S(2)}) copy-start(bf16[2,1024,768]{2,1,0:T(8,128)(2,1)} %param.15) | copy-start | bytes 9437188
  7.2 510.8 %reduce-scatter.7.cloned.1.call-start = ((), (), s32[]{:S(2)}) async-start(), calls=%async_computation.3 | async-start | bytes 61440
  8.1 24.6 %collective-permute-start = (s32[3,64]{1,0:T(4,128)S(1)}, s32[3,64]{1,0:T(4,128)S(1)}, u32[]{:S(2)}, u32[]{:S(2)}) collective-permute-start(s32[3,64]{1,0:T(4,128)S(1)} %bitcast.112), channel_id=1, source_target_pairs={{0,16},{16,0},{1,17},{17,1},{2,18},{18,2},{3,19},{19,3},{4,20},{20... | collective-permute-start | bytes 2312 | tf_op jit(solution)/shard_map/ppermute | solution.py:1013
  9.3 39.3 %collective-permute-start.3 = (bf16[16,768]{1,0:T(8,128)(2,1)S(1)}, bf16[16,768]{1,0:T(8,128)(2,1)S(1)}, u32[]{:S(2)}, u32[]{:S(2)}) collective-permute-start(bf16[16,768]{1,0:T(8,128)(2,1)S(1)} %pad.15), channel_id=1, source_target_pairs={{0,16},{16,0},{1,17},{17,1},{2,18},{18,2},{3,19},{19,3},{4,20},{20... | collective-permute-start | bytes 73736 | tf_op jit(solution)/shard_map/ppermute | solution.py:1013
  11.9 37.9 %collective-permute-start.1 = (f32[8,768]{1,0:T(8,128)S(1)}, f32[8,768]{1,0:T(8,128)S(1)}, u32[]{:S(2)}, u32[]{:S(2)}) collective-permute-start(f32[8,768]{1,0:T(8,128)S(1)} %concatenate.52), channel_id=1, source_target_pairs={{0,16},{16,0},{1,17},{17,1},{2,18},{18,2},{3,19},{19,3},{4,20},{20... | collective-permute-start | bytes 73736 | tf_op jit(solution)/shard_map/ppermute | solution.py:1013
  14.1 36.3 %collective-permute-start.4 = (bf16[256,768]{1,0:T(8,128)(2,1)}, bf16[256,768]{1,0:T(8,128)(2,1)}, u32[]{:S(2)}, u32[]{:S(2)}) collective-permute-start(bf16[256,768]{1,0:T(8,128)(2,1)} %pad.16), channel_id=1, source_target_pairs={{0,16},{16,0},{1,17},{17,1},{2,18},{18,2},{3,19},{19,3},{4,20},{20... | collective-permute-start | bytes 1179656 | tf_op jit(solution)/shard_map/ppermute | solution.py:1013
  20.9 4.9 copy-start.15
  25.4 28.4 %collective-permute-start.2 = (bf16[768,768]{1,0:T(8,128)(2,1)}, bf16[768,768]{1,0:T(8,128)(2,1)}, u32[]{:S(2)}, u32[]{:S(2)}) collective-permute-start(bf16[768,768]{1,0:T(8,128)(2,1)} %pad_maximum_fusion), channel_id=1, source_target_pairs={{0,16},{16,0},{1,17},{17,1},{2,18},{18,2},{3,19},{19,3},{4,20},{20... | collective-permute-start | bytes 3538952 | tf_op jit(solution)/shard_map/ppermute | solution.py:1013
  26.4 2.5 copy-start.11
  28.9 3.8 copy-start.8
  28.9 20.2 %copy-start.14 = (bf16[1,768,3]{1,2,0:T(4,128)(2,1)S(1)}, bf16[1,768,3]{1,2,0:T(4,128)(2,1)}, u32[]{:S(2)}) copy-start(bf16[1,768,3]{1,2,0:T(4,128)(2,1)} %param.21) | copy-start | bytes 13828
  32.7 19.8 %collective-permute-start.8 = (bf16[384,768]{1,0:T(8,128)(2,1)S(1)}, bf16[384,768]{1,0:T(8,128)(2,1)S(1)}, u32[]{:S(2)}, u32[]{:S(2)}) collective-permute-start(bf16[384,768]{1,0:T(8,128)(2,1)S(1)} %bitcast.99), channel_id=1, source_target_pairs={{0,16},{16,0},{1,17},{17,1},{2,18},{18,2},{3,19},{19,3},{4,20},{20... | collective-permute-start | bytes 1769480 | tf_op jit(solution)/shard_map/ppermute | solution.py:1013
  48.6 8.3 %collective-permute-start.6 = (bf16[768,768]{1,0:T(8,128)(2,1)}, bf16[768,768]{1,0:T(8,128)(2,1)S(1)}, u32[]{:S(2)}, u32[]{:S(2)}) collective-permute-start(bf16[768,768]{1,0:T(8,128)(2,1)} %bitcast.21), channel_id=1, source_target_pairs={{0,16},{16,0},{1,17},{17,1},{2,18},{18,2},{3,19},{19,3},{4,20},{20... | collective-permute-start | bytes 3538952 | tf_op jit(solution)/shard_map/ppermute | solution.py:1013
  49.8 10.2 %collective-permute-start.5 = (bf16[768,768]{1,0:T(8,128)(2,1)}, bf16[768,768]{1,0:T(8,128)(2,1)S(1)}, u32[]{:S(2)}, u32[]{:S(2)}) collective-permute-start(bf16[768,768]{1,0:T(8,128)(2,1)} %bitcast.20), channel_id=1, source_target_pairs={{0,16},{16,0},{1,17},{17,1},{2,18},{18,2},{3,19},{19,3},{4,20},{20... | collective-permute-start | bytes 3538952 | tf_op jit(solution)/shard_map/ppermute | solution.py:1013
  50.4 3.3 copy-start.6
  50.4 3.3 copy-start.7
  486.0 4.6 copy-start.12
  486.0 4.6 copy-start.13
  490.6 8.1 %collective-permute-start.10 = (bf16[768,2688]{1,0:T(8,128)(2,1)}, bf16[768,2688]{1,0:T(8,128)(2,1)}, u32[]{:S(2)}, u32[]{:S(2)}) collective-permute-start(bf16[768,2688]{1,0:T(8,128)(2,1)} %broadcast_select_fusion), channel_id=1, source_target_pairs={{0,16},{16,0},{1,17},{17,1},{2,18},{18,2},{3,19},{19,3},{4,20},{20... | collective-permute-start | bytes 12386312 | tf_op jit(solution)/shard_map/ppermute | solution.py:1013
  490.7 6.7 %collective-permute-start.11 = (f32[8,768]{1,0:T(8,128)S(1)}, f32[8,768]{1,0:T(8,128)S(1)}, u32[]{:S(2)}, u32[]{:S(2)}) collective-permute-start(f32[8,768]{1,0:T(8,128)S(1)} %broadcast_select_fusion.16), channel_id=1, source_target_pairs={{0,16},{16,0},{1,17},{17,1},{2,18},{18,2},{3,19},{19,3},{4,20},{20... | collective-permute-start | bytes 73736 | tf_op jit(solution)/shard_map/ppermute | solution.py:1013
  498.5 95.9 %reduce-scatter.5.cloned.1.call-start = ((), (), s32[]{:S(2)}) async-start(), calls=%async_computation.2 | async-start | bytes 5160960 | tf_op jit(solution)/shard_map/reduce_scatter | solution.py:1110
  505.7 1.4 copy-start.2
  507.1 3.8 copy-start.3
  507.1 3.8 copy-start.10
  510.5 8.8 %collective-permute-start.7 = (bf16[1024,768]{1,0:T(8,128)(2,1)}, bf16[1024,768]{1,0:T(8,128)(2,1)}, u32[]{:S(2)}, u32[]{:S(2)}) collective-permute-start(bf16[1024,768]{1,0:T(8,128)(2,1)} %get-tuple-element.134), channel_id=1, source_target_pairs={{0,16},{16,0},{1,17},{17,1},{2,18},{18,2},{3,19},{19,3},{4,20},{20... | collective-permute-start | bytes 4718600 | tf_op jit(solution)/shard_map/ppermute | solution.py:1013
  510.9 8.5 %copy-start.4 = (bf16[1,1,1024,768]{3,2,1,0:T(8,128)(2,1)S(1)}, bf16[1,1,1024,768]{3,2,1,0:T(8,128)(2,1)}, u32[]{:S(2)}) copy-start(bf16[1,1,1024,768]{3,2,1,0:T(8,128)(2,1)} %get-tuple-element.133) | copy-start | bytes 4718596
  512.8 10.4 %collective-permute-start.9 = (bf16[1024,768]{1,0:T(8,128)(2,1)}, bf16[1024,768]{1,0:T(8,128)(2,1)}, u32[]{:S(2)}, u32[]{:S(2)}) collective-permute-start(bf16[1024,768]{1,0:T(8,128)(2,1)} %get-tuple-element.132), channel_id=1, source_target_pairs={{0,16},{16,0},{1,17},{17,1},{2,18},{18,2},{3,19},{19,3},{4,20},{20... | collective-permute-start | bytes 4718600 | tf_op jit(solution)/shard_map/ppermute | solution.py:1013
  519.4 3.8 copy-start.5
  595.7 1.4 copy-start.9
  599.0 11.7 %copy-start.1 = (bf16[2,1024,768]{2,1,0:T(8,128)(2,1)S(1)}, bf16[2,1024,768]{2,1,0:T(8,128)(2,1)}, u32[]{:S(2)}) copy-start(bf16[2,1024,768]{2,1,0:T(8,128)(2,1)} %param.15) | copy-start | bytes 9437188
Sparse Core Ops, SparseCore 0:
  498.6 19.3 reduce-scatter.6
  520.5 73.8 reduce-scatter.4

commit v2 on v1

v2 whole, which is shorter than its diff:
```python
import functools
import math

import jax
import jax.numpy as jnp
from jax import lax
from jax.experimental import pallas as pl
from jax.experimental.pallas import tpu as pltpu
from jax.sharding import PartitionSpec as P

TILE = 64
LANES = 128
MASKED = -1e30
EPSILON = 1e-05
FAR = -(1 << 20)
MESH = pl.DeviceIdType.MESH
BF = jnp.bfloat16
F32 = jnp.float32
GELU_A = 0.044715
GELU_K = math.sqrt(2.0 / math.pi)
LIMIT = 60 * 1024 * 1024


class Sizes:
    def __init__(self, mesh_tensor, mesh_seq, rows, width, heads, hidden):
        self.T, self.S = mesh_tensor, mesh_seq
        self.rows, self.width, self.heads, self.hidden = rows, width, heads, hidden
        self.tiles = rows // TILE
        self.slots = heads * self.tiles
        self.cap = -(-self.slots // (mesh_seq - 1))
        self.capg = -(-self.cap // 8) * 8
        self.n = mesh_seq * self.cap
        self.block = rows // mesh_tensor
        self.pad = heads * LANES
        self.share = width // mesh_seq
        self.padded = -(-self.share // 16) * 16
        self.pieces = (hidden, LANES, self.pad)


SEND, INV, ORD, CONT, ARR, POS, LAST, ENDS = range(8)
WEIGHTS = ("vec", "w1", "swt", "wo", "wup", "wdn")
KEPT = ("n1", "q", "kvt", "st", "p", "ckv", "o", "mid", "n2", "u", "act")


def nn(a, b):
    return jnp.dot(a, b, preferred_element_type=F32)


def nt(a, b):
    return lax.dot_general(a, b, (((1,), (1,)), ((), ())), preferred_element_type=F32)


def tn(a, b):
    return lax.dot_general(a, b, (((0,), (0,)), ((), ())), preferred_element_type=F32)


def normed(x):
    centred = x - jnp.mean(x, axis=-1, keepdims=True)
    spread = lax.rsqrt(jnp.mean(centred * centred, axis=-1, keepdims=True) + EPSILON)
    return centred * spread, spread


def norm_back(grad, gain, y, spread):
    scaled = grad * gain
    return spread * (
        scaled
        - jnp.mean(scaled, axis=-1, keepdims=True)
        - y * jnp.mean(scaled * y, axis=-1, keepdims=True)
    )


def partner(me, step):
    return (me // 2 + step // 2) % 2 * 2 + (me % 2 + step % 2) % 2


def column_sum(x):
    return jnp.sum(x, axis=0, keepdims=True)


def smem():
    return pl.BlockSpec(memory_space=pltpu.SMEM)


def vmem():
    return pl.BlockSpec(memory_space=pltpu.VMEM)


def anywhere():
    return pl.BlockSpec(memory_space=pl.ANY)


def grid_of(shape, axis):
    return lax.broadcasted_iota(jnp.int32, shape, axis)


def prepare_kernel(
    z,
    ends_ref,
    sel_ref,
    win_ref,
    bin_ref,
    sw_ref,
    wout_ref,
    bout_ref,
    bup_ref,
    bdn_ref,
    gain_ref,
    shift_ref,
    vec_ref,
    w1_ref,
    swt_ref,
    wo_ref,
    rt0_ref,
    rt1_ref,
):
    inner, head = win_ref.shape[2], win_ref.shape[2] // z.heads
    row, col = grid_of((inner, z.pad), 0), grid_of((inner, z.pad), 1)
    lane_of = row // head * LANES + row % head
    first = (col == lane_of).astype(F32)
    second = (col == lane_of + head).astype(F32)
    low, high = first.astype(BF), second.astype(BF)
    scaled = (first * head**-0.5).astype(BF)
    w1_ref[:, : z.pad] = nn(win_ref[0], scaled).astype(BF)
    w1_ref[:, z.pad :] = (nn(win_ref[1], low) + nn(win_ref[2], high)).astype(BF)
    vec_ref[0:1, :] = gain_ref[...].astype(F32)[0:1]
    vec_ref[1:2, :] = shift_ref[...].astype(F32)[0:1]
    vec_ref[2:3, : z.pad] = nn(bin_ref[...], scaled)[0:1]
    vec_ref[2:3, z.pad :] = nn(bin_ref[...], high)[1:2]
    vec_ref[3:4, :] = bout_ref[...].astype(F32)
    vec_ref[4:5, :] = gain_ref[...].astype(F32)[1:2]
    vec_ref[5:6, :] = shift_ref[...].astype(F32)[1:2]
    vec_ref[6:7, :] = bup_ref[...].astype(F32)
    vec_ref[7:8, :] = bdn_ref[...].astype(F32)
    unit = (grid_of((16, z.heads), 0) == grid_of((16, z.heads), 1)).astype(F32).astype(BF)
    swt_ref[...] = nt(unit, sw_ref[...]).astype(BF)
    wo_ref[0:inner, :] = wout_ref[...]
    wo_ref[inner:, :] = jnp.zeros((2 * LANES - inner, z.width), BF)

    at = lax.axis_index("seq")
    n, slots, cap = z.n, z.slots, z.cap
    shift = z.tiles.bit_length() - 1
    near = 1e-3

    def total(mask, value, axis):
        return jnp.sum(jnp.where(mask, value, 0.0), axis=axis, keepdims=True)

    def whole(x):
        return (x + near).astype(jnp.int32)

    for layer, rt in enumerate((rt0_ref, rt1_ref)):
        rt[...] = jnp.zeros((8, LANES), jnp.int32)
        chosen = sel_ref[layer]
        owner = lax.shift_right_arithmetic(chosen, shift)
        sub, lan = grid_of((slots, n), 0), grid_of((slots, n), 1)
        wide = jnp.zeros((slots, n), jnp.int32)
        for d in range(z.S):
            column = jnp.sum(
                jnp.where(
                    grid_of((slots, slots), 0) == grid_of((slots, slots), 1),
                    chosen[d : d + 1].astype(F32) + 1.0,
                    0.0,
                ),
                axis=1,
                keepdims=True,
            )
            wide = jnp.where(lan // cap == d, whole(column) - 1, wide)
        mine = lax.shift_right_arithmetic(wide, shift) == at
        order = nn(
            (grid_of((slots, slots), 0) > grid_of((slots, slots), 1)).astype(F32), mine.astype(F32)
        )
        taken = mine & (whole(order) == lan % cap)
        head_of = sub // z.tiles
        inner_tile = wide - at * z.tiles
        rt[SEND : SEND + 1, :n] = whole(
            total(taken, (head_of * (z.tiles + 1) + inner_tile).astype(F32), 0)
        ) + 1
        present = jnp.sum(taken.astype(F32), axis=0, keepdims=True)
        key = total(taken, (head_of * z.tiles + inner_tile - slots).astype(F32), 0) + slots
        own = jnp.sum(
            jnp.where(grid_of((z.S, slots), 0) == at, chosen.astype(F32) + 1.0, 0.0), axis=0, keepdims=True
        )
        square_row, square_col = grid_of((slots, slots), 0), grid_of((slots, slots), 1)
        own_column = total(square_row == square_col, own, 1)
        own_row = whole(own) - 1
        own_col = whole(own_column) - 1
        owner_row = lax.shift_right_arithmetic(own_row, shift)
        owner_col = lax.shift_right_arithmetic(own_col, shift)
        same = owner_row == owner_col
        place_row = whole(jnp.sum((same & (square_row < square_col)).astype(F32), axis=0, keepdims=True))
        place_col = whole(jnp.sum((same & (square_col < square_row)).astype(F32), axis=1, keepdims=True))
        live = own_row >= 0
        rt[ARR : ARR + 1, :slots] = jnp.where(live, owner_row * cap + place_row, at * cap)
        rt[POS : POS + 1, :slots] = jnp.where(live, own_row * TILE, FAR)
        matched = (owner_col == lan // cap) & (place_col == lan % cap)
        rt[INV : INV + 1, :n] = whole(total(matched, sub.astype(F32), 0))
        big_row, big_col = grid_of((n, n), 0), grid_of((n, n), 1)
        key_col = total(big_row == big_col, key, 1)
        rank = jnp.sum(
            ((key < key_col) | ((key == key_col) & (big_col < big_row))).astype(F32), axis=1, keepdims=True
        )
        at_rank = whole(rank) == big_col
        rt[ORD : ORD + 1, :n] = whole(total(at_rank, big_row.astype(F32), 0))
        sorted_key = total(at_rank, key_col, 0)
        before = total(whole(rank) + 1 == big_col, key_col + 1.0, 0) - 1.0
        rt[CONT : CONT + 1, :n] = (sorted_key == before).astype(jnp.int32)
        tile = grid_of((n, slots), 1).astype(F32)
        upto = jnp.sum((key_col <= tile).astype(F32), axis=0, keepdims=True)
        has = jnp.sum((key_col == tile).astype(F32), axis=0, keepdims=True)
        rt[LAST : LAST + 1, :slots] = whole(jnp.where(has > 0.5, upto - 1.0, n * 1.0))
        rt[ENDS : ENDS + 1, :] = jnp.where(grid_of((1, LANES), 1) == 0, ends_ref[0], ends_ref[1])


def prepare(z, ends, sel, win, bin_, sw, wout, bout, bup, bdn, gain, shift):
    table = jax.ShapeDtypeStruct((8, LANES), jnp.int32)
    outs = pl.pallas_call(
        functools.partial(prepare_kernel, z),
        out_shape=(
            jax.ShapeDtypeStruct((8, z.width), F32),
            jax.ShapeDtypeStruct((z.width, 2 * z.pad), BF),
            jax.ShapeDtypeStruct((16, z.width), BF),
            jax.ShapeDtypeStruct((2 * LANES, z.width), BF),
            table,
            table,
        ),
        in_specs=[smem()] + [vmem()] * 10,
        out_specs=tuple(vmem() for _ in range(6)),
        name="prepare",
    )(ends, sel, win, bin_, sw, wout, bout, bup, bdn, gain, shift)
    return dict(zip(WEIGHTS[:4], outs)), outs[4:]


def to_tensor(step, me):
    return {"tensor": partner(me, step)}


def remote(src, dst, send, recv, target):
    return pltpu.make_async_remote_copy(
        src_ref=src, dst_ref=dst, send_sem=send, recv_sem=recv, device_id=target, device_id_type=MESH
    )


def signal(target, barrier):
    pl.semaphore_signal(barrier, inc=1, device_id=target, device_id_type=MESH)


class Saver:
    def __init__(self, sems):
        self.sems, self.copies = sems, []

    def save(self, src, dst):
        copy = pltpu.make_async_copy(src, dst, self.sems.at[len(self.copies)])
        copy.start()
        self.copies.append(copy)

    def finish(self):
        for copy in self.copies:
            copy.wait()


FORWARD_OUTS = KEPT + ("res",)
FORWARD_SCRATCH = (
    "gt", "gate", "edge", "edge_gate", "send_kv", "send_gate", "got_gate", "far_gate", "wo_all", "o_all",
    "part_send", "part_got", "own_part", "kv_ss", "kv_rs", "gate_ss", "gate_rs", "edge_ss", "edge_rs",
    "wo_ss", "wo_rs", "o_ss", "o_rs", "part_ss", "part_rs", "res_ss", "res_rs", "swap_ss", "swap_rs", "load", "saved",
)


class Refs:
    def __init__(self, names, refs):
        assert len(names) == len(refs), (len(names), len(refs))
        for name, ref in zip(names, refs):
            setattr(self, name, ref)


def forward_kernel(z, layer, *refs):
    count = len(WEIGHTS)
    rt, r_ref = refs[:2]
    own = dict(zip(WEIGHTS, refs[2 : 2 + count]))
    refs = refs[2 + count :]
    theirs = None
    if layer == 1:
        theirs, refs = dict(zip(WEIGHTS, refs[:count])), refs[count:]
    outs, refs = dict(zip(FORWARD_OUTS, refs)), refs[len(FORWARD_OUTS) :]
    if layer == 0:
        theirs, refs = dict(zip(WEIGHTS, refs[:count])), refs[count:]
    held, refs = Refs(FORWARD_OUTS, refs[: len(FORWARD_OUTS)]), refs[len(FORWARD_OUTS) :]
    used, refs = dict(zip(WEIGHTS, refs[:count])), refs[count:]
    s = Refs(FORWARD_SCRATCH, refs)
    me, at, core = lax.axis_index("tensor"), lax.axis_index("seq"), lax.axis_index("section")
    last = z.S - 1
    first_row = at * z.rows
    vec = used["vec"]

    def load(i, source):
        name = WEIGHTS[i]
        return pltpu.make_async_copy(source[name], used[name], s.load.at[i])

    def swap(i):
        name = WEIGHTS[i]
        return remote(own[name], theirs[name], s.swap_ss.at[i], s.swap_rs.at[i], {"section": 1 - core})

    @pl.when(core == layer)
    def _():
        for i in range(count):
            load(i, own).start()

    if layer == 1:

        @pl.when(core != layer)
        def _():
            for i in range(count):
                load(i, theirs).start()

    def ready(*wanted):
        if layer == 0:

            @pl.when(core != layer)
            def _():
                for i in wanted:
                    swap(i).wait_recv()
                    load(i, theirs).start()

        for i in wanted:
            load(i, own).wait()

    held.ckv[at * z.cap] = jnp.zeros((TILE, LANES), BF)
    barrier = pltpu.get_barrier_semaphore()
    for step in range(1, z.T):
        signal(to_tensor(step, me), barrier)
    if layer == 0:
        signal({"section": 1 - core}, barrier)

    def greet(d, _):
        signal({"seq": d}, barrier)
        return 0

    lax.fori_loop(0, at, greet, 0)
    pl.semaphore_wait(barrier, z.T - 1 + last - at + (layer == 0))
    if layer == 0:
        for i in range(count):
            swap(i).start()
    saver = Saver(s.saved)
    per_block = z.block // TILE
    ready(0)

    def norm_in(b, _):
        rows = pl.ds(b * z.block, z.block)
        y, _ = normed(r_ref[rows, :].astype(F32))
        held.n1[rows, :] = (y * vec[0:1, :] + vec[1:2, :]).astype(BF)
        return 0

    lax.fori_loop(0, z.T, norm_in, 0)
    saver.save(held.n1, outs["n1"])
    ready(1, 2)

    def project(b, _):
        rows = pl.ds(b * z.block, z.block)
        qkv = (nn(held.n1[rows, :], used["w1"][...]) + vec[2:3, :]).astype(BF)
        held.q[rows, :] = qkv[:, : z.pad]
        for h in range(z.heads):
            pairs = qkv[:, z.pad + h * LANES : z.pad + (h + 1) * LANES]
            held.kvt[pl.ds(h * (z.tiles + 1) + 1 + b * per_block, per_block)] = pairs.reshape(
                per_block, TILE, LANES
            )
        return 0

    lax.fori_loop(0, z.T, project, 0)
    score = nt(used["swt"][...], held.n1[...])[0:8]
    held.st[...] = score
    gate = jnp.minimum(score, 0.0) - jnp.log1p(jnp.exp(-jnp.abs(score)))
    s.gt[:, 0:LANES] = jnp.zeros((8, LANES), F32)
    s.gt[:, LANES : LANES + z.rows] = gate.astype(BF).astype(F32)
    s.gt[:, LANES + z.rows :] = jnp.zeros((8, LANES), F32)
    for t in range(z.tiles + 1):
        for h in range(z.heads):
            s.gate[h * (z.tiles + 1) + t, 0:1, :] = s.gt[
                h : h + 1, TILE + t * TILE : TILE + t * TILE + LANES
            ]

    def edge_copies():
        after = {"seq": jnp.minimum(at + 1, last)}
        return [
            remote(
                held.kvt.at[h * (z.tiles + 1) + z.tiles],
                s.edge.at[h],
                s.edge_ss.at[h],
                s.edge_rs.at[h],
                after,
            )
            for h in range(z.heads)
        ] + [
            remote(
                s.gt.at[:, pl.ds(z.rows, LANES)],
                s.edge_gate,
                s.edge_ss.at[z.heads],
                s.edge_rs.at[z.heads],
                after,
            )
        ]

    @pl.when(at < last)
    def _():
        for copy in edge_copies():
            copy.start()

    def tile_copies(d, source):
        return (
            remote(
                s.send_kv.at[d],
                held.ckv.at[pl.ds(source * z.cap, z.cap)],
                s.kv_ss.at[d],
                s.kv_rs.at[source],
                {"seq": d},
            ),
            remote(
                s.send_gate.at[d], s.got_gate.at[source], s.gate_ss.at[d], s.gate_rs.at[source], {"seq": d}
            ),
        )

    def pack(k, _):
        d = z.S - 1 - k

        def slot(i, _):
            u = rt[SEND, d * z.cap + i]
            s.send_kv[d, i] = held.kvt[u]
            s.send_gate[d, pl.ds(i, 1), :] = s.gate[u][0:1]
            return 0

        lax.fori_loop(0, z.cap, slot, 0)
        for copy in tile_copies(d, at):
            copy.start()
        return 0

    lax.fori_loop(0, last - at, pack, 0)
    ready(3)

    def wo_copy(step):
        return remote(
            used["wo"], s.wo_all.at[me], s.wo_ss.at[step], s.wo_rs.at[step], to_tensor(step, me)
        )

    for step in range(1, z.T):
        wo_copy(step).start()
    s.wo_all[me] = used["wo"][...]
    saver.save(held.q, outs["q"])
    saver.save(held.st, outs["st"])

    def landed(source, _):
        for copy in tile_copies(last, source):
            copy.wait_recv()
        for i in range(z.cap):
            s.far_gate[source * z.cap + i, 0:1, :] = s.got_gate[source, i : i + 1, :]
        return 0

    lax.fori_loop(0, at, landed, 0)
    lane = grid_of((TILE, LANES), 1)
    row = grid_of((TILE, LANES), 0)
    for h in range(z.heads):
        held.kvt[h * (z.tiles + 1)] = jnp.zeros((TILE, LANES), BF)

    @pl.when(at > 0)
    def _():
        for copy in edge_copies():
            copy.wait_recv()
        for h in range(z.heads):
            held.kvt[h * (z.tiles + 1)] = s.edge[h]
            s.gate[h * (z.tiles + 1), 0:1, :] = jnp.where(
                lane[0:1] < TILE,
                pltpu.roll(s.edge_gate[...], TILE, 1)[h : h + 1],
                s.gate[h * (z.tiles + 1), 0:1, :],
            )

    saver.save(held.kvt, outs["kvt"])
    saver.save(held.ckv, outs["ckv"])

    def attend(t):
        base = pl.multiple_of(t * TILE, TILE)
        query = first_row + base + row
        begin = jnp.where(
            query >= rt[ENDS, 1],
            rt[ENDS, 1],
            jnp.where(query >= rt[ENDS, 0], rt[ENDS, 0], 0),
        )
        key = first_row + base - TILE + lane
        near_ok = (key <= query) & (key > query - TILE) & (key >= begin)
        mixed = []
        for h in range(z.heads):
            cols = slice(h * LANES, (h + 1) * LANES)
            u = h * z.tiles + t
            arrived = rt[ARR, u]
            query_tile = held.q[pl.ds(base, TILE), cols]
            near = held.kvt[pl.ds(h * (z.tiles + 1) + t, 2)].reshape(2 * TILE, LANES)
            far = held.ckv[arrived]
            near_score = nt(query_tile, near) + s.gate[h * (z.tiles + 1) + t, 0:1, :]
            far_score = nt(query_tile, jnp.concatenate([far, far], axis=0)) + s.far_gate[arrived][0:1]
            far_ok = (rt[POS, u] + lane >= begin) & (lane < TILE)
            near_score = jnp.where(near_ok, near_score, MASKED)
            far_score = jnp.where(far_ok, far_score, MASKED)
            top = jnp.max(jnp.maximum(near_score, far_score), axis=-1, keepdims=True)
            near_exp = jnp.exp(near_score - top)
            far_exp = jnp.exp(far_score - top)
            scale = 1.0 / jnp.sum(near_exp + far_exp, axis=-1, keepdims=True)
            near_p = (near_exp * scale).astype(BF)
            far_p = (far_exp * scale).astype(BF)
            held.p[t * z.heads + h, :, 0:LANES] = near_p
            held.p[t * z.heads + h, :, LANES:] = far_p
            mixed.append(nn(near_p, near) + nn(far_p[:, :TILE], far))
        pair = jnp.where(lane < TILE, pltpu.roll(mixed[0], TILE, 1), mixed[1]).astype(BF)
        single = pltpu.roll(mixed[2], TILE, 1).astype(BF)
        held.o[pl.ds(base, TILE), 0:LANES] = pair
        held.o[pl.ds(base, TILE), LANES:] = single

    def o_copy(step, b):
        rows = pl.ds(b * z.block, z.block)
        return remote(
            held.o.at[rows, :],
            s.o_all.at[me, rows, :],
            s.o_ss.at[step * z.T + b],
            s.o_rs.at[step * z.T + b],
            to_tensor(step, me),
        )

    def attend_block(b, _):
        def pair(i, _):
            attend(b * per_block + 2 * i)
            attend(b * per_block + 2 * i + 1)
            return 0

        lax.fori_loop(0, per_block // 2, pair, 0)
        for step in range(1, z.T):
            o_copy(step, b).start()
        rows = pl.ds(b * z.block, z.block)
        s.o_all[me, rows, :] = held.o[rows, :]
        return 0

    lax.fori_loop(0, z.T, attend_block, 0)
    saver.save(held.p, outs["p"])
    saver.save(held.o, outs["o"])
    ready(4, 5)
    for step in range(1, z.T):
        wo_copy(step).wait()

    def part_copy(step):
        return remote(
            s.part_send.at[step - 1],
            s.part_got.at[step - 1],
            s.part_ss.at[step - 1],
            s.part_rs.at[step - 1],
            to_tensor(step, me),
        )

    def feed(k, _):
        step = (k + 1) % z.T
        block = partner(me, step)
        rows = pl.ds(pl.multiple_of(block * z.block, z.block), z.block)
        for other in range(1, z.T):
            o_copy(other, block).wait_recv()
        mixed = nn(s.o_all[0, rows, :], s.wo_all[0])
        for other in range(1, z.T):
            mixed += nn(s.o_all[other, rows, :], s.wo_all[other])
        middle = r_ref[rows, :].astype(F32) + mixed + vec[3:4, :]
        held.mid[...] = middle
        y, _ = normed(middle)
        n2 = (y * vec[4:5, :] + vec[5:6, :]).astype(BF)
        held.n2[rows, :] = n2
        u = nn(n2, used["wup"][...]) + vec[6:7, :]
        held.u[rows, :] = u.astype(BF)
        act = (0.5 * u * (1.0 + jnp.tanh(GELU_K * (u + GELU_A * u * u * u)))).astype(BF)
        held.act[rows, :] = act
        s.own_part[...] = nn(act, used["wdn"][...])

        @pl.when(step > 0)
        def _():
            s.part_send[step - 1] = s.own_part[...].astype(BF)
            part_copy(step).start()

        return 0

    lax.fori_loop(0, z.T, feed, 0)
    for name in ("mid", "n2", "u", "act"):
        saver.save(getattr(held, name), outs[name])
    total = held.mid[...] + s.own_part[...] + vec[7:8, :]
    for step in range(1, z.T):
        part_copy(step).wait_recv()
        total += s.part_got[step - 1].astype(F32)
    own_rows = pl.ds(pl.multiple_of(me * z.block, z.block), z.block)
    held.res[own_rows, :] = total.astype(BF)

    def res_copy(step):
        return remote(
            held.res.at[own_rows, :],
            held.res.at[own_rows, :],
            s.res_ss.at[step],
            s.res_rs.at[step],
            to_tensor(step, me),
        )

    for step in range(1, z.T):
        res_copy(step).start()
    for step in range(1, z.T):
        part_copy(step).wait_send()
        for b in range(z.T):
            o_copy(step, b).wait_send()

    def sent(d, _):
        for copy in tile_copies(d, at):
            copy.wait_send()
        return 0

    lax.fori_loop(at + 1, z.S, sent, 0)

    @pl.when(at < last)
    def _():
        for copy in edge_copies():
            copy.wait_send()

    if layer == 0:

        @pl.when(core == layer)
        def _():
            for i in range(count):
                swap(i).wait_recv()

        for i in range(count):
            swap(i).wait_send()
    for step in range(1, z.T):
        res_copy(step).wait()
    saver.save(held.res, outs["res"])
    saver.finish()


def forward(z, layer, route, r, own, theirs):
    rows, width, heads = z.rows, z.width, z.heads
    shapes = dict(
        n1=((rows, width), BF),
        q=((rows, z.pad), BF),
        kvt=((heads * (z.tiles + 1), TILE, LANES), BF),
        st=((8, rows), F32),
        p=((z.slots, TILE, 2 * LANES), BF),
        ckv=((z.n, TILE, LANES), BF),
        o=((rows, 2 * LANES), BF),
        mid=((z.block, width), F32),
        n2=((rows, width), BF),
        u=((rows, z.hidden), BF),
        act=((rows, z.hidden), BF),
        res=((rows, width), BF),
    )
    dma = pltpu.SemaphoreType.DMA
    shaped = [jax.ShapeDtypeStruct(*shapes[name]) for name in FORWARD_OUTS]
    mine = [own[name] for name in WEIGHTS]
    if layer == 0:
        shaped += [jax.ShapeDtypeStruct(value.shape, value.dtype) for value in mine]
        inputs = [route, r, *mine]
    else:
        inputs = [route, r, *mine, *(theirs[name] for name in WEIGHTS)]
    outs = pl.pallas_call(
        functools.partial(forward_kernel, z, layer),
        out_shape=tuple(shaped),
        in_specs=[smem(), vmem()] + [anywhere()] * (len(inputs) - 2),
        out_specs=tuple(anywhere() for _ in shaped),
        scratch_shapes=[
            *(pltpu.VMEM(*shapes[name]) for name in FORWARD_OUTS),
            *(pltpu.VMEM(value.shape, value.dtype) for value in mine),
            pltpu.VMEM((8, rows + 2 * LANES), F32),
            pltpu.VMEM((heads * (z.tiles + 1), 8, LANES), F32),
            pltpu.VMEM((heads, TILE, LANES), BF),
            pltpu.VMEM((8, LANES), F32),
            pltpu.VMEM((z.S, z.cap, TILE, LANES), BF),
            pltpu.VMEM((z.S, z.capg, LANES), F32),
            pltpu.VMEM((z.S, z.capg, LANES), F32),
            pltpu.VMEM((z.n, 8, LANES), F32),
            pltpu.VMEM((z.T, 2 * LANES, width), BF),
            pltpu.VMEM((z.T, rows, 2 * LANES), BF),
            pltpu.VMEM((z.T - 1, z.block, width), BF),
            pltpu.VMEM((z.T - 1, z.block, width), BF),
            pltpu.VMEM((z.block, width), F32),
            dma((z.S,)),
            dma((z.S,)),
            dma((z.S,)),
            dma((z.S,)),
            dma((heads + 1,)),
            dma((heads + 1,)),
            dma((z.T,)),
            dma((z.T,)),
            dma((z.T * z.T,)),
            dma((z.T * z.T,)),
            dma((z.T,)),
            dma((z.T,)),
            dma((z.T,)),
            dma((z.T,)),
            dma((len(WEIGHTS),)),
            dma((len(WEIGHTS),)),
            dma((len(WEIGHTS),)),
            dma((len(FORWARD_OUTS),)),
        ],
        compiler_params=pltpu.CompilerParams(
            collective_id=layer, has_side_effects=True, vmem_limit_bytes=LIMIT
        ),
        name=f"forward{layer}",
    )(*inputs)
    kept = dict(zip(FORWARD_OUTS, outs))
    return (kept, dict(zip(WEIGHTS, outs[len(FORWARD_OUTS) :]))) if layer == 0 else (kept, theirs)


BACKWARD_SCRATCH = (
    "du", "part_send", "part_got", "own_part", "dr2", "ob", "dout", "dqkv", "dkv", "dgate", "far", "far_gate",
    "send_kv", "send_gate", "got_kv", "got_gate", "got_gate_row", "edge_send", "edge_got", "edge_gate_got", "sum",
    "gate_sum", "tile_gate", "ds", "stat", "stat_got", "grad",
    "pa", "pb", "pc", "xa", "xb", "xc", "sa", "sb", "sc", "ta", "tb", "tc", "ha", "hb", "hc",
    "kv_ss", "kv_rs", "gate_ss", "gate_rs", "edge_ss", "edge_rs", "part_ss", "part_rs", "ob_ss", "ob_rs",
    "grad_ss", "grad_rs", "stat_ss", "stat_rs", "give_ss", "give_rs", "cross_ss", "cross_rs", "hand_ss", "hand_rs",
    "move_ss", "move_rs", "load", "saved",
)


def backward_kernel(z, layer, *refs):
    count = len(WEIGHTS)
    rt = refs[0]
    c_any, r_any, first_any, second_any = refs[1:5]
    refs = refs[5:]
    own, refs = dict(zip(WEIGHTS, refs[:count])), refs[count:]
    theirs, refs = dict(zip(WEIGHTS, refs[:count])), refs[count:]
    kept, refs = dict(zip(KEPT, refs[: len(KEPT)])), refs[len(KEPT) :]
    grad_out, both_out, g_out = refs[:3]
    refs = refs[3:]
    c_ref, r_ref, refs = refs[0], refs[1], refs[2:]
    used, refs = dict(zip(WEIGHTS, refs[:count])), refs[count:]
    k, refs = Refs(KEPT, refs[: len(KEPT)]), refs[len(KEPT) :]
    s = Refs(BACKWARD_SCRATCH, refs)
    me, at, core = lax.axis_index("tensor"), lax.axis_index("seq"), lax.axis_index("section")
    last = z.S - 1
    vec = used["vec"]
    own_rows = pl.ds(pl.multiple_of(me * z.block, z.block), z.block)
    W = z.width
    sources = {"c": (c_any, c_ref)}
    sources |= {name: (kept[name], getattr(k, name)) for name in KEPT}
    sources["r"] = (r_any.at[own_rows, :], r_ref)
    order = ("c", "wdn", "u", "wup", "act", "n2", "vec", "mid", "wo", "p", "q", "kvt", "ckv", "o", "st", "w1", "swt", "n1", "r")

    def loads(name, which):
        i = order.index(name)
        if name in WEIGHTS:
            return pltpu.make_async_copy(which[name], used[name], s.load.at[i])
        return pltpu.make_async_copy(*sources[name], s.load.at[i])

    for name in order:
        if name in WEIGHTS:

            @pl.when(core == layer)
            def _(name=name):
                loads(name, own).start()

            @pl.when(core != layer)
            def _(name=name):
                loads(name, theirs).start()
        else:
            loads(name, None).start()

    def ready(*names):
        for name in names:
            loads(name, own).wait()

    barrier = pltpu.get_barrier_semaphore()
    for step in range(1, z.T):
        signal(to_tensor(step, me), barrier)
    signal({"section": 1 - core}, barrier)

    def greet(i, _):
        signal({"seq": (at + i) % z.S}, barrier)
        return 0

    lax.fori_loop(1, z.S, greet, 0)
    pl.semaphore_wait(barrier, z.T - 1 + 1 + last)
    saver = Saver(s.saved)
    across = {"section": 1 - core}

    def move(src, i, part):
        return remote(src.at[part], both_out.at[core].at[part], s.move_ss.at[i], s.move_rs.at[i], across)

    def keep(src, part):
        return pltpu.make_async_copy(src.at[part], both_out.at[core].at[part], s.saved.at[3])

    everything = pl.ds(0, z.rows)

    @pl.when(core == 0)
    def _():
        move(second_any, 0, everything).start()

    if layer == 1:

        @pl.when(core == 0)
        def _():
            keep(first_any, everything).start()

        @pl.when(core == 1)
        def _():
            move(first_any, 0, everything).start()
            keep(second_any, everything).start()

    else:

        @pl.when(core == 1)
        def _():
            keep(second_any, everything).start()

    def part_copy(step, phase):
        return remote(
            s.part_send.at[phase, step - 1],
            s.part_got.at[phase, step - 1],
            s.part_ss.at[phase, step],
            s.part_rs.at[phase, step],
            to_tensor(step, me),
        )

    ready("c", "wdn", "u", "wup")

    def ff_back(i, _):
        step = (i + 1) % z.T
        rows = pl.ds(pl.multiple_of(partner(me, step) * z.block, z.block), z.block)
        u = k.u[rows, :].astype(F32)
        squared = u * u
        bent = jnp.tanh(GELU_K * (u + GELU_A * squared * u))
        slope = 0.5 * (1.0 + bent) + 0.5 * u * (1.0 - bent * bent) * (
            GELU_K * (1.0 + 3.0 * GELU_A * squared)
        )
        du = (nt(c_ref[rows, :], used["wdn"][...]) * slope).astype(BF)
        s.du[rows, :] = du
        s.own_part[...] = nt(du, used["wup"][...])

        @pl.when(step > 0)
        def _():
            s.part_send[0, step - 1] = s.own_part[...].astype(BF)
            part_copy(step, 0).start()

        return 0

    lax.fori_loop(0, z.T, ff_back, 0)
    ones = jnp.ones((16, z.rows), BF)
    s.stat[...] = jnp.zeros((24, W), F32)

    mine = {0: s.pa, 1: s.pb, 2: s.pc}
    theirs_part = {0: s.xa, 1: s.xb, 2: s.xc}
    summed = {0: s.sa, 1: s.sb, 2: s.sc}
    crossed = {0: s.ta, 1: s.tb, 2: s.tc}
    handed = {0: s.ha, 1: s.hb, 2: s.hc}

    def give(piece):
        return remote(
            mine[piece].at[1 - core], theirs_part[piece], s.give_ss.at[piece], s.give_rs.at[piece], across
        )

    def cross(piece, d, source):
        return remote(
            summed[piece].at[d],
            crossed[piece].at[source],
            s.cross_ss.at[piece, d],
            s.cross_rs.at[piece, source],
            {"seq": d},
        )

    def hand(piece):
        return remote(
            summed[piece].at[at], handed[piece], s.hand_ss.at[piece], s.hand_rs.at[piece], across
        )

    span = math.lcm(z.share, 16)

    def add_up(piece):
        give(piece).wait_recv()

        def chunk(i, _):
            rows = pl.ds(pl.multiple_of(i * span, span), span)
            value = mine[piece][core, rows, :].astype(F32) + theirs_part[piece][rows, :].astype(F32)
            for j in range(span // z.share):
                d = i * (span // z.share) + j
                rows_of = value[j * z.share : (j + 1) * z.share]
                if z.padded > z.share:
                    rows_of = jnp.concatenate(
                        [rows_of, jnp.zeros((z.padded - z.share, value.shape[1]), F32)], axis=0
                    )
                summed[piece][d] = rows_of.astype(BF)

                @pl.when(d != at)
                def _():
                    cross(piece, d, at).start()

            return 0

        lax.fori_loop(0, W // span, chunk, 0)

    offsets = (0, z.pieces[0], z.pieces[0] + z.pieces[1])

    def reduce(piece):
        def wait(i, _):
            d = (at + i) % z.S
            cross(piece, d, d).wait_recv()
            return 0

        lax.fori_loop(1, z.S, wait, 0)

        def add(i, running):
            return running + crossed[piece][(at + i) % z.S].astype(F32)

        total = lax.fori_loop(1, z.S, add, summed[piece][at].astype(F32))
        cols = slice(offsets[piece], offsets[piece] + z.pieces[piece])
        g_out[core, :, cols] = total[: z.share]

        @pl.when(core != layer)
        def _():
            summed[piece][at] = total.astype(BF)
            hand(piece).start()

    def take(piece):
        cols = slice(offsets[piece], offsets[piece] + z.pieces[piece])

        @pl.when(core == layer)
        def _():
            hand(piece).wait_recv()
            g_out[1 - core, :, cols] = handed[piece][...].astype(F32)[: z.share]

    ready("act", "n2")
    s.pa[0] = tn(c_ref[...], k.act[...]).astype(BF)
    s.pa[1] = tn(k.n2[...], s.du[...]).astype(BF)
    give(0).start()
    s.stat[8:9, :] = nn(ones, s.du[...])[0:1]
    s.stat[9:10, :] = nn(ones, c_ref[...])[0:1]
    ready("vec", "mid", "wo")
    grad = s.own_part[...]
    for step in range(1, z.T):
        part_copy(step, 0).wait_recv()
        grad += s.part_got[0, step - 1].astype(F32)
    y, spread = normed(k.mid[...])
    dr2 = c_ref[own_rows, :].astype(F32) + norm_back(grad, vec[4:5, :], y, spread)
    s.dr2[...] = dr2
    s.ob[own_rows, :] = dr2.astype(BF)

    def rows_copy(ref, sends, recvs, step):
        return remote(
            ref.at[own_rows, :], ref.at[own_rows, :], sends.at[step], recvs.at[step], to_tensor(step, me)
        )

    for step in range(1, z.T):
        rows_copy(s.ob, s.ob_ss, s.ob_rs, step).start()
    s.stat[0:1, :] = column_sum(dr2)
    s.stat[1:2, :] = column_sum(grad * y)
    s.stat[2:3, :] = column_sum(grad)
    s.dkv[...] = jnp.zeros((z.rows + TILE, z.pad), F32)
    add_up(0)
    lane_wide = grid_of((z.block, LANES), 1)

    def out_back(step, _):
        @pl.when(step > 0)
        def _():
            rows_copy(s.ob, s.ob_ss, s.ob_rs, step).wait_recv()

        rows = pl.ds(pl.multiple_of(partner(me, step) * z.block, z.block), z.block)
        dout = nt(s.ob[rows, :], used["wo"][...])
        pair, single = dout[:, :LANES], dout[:, LANES:]
        for h, value in enumerate((pltpu.roll(pair, TILE, 1), pair, pltpu.roll(single, TILE, 1))):
            s.dout[rows, h * LANES : (h + 1) * LANES] = jnp.where(lane_wide < TILE, 0.0, value).astype(BF)
        return 0

    lax.fori_loop(0, z.T, out_back, 0)
    ready("p", "q", "kvt", "ckv")

    def attend_back(t):
        base = pl.multiple_of(t * TILE, TILE)
        for h in range(z.heads):
            cols = slice(h * LANES, (h + 1) * LANES)
            u = h * z.tiles + t
            arrived = rt[ARR, u]
            near = k.kvt[pl.ds(h * (z.tiles + 1) + t, 2)].reshape(2 * TILE, LANES)
            far = k.ckv[arrived]
            query = k.q[pl.ds(base, TILE), cols]
            dout = s.dout[pl.ds(base, TILE), cols]
            near_p = k.p[t * z.heads + h, :, 0:LANES]
            far_p = k.p[t * z.heads + h, :, LANES : LANES + TILE]
            near_pf, far_pf = near_p.astype(F32), far_p.astype(F32)
            near_dp, far_dp = nt(dout, near), nt(dout, far)
            total = jnp.sum(near_pf * near_dp, axis=-1, keepdims=True) + jnp.sum(
                far_pf * far_dp, axis=-1, keepdims=True
            )
            near_dz = (near_pf * (near_dp - total)).astype(BF)
            far_dz = (far_pf * (far_dp - total)).astype(BF)
            s.dqkv[pl.ds(base, TILE), cols] = (nn(near_dz, near) + nn(far_dz, far)).astype(BF)
            s.dkv[pl.ds(base, 2 * TILE), cols] += tn(near_dz, query) + tn(near_p, dout)
            s.far[u] = (tn(far_dz, query) + tn(far_p, dout)).astype(BF)
            s.dgate[t, h : h + 1, :] = column_sum(near_dz.astype(F32))
            s.far_gate[u, 0:1, 0:TILE] = column_sum(far_dz.astype(F32))

    def attend_back_pair(i, _):
        attend_back(2 * i)
        attend_back(2 * i + 1)
        return 0

    lax.fori_loop(0, z.tiles // 2, attend_back_pair, 0)
    s.dgate[z.tiles] = jnp.zeros((8, LANES), F32)

    def edge_copies():
        behind = {"seq": jnp.maximum(at - 1, 0)}
        return (
            remote(s.edge_send, s.edge_got, s.edge_ss.at[0], s.edge_rs.at[0], behind),
            remote(s.dgate.at[0], s.edge_gate_got, s.edge_ss.at[1], s.edge_rs.at[1], behind),
        )

    @pl.when(at > 0)
    def _():
        s.edge_send[...] = s.dkv[0:TILE, :].astype(BF)
        for copy in edge_copies():
            copy.start()

    def tile_copies(d, source):
        return (
            remote(
                s.send_kv.at[d],
                s.got_kv.at[pl.ds(source * z.cap, z.cap)],
                s.kv_ss.at[d],
                s.kv_rs.at[source],
                {"seq": d},
            ),
            remote(
                s.send_gate.at[d], s.got_gate.at[source], s.gate_ss.at[d], s.gate_rs.at[source], {"seq": d}
            ),
        )

    def pack(d, _):
        def slot(i, _):
            u = rt[INV, d * z.cap + i]
            s.send_kv[d, i] = s.far[u]
            s.send_gate[d, pl.ds(i, 1), :] = s.far_gate[u][0:1]
            return 0

        lax.fori_loop(0, z.cap, slot, 0)
        for copy in tile_copies(d, at):
            copy.start()
        return 0

    lax.fori_loop(0, at, pack, 0)
    ready("o")
    out_grad = tn(s.ob[...], k.o[...]).astype(BF)
    s.pb[0] = out_grad[:, :LANES]
    s.pb[1] = out_grad[:, LANES:]
    give(1).start()
    s.sum[z.n] = jnp.zeros((TILE, LANES), F32)
    s.gate_sum[z.n] = jnp.zeros((8, LANES), F32)
    ready("st", "w1", "swt", "n1", "r")
    add_up(1)

    @pl.when(at < last)
    def _():
        for copy in edge_copies():
            copy.wait_recv()
        s.dkv[pl.ds(z.rows, TILE), :] += s.edge_got[...].astype(F32)
        s.dgate[z.tiles] = s.edge_gate_got[...]

    def landed(source, _):
        for copy in tile_copies(0, source):
            copy.wait_recv()
        for i in range(z.cap):
            s.got_gate_row[source * z.cap + i, 0:1, :] = s.got_gate[source, i : i + 1, :]
        return 0

    lax.fori_loop(at + 1, z.S, landed, 0)

    def gather(i, carry):
        running, gates = carry
        index = rt[ORD, i]
        joined = rt[CONT, i].astype(F32)
        running = running * joined + s.got_kv[index].astype(F32)
        gates = gates * joined + s.got_gate_row[index]
        s.sum[i] = running
        s.gate_sum[i] = gates
        return running, gates

    lax.fori_loop(0, z.n, gather, (jnp.zeros((TILE, LANES), F32), jnp.zeros((8, LANES), F32)))

    def settle(t, _):
        base = pl.multiple_of((t + 1) * TILE, TILE)
        rows = pl.ds(pl.multiple_of(t * TILE, TILE), TILE)
        for h in range(z.heads):
            cols = slice(h * LANES, (h + 1) * LANES)
            index = rt[LAST, h * z.tiles + t]
            s.dqkv[rows, z.pad + h * LANES : z.pad + (h + 1) * LANES] = (
                s.dkv[pl.ds(base, TILE), cols] + s.sum[index]
            ).astype(BF)
            s.tile_gate[t, h : h + 1, :] = s.gate_sum[index][0:1]
        return 0

    lax.fori_loop(0, z.tiles, settle, 0)
    lane = grid_of((8, LANES), 1)
    head_row = grid_of((8, LANES), 0)
    for i in range(z.tiles // 2):
        halves = []
        for t in (2 * i, 2 * i + 1):
            halves.append(pltpu.roll(s.dgate[t], TILE, 1) + s.dgate[t + 1] + s.tile_gate[t])
        joint = jnp.where(lane < TILE, halves[0], pltpu.roll(halves[1], TILE, 1))
        score = k.st[:, i * LANES : (i + 1) * LANES]
        grads = jnp.where(head_row < z.heads, joint / (1.0 + jnp.exp(score)), 0.0)
        s.ds[0:8, i * LANES : (i + 1) * LANES] = grads
        s.ds[8:16, i * LANES : (i + 1) * LANES] = jnp.zeros((8, LANES), F32)

    def in_back(i, _):
        step = (i + 1) % z.T
        rows = pl.ds(pl.multiple_of(partner(me, step) * z.block, z.block), z.block)
        s.own_part[...] = nt(s.dqkv[rows, :], used["w1"][...]) + tn(
            s.ds[:, rows].astype(BF), used["swt"][...]
        )

        @pl.when(step > 0)
        def _():
            s.part_send[1, step - 1] = s.own_part[...].astype(BF)
            part_copy(step, 1).start()

        return 0

    lax.fori_loop(0, z.T, in_back, 0)
    s.pc[0] = tn(k.n1[...], s.dqkv[:, z.pad :]).astype(BF)
    queries = tn(k.n1[...], s.dqkv[:, : z.pad])
    lane_full = grid_of((W, LANES), 1)
    s.pc[1, :, :LANES] = jnp.where(
        lane_full < TILE, queries[:, :LANES], pltpu.roll(queries[:, LANES : 2 * LANES], TILE, 1)
    ).astype(BF)
    s.pc[1, :, LANES : 2 * LANES] = queries[:, 2 * LANES :].astype(BF)
    s.stat[10:13, :] = nn(s.ds[...].astype(BF), k.n1[...])[0:3]
    source, target = grid_of((W, W), 0), grid_of((W, W), 1)
    is_value = source >= z.pad
    index = jnp.where(is_value, source - z.pad, source)
    index = index // LANES * TILE + index % TILE
    each = z.heads * TILE // z.S
    wanted = index // each * z.share + index % each + jnp.where(is_value, each, 0)
    filled = (source % LANES >= TILE) == is_value
    spread_out = jnp.where(
        (wanted == target) & filled, jnp.where(is_value, 1.0, TILE**-0.5), 0.0
    ).astype(BF)
    s.stat[13:14, :] = nn(nn(ones, s.dqkv[...]).astype(BF), spread_out)[0:1]
    grad = s.own_part[...]
    for step in range(1, z.T):
        part_copy(step, 1).wait_recv()
        grad += s.part_got[1, step - 1].astype(F32)
    y, spread = normed(r_ref[...].astype(F32))
    dr = s.dr2[...] + norm_back(grad, vec[0:1, :], y, spread)
    s.grad[own_rows, :] = dr.astype(BF)
    for step in range(1, z.T):
        rows_copy(s.grad, s.grad_ss, s.grad_rs, step).start()
    s.stat[3:4, :] = column_sum(grad * y)
    s.stat[4:5, :] = column_sum(grad)

    def stat_copy(step):
        return remote(
            s.stat.at[pl.ds(0, 8), :],
            s.stat_got.at[step - 1],
            s.stat_ss.at[step],
            s.stat_rs.at[step],
            to_tensor(step, me),
        )

    for step in range(1, z.T):
        stat_copy(step).start()
    shared = s.stat[0:8, :]
    for step in range(1, z.T):
        stat_copy(step).wait()
        shared += s.stat_got[step - 1]
    stats = jnp.concatenate([shared, s.stat[8:16, :]], axis=0).astype(BF)
    unit = (grid_of((16, LANES), 0) == grid_of((16, LANES), 1)).astype(F32).astype(BF)
    s.pc[1, :, 2 * LANES :] = tn(stats, unit).astype(BF)
    give(2).start()

    reduce(0)
    reduce(1)
    add_up(2)
    take(0)
    take(1)

    def block_of(step):
        return pl.ds(pl.multiple_of(partner(me, step) * z.block, z.block), z.block)

    for step in range(z.T):
        if step > 0:
            rows_copy(s.grad, s.grad_ss, s.grad_rs, step).wait_recv()
        if layer == 0:

            @pl.when(core == 1)
            def _(step=step):
                move(s.grad, step, block_of(step)).start()

    saver.save(s.grad, grad_out)
    reduce(2)
    take(2)
    for piece in range(3):
        give(piece).wait_send()

        @pl.when(core != layer)
        def _(piece=piece):
            hand(piece).wait_send()

        def crossed_over(i, _, piece=piece):
            cross(piece, (at + i) % z.S, at).wait_send()
            return 0

        lax.fori_loop(1, z.S, crossed_over, 0)
    for step in range(1, z.T):
        for phase in range(2):
            part_copy(step, phase).wait_send()
        rows_copy(s.ob, s.ob_ss, s.ob_rs, step).wait_send()
        rows_copy(s.grad, s.grad_ss, s.grad_rs, step).wait_send()

    def sent(d, _):
        for copy in tile_copies(d, at):
            copy.wait_send()
        return 0

    lax.fori_loop(0, at, sent, 0)

    @pl.when(at > 0)
    def _():
        for copy in edge_copies():
            copy.wait_send()

    if layer == 1:
        move(first_any, 0, everything).wait()
        keep(first_any, everything).wait()
    else:

        @pl.when(core == 0)
        def _():
            keep(s.grad, everything).start()
            move(second_any, 0, everything).wait_send()
            for step in range(z.T):
                move(s.grad, step, block_of(step)).wait_recv()

        @pl.when(core == 1)
        def _():
            move(second_any, 0, everything).wait_recv()
            for step in range(z.T):
                move(s.grad, step, block_of(step)).wait_send()

        keep(s.grad, everything).wait()
    saver.finish()


def backward(z, layer, route, c, r, first, second, own, theirs, kept):
    rows, width = z.rows, z.width
    dma = pltpu.SemaphoreType.DMA
    wide = sum(z.pieces)
    weights = [own[name] for name in WEIGHTS]
    saved = [kept[name] for name in KEPT]
    inputs = [route, c, r, first, second, *weights, *(theirs[name] for name in WEIGHTS), *saved]
    parts = [(w,) for w in z.pieces]
    return pl.pallas_call(
        functools.partial(backward_kernel, z, layer),
        out_shape=(
            jax.ShapeDtypeStruct((rows, width), BF),
            jax.ShapeDtypeStruct((2, rows, width), BF),
            jax.ShapeDtypeStruct((2, z.share, wide), F32),
        ),
        in_specs=[smem()] + [anywhere()] * (len(inputs) - 1),
        out_specs=(anywhere(), anywhere(), vmem()),
        scratch_shapes=[
            pltpu.VMEM((rows, width), BF),
            pltpu.VMEM((z.block, width), BF),
            *(pltpu.VMEM(value.shape, value.dtype) for value in weights),
            *(pltpu.VMEM(value.shape, value.dtype) for value in saved),
            pltpu.VMEM((rows, z.hidden), BF),
            pltpu.VMEM((2, z.T - 1, z.block, width), BF),
            pltpu.VMEM((2, z.T - 1, z.block, width), BF),
            pltpu.VMEM((z.block, width), F32),
            pltpu.VMEM((z.block, width), F32),
            pltpu.VMEM((rows, width), BF),
            pltpu.VMEM((rows, z.pad), BF),
            pltpu.VMEM((rows, 2 * z.pad), BF),
            pltpu.VMEM((rows + TILE, z.pad), F32),
            pltpu.VMEM((z.tiles + 1, 8, LANES), F32),
            pltpu.VMEM((z.slots, TILE, LANES), BF),
            pltpu.VMEM((z.slots, 8, LANES), F32),
            pltpu.VMEM((z.S, z.cap, TILE, LANES), BF),
            pltpu.VMEM((z.S, z.capg, LANES), F32),
            pltpu.VMEM((z.n, TILE, LANES), BF),
            pltpu.VMEM((z.S, z.capg, LANES), F32),
            pltpu.VMEM((z.n, 8, LANES), F32),
            pltpu.VMEM((TILE, z.pad), BF),
            pltpu.VMEM((TILE, z.pad), BF),
            pltpu.VMEM((8, LANES), F32),
            pltpu.VMEM((z.n + 1, TILE, LANES), F32),
            pltpu.VMEM((z.n + 1, 8, LANES), F32),
            pltpu.VMEM((z.tiles, 8, LANES), F32),
            pltpu.VMEM((16, rows), F32),
            pltpu.VMEM((24, width), F32),
            pltpu.VMEM((z.T - 1, 8, width), F32),
            pltpu.VMEM((rows, width), BF),
            *(pltpu.VMEM((2, width, w), BF) for w in z.pieces),
            *(pltpu.VMEM((width, w), BF) for w in z.pieces),
            *(pltpu.VMEM((z.S, z.padded, w), BF) for w in z.pieces),
            *(pltpu.VMEM((z.S, z.padded, w), BF) for w in z.pieces),
            *(pltpu.VMEM((z.padded, w), BF) for w in z.pieces),
            dma((z.S,)),
            dma((z.S,)),
            dma((z.S,)),
            dma((z.S,)),
            dma((2,)),
            dma((2,)),
            dma((2, z.T)),
            dma((2, z.T)),
            dma((z.T,)),
            dma((z.T,)),
            dma((z.T,)),
            dma((z.T,)),
            dma((z.T,)),
            dma((z.T,)),
            dma((3,)),
            dma((3,)),
            dma((3, z.S)),
            dma((3, z.S)),
            dma((3,)),
            dma((3,)),
            dma((z.T,)),
            dma((z.T,)),
            dma((2 + len(WEIGHTS) + len(KEPT),)),
            dma((4,)),
        ],
        compiler_params=pltpu.CompilerParams(
            collective_id=2 + layer, has_side_effects=True, vmem_limit_bytes=LIMIT
        ),
        name=f"backward{layer}",
    )(*inputs)


def swapped(value):
    return lax.ppermute(value, "section", [(0, 1), (1, 0)])


def body(
    tokens,
    cotangent,
    lengths,
    selected,
    input_weight,
    input_bias,
    score_weight,
    output_weight,
    output_bias,
    up_weight,
    up_bias,
    down_weight,
    down_bias,
    norm_gain,
    norm_bias,
):
    core = lax.axis_index("section")
    _, rows, width = tokens.shape
    heads, hidden = score_weight.shape[2], up_weight.shape[2]
    head = input_weight.shape[3] // heads
    inner = heads * head
    z = Sizes(lax.axis_size("tensor"), lax.axis_size("seq"), rows, width, heads, hidden)
    scale = head**-0.5
    grouped = (
        selected[0].reshape(2, heads, z.S, z.tiles).transpose(0, 2, 1, 3).reshape(2, z.S, z.slots)
    )
    kept_choice = lax.dynamic_index_in_dim(grouped, core, 0, keepdims=False)
    got_choice = swapped(lax.dynamic_index_in_dim(grouped, 1 - core, 0, keepdims=False))
    choice = jnp.where(
        core == 0, jnp.stack([kept_choice, got_choice]), jnp.stack([got_choice, kept_choice])
    )
    length = lax.dynamic_index_in_dim(lengths, core, 0, keepdims=False)
    ends = jnp.stack([length[0], length[0] + length[1]])
    own, routes = prepare(
        z,
        ends,
        choice,
        input_weight[0].transpose(1, 0, 2),
        input_bias[0],
        score_weight[0],
        output_weight[0],
        output_bias,
        up_bias,
        down_bias,
        norm_gain[0],
        norm_bias[0],
    )
    own |= dict(wup=up_weight[0], wdn=down_weight[0])
    first = lax.dynamic_index_in_dim(tokens, core, 0, keepdims=False)
    cotan = lax.dynamic_index_in_dim(cotangent, core, 0, keepdims=False)
    zero, theirs = forward(z, 0, routes[0], first, own, None)
    one, _ = forward(z, 1, routes[1], zero["res"], own, theirs)
    grad1, layer_out, g1 = backward(
        z, 1, routes[1], cotan, zero["res"], zero["res"], one["res"], own, theirs, one
    )
    grad0, input_grad, g0 = backward(
        z, 0, routes[0], grad1, first, grad1, grad1, own, theirs, zero
    )
    total = jnp.where(core == 0, g0, g1)
    share = z.share
    c_o, c_i = hidden, hidden + LANES
    pairs = total[0, :, c_i:].reshape(share, heads, LANES)
    input_weight_grad = jnp.stack(
        [
            scale * total[1, :, c_i : c_i + inner],
            pairs[:, :, :head].reshape(share, inner),
            pairs[:, :, head:].reshape(share, inner),
        ],
        axis=1,
    )
    out_grad = jnp.concatenate([total[0, :, c_o:c_i], total[1, :, c_o:c_i]], axis=1)[:, :inner]
    c_s = c_i + 2 * LANES
    stats = total[1, :, c_s : c_s + 16].T
    each = inner // z.S
    return (
        layer_out[None],
        input_grad[None],
        input_weight_grad[None],
        jnp.stack([stats[13, :each], stats[13, each : 2 * each]])[None],
        total[1, :, c_s + 10 : c_s + 10 + heads][None],
        out_grad.T[None],
        stats[0][None],
        total[1, :, :hidden][None],
        stats[8][None],
        total[0, :, :hidden].T[None],
        stats[9][None],
        jnp.stack([stats[3], stats[1]])[None],
        jnp.stack([stats[4], stats[2]])[None],
    )


def solution(mesh):
    return jax.shard_map(
        body,
        mesh=mesh,
        in_specs=(
            P(None, "seq", None),
            P(None, "seq", None),
            P(),
            P("section", None, "tensor", None),
            P("section", None, None, "tensor"),
            P("section", None, "tensor"),
            P("section", None, "tensor"),
            P("section", "tensor", None),
            P("section", None),
            P("section", None, "tensor"),
            P("section", "tensor"),
            P("section", "tensor", None),
            P("section", None),
            P("section", None, None),
            P("section", None, None),
        ),
        out_specs=(
            P("section", None, "seq", None),
            P("section", None, "seq", None),
            P("section", "seq", None, "tensor"),
            P("section", None, ("tensor", "seq")),
            P("section", "seq", "tensor"),
            P("section", "tensor", "seq"),
            P("section", "seq"),
            P("section", "seq", "tensor"),
            P("section", ("tensor", "seq")),
            P("section", "tensor", "seq"),
            P("section", "seq"),
            P("section", None, "seq"),
            P("section", None, "seq"),
        ),
        check_vma=False,
    )
```

time: 618 us -> 526 us (0.85)
  waiting for transfers between devices: 78.6 us -> 0.01 us
  Pallas kernels: 438 us -> 482 us
  other arithmetic: 51.7 us -> 8.11 us
  between operations: 15.6 us -> 2.08 us
    reduce_scatter x1 -> x0, waiting for transfers between devices: 67.3 us -> none  [body(): lax.psum_scatter(added(g0, g1).astype(BF), 'seq', scatter_dimension=0, ti...]
    pallas_call x5, Pallas kernels: 438 us -> 482 us  [the longest x2 280 us: backward(): pl.pallas_call(functools.partial(backward_kernel, z, layer), out_shape=(j...]
    select_n x11 -> x1, other arithmetic: 26 us -> 1.94 us  [body(): total = jnp.where(core == 0, g0, g1)]
    convert_element_type x4 -> x0, other arithmetic: 9.73 us -> none  [the longest x1 6.92 us: body(): added(g0, g1).astype(BF)]
    unnamed x43 -> x23, local copies, waits for them, and re-layouts: 10.1 us -> 13.1 us
  transfers between devices with their start and end apart: 14 -> 1, of which waited for: 3 -> 0; matrix products, arithmetic and copies ran while one was open for 9% -> 2% of each run, Pallas kernels for 2% -> 0%
where the time goes in v2:
time: 526 us; the launch traced here: 522 us
  Pallas kernels  482 us (92%)
  local copies, waits for them, and re-layouts  29.8 us (6%)
  other arithmetic  8.11 us (2%)
    pallas_call x2, Pallas kernels, backward(): pl.pallas_call(functools.partial(backward_kernel, z, layer), out_shape=(j...  280 us
    pallas_call x2, Pallas kernels, forward(): pl.pallas_call(functools.partial(forward_kernel, z, layer), out_shape=tup...  198 us
    unnamed x23, local copies, waits for them, and re-layouts  13.1 us
  transfers between devices with their start and end apart: 1, of which 0 were waited for; matrix products, arithmetic and copies ran while one was open for 2% of the time, Pallas kernels for 0%

profile of v2, /device:TPU:0, one launch (start us, length us, event | category | flops | bytes accessed | tf_op | source)
XLA Modules:
  0.0 522.2 jit_solution(4094457555572411729)
XLA Ops:
  0.6 0.0 copy-start
  0.7 0.8 reshape_squeeze.6
  1.4 0.1 reshape.47
  1.5 0.5 collective-permute-start
  2.0 0.6 fusion.5
  3.9 0.0 copy-start.6
  3.9 0.0 copy-start.5
  3.9 3.8 dynamic-slice_bitcast_fusion
  7.7 1.2 pad_add_fusion.ends_ref
  9.0 0.8 copy.56
  9.8 1.4 copy.55
  11.3 0.0 collective-permute-done
  11.3 0.6 add_select_fusion.sel_ref
  11.9 3.4 prepare.1
  15.3 85.6 %forward0.1 = (bf16[1024,768]{1,0:T(8,128)(2,1)}, bf16[1024,384]{1,0:T(8,128)(2,1)}, bf16[51,64,128]{2,1,0:T(8,128)(2,1)}, f32[8,1024]{1,0:T(8,128)}, bf16[48,64...) custom-call(s32[8,128]{1,0:T(8,128)} %get-tuple-element.55.refs_0_, ...), custom_call_target="tpu_custom_call" | custom-call | tf_op jit(solution)/shard_map/forward0/pallas_call | solution.py:656
  100.8 112.6 %forward1.1 = (bf16[1024,768]{1,0:T(8,128)(2,1)}, bf16[1024,384]{1,0:T(8,128)(2,1)}, bf16[51,64,128]{2,1,0:T(8,128)(2,1)}, f32[8,1024]{1,0:T(8,128)}, bf16[48,64...) custom-call(s32[8,128]{1,0:T(8,128)} %get-tuple-element.54.refs_0_, ...), custom_call_target="tpu_custom_call" | custom-call | tf_op jit(solution)/shard_map/forward1/pallas_call | solution.py:656
  213.4 136.3 %backward1.1 = (bf16[1024,768]{1,0:T(8,128)(2,1)}, bf16[2,1024,768]{2,1,0:T(8,128)(2,1)}, f32[2,192,1280]{2,1,0:T(8,128)}) custom-call(s32[8,128]{1,0:T(8,128)} %get-tuple-element.54.refs_0_, bf16[1024,768]{1,0:T(8,128)(2,1)} %get-tuple-element.154.refs_1_, bf16[1024,768]{1,0:T(8,128)(2,1)} %get-tuple-element.60.refs_1_.refs_2_.refs_3_, ...), custom_call_target="tpu_custom_call" | custom-call | tf_op jit(solution)/shard_map/backward1/pallas_call | solution.py:1249
  349.7 143.9 %backward0.1 = (bf16[1024,768]{1,0:T(8,128)(2,1)}, bf16[2,1024,768]{2,1,0:T(8,128)(2,1)}, f32[2,192,1280]{2,1,0:T(8,128)}) custom-call(s32[8,128]{1,0:T(8,128)} %get-tuple-element.55.refs_0_, bf16[1024,768]{1,0:T(8,128)(2,1)} %get-tuple-element.80.refs_1_.refs_3_.refs_4_, bf16[1024,768]{1,0:T(8,128)(2,1)} %get-tuple-element.153.refs_1_.refs_2_, ...), custom_call_target="tpu_custom_call" | custom-call | tf_op jit(solution)/shard_map/backward0/pallas_call | solution.py:1249
  493.7 1.9 broadcast_select_fusion
  495.6 0.1 slice.101
  495.7 0.7 fusion.1
  496.5 1.1 slice_bitcast_fusion
  497.6 0.1 fusion.4
  497.6 1.1 fusion.3
  498.7 0.1 copy.61
  498.8 0.1 copy.62
  498.9 0.7 copy.67
  499.6 0.8 copy.68
  500.4 0.1 reshape_squeeze.7
  500.5 0.3 fusion.2
  500.8 0.8 copy.57
  501.6 1.9 copy.59
  503.5 0.8 copy.58
  504.3 1.0 copy.60
  505.4 1.0 copy.65
  506.3 1.0 copy.66
  507.3 1.0 copy.64
  508.3 1.0 copy.63
  509.3 1.5 copy.71
  510.8 1.5 copy.70
  512.3 1.5 copy.69
  513.9 0.6 maximum_bitcast_fusion.3
  514.5 0.6 maximum_bitcast_fusion.2
  515.0 0.6 maximum_bitcast_fusion.1
  515.6 1.9 maximum_bitcast_fusion
  517.5 1.7 copy.76
  519.2 1.4 copy-done.3
  520.6 1.7 copy.77
  (17 shorter events, 0.1 us)
Async XLA Ops:
  0.6 1.4 copy-start
  1.5 9.7 %collective-permute-start = (s32[4,48]{1,0:T(4,128)S(1)}, s32[4,48]{1,0:T(4,128)S(1)}, u32[]{:S(2)}, u32[]{:S(2)}) collective-permute-start(s32[4,48]{1,0:T(4,128)S(1)} %get-tuple-element.150), channel_id=1, source_target_pairs={{0,16},{16,0},{1,17},{17,1},{2,18},{18,2},{3,19},{19,3},{4,20},{20... | collective-permute-start | bytes 2312 | tf_op jit(solution)/shard_map/ppermute | solution.py:1328
  3.9 5.1 copy-start.6
  3.9 5.9 %copy-start.5 = (bf16[1,768,3,192]{1,3,2,0:T(8,128)(2,1)S(1)}, bf16[1,768,3,192]{1,3,2,0:T(8,128)(2,1)}, u32[]{:S(2)}) copy-start(bf16[1,768,3,192]{1,3,2,0:T(8,128)(2,1)} %param.19) | copy-start | bytes 2654212
  349.7 144.0 %copy-start.4 = (f32[2,192,1280]{2,1,0:T(8,128)S(1)}, f32[2,192,1280]{2,1,0:T(8,128)}, u32[]{:S(2)}) copy-start(f32[2,192,1280]{2,1,0:T(8,128)} %get-tuple-element.94) | copy-start | bytes 5898244
  501.6 15.9 %copy-start.2 = (bf16[2,1024,768]{2,1,0:T(8,128)(2,1)S(1)}, bf16[2,1024,768]{2,1,0:T(8,128)(2,1)}, u32[]{:S(2)}) copy-start(bf16[2,1024,768]{2,1,0:T(8,128)(2,1)} %get-tuple-element.79) | copy-start | bytes 9437188
  517.5 3.0 copy-start.3
  520.6 1.7 copy-start.1

commit v3 on v2

--- a/solution.py
+++ b/solution.py
@@ -34,7 +34,7 @@
         self.pad = heads * LANES
         self.share = width // mesh_seq
         self.padded = -(-self.share // 16) * 16
-        self.pieces = (hidden, LANES, self.pad)
+        self.pieces = (hidden, LANES, self.pad, LANES)
 
 
 SEND, INV, ORD, CONT, ARR, POS, LAST, ENDS = range(8)
@@ -243,6 +243,85 @@
     pl.semaphore_signal(barrier, inc=1, device_id=target, device_id_type=MESH)
 
 
+class Spread:
+    def __init__(self, me, view, sends, recvs):
+        self.me, self.view, self.sends, self.recvs = me, view, sends, recvs
+
+    def copy(self, i):
+        me, x, y = self.me, partner(self.me, 1), partner(self.me, 2)
+        owner, half, step = ((me, 0, 1), (me, 1, 2), (me, 1, 1), (me, 0, 2), (x, 0, 2), (y, 1, 1))[i]
+        ref = self.view(owner, half)
+        return remote(ref, ref, self.sends(i), self.recvs(i), to_tensor(step, me))
+
+    def start(self):
+        for i in range(4):
+            self.copy(i).start()
+
+    def forward(self):
+        for i in range(2):
+            self.copy(i).wait_recv()
+            self.copy(4 + i).start()
+
+    def wait(self, step):
+        for i in ((), (2,), (3,), (4, 5))[step]:
+            self.copy(i).wait_recv()
+
+    def finish(self):
+        for i in range(6):
+            self.copy(i).wait_send()
+
+
+class Collect:
+    def __init__(self, z, me, send, got, via, sends, recvs):
+        self.me, self.send, self.got, self.via, self.sends, self.recvs = me, send, got, via, sends, recvs
+        half = z.block // 2
+        self.halves = (pl.ds(0, half), pl.ds(half, half))
+
+    def copy(self, i):
+        top, bottom = self.halves
+        block, rows, target, step = (
+            (2, top, self.via.at[0], 1),
+            (2, bottom, self.via.at[1], 2),
+            (0, top, self.got.at[0, top, :], 1),
+            (1, bottom, self.got.at[1, bottom, :], 2),
+            (0, bottom, self.got.at[0, bottom, :], 1),
+            (1, top, self.got.at[1, top, :], 2),
+        )[i]
+        return remote(
+            self.send.at[block, rows, :], target, self.sends(i), self.recvs(i), to_tensor(step, self.me)
+        )
+
+    def put(self, step, value):
+        for wanted, copies in ((3, (0, 1)), (1, (2,)), (2, (3,))):
+
+            @pl.when(step == wanted)
+            def _(wanted=wanted, copies=copies):
+                self.send[wanted - 1] = value().astype(BF)
+                for i in copies:
+                    self.copy(i).start()
+
+    def join(self):
+        top, bottom = self.halves
+        for i, block, rows in ((1, 0, bottom), (0, 1, top)):
+            self.copy(i).wait_recv()
+            joined = self.send[block, rows, :].astype(F32) + self.via[i].astype(F32)
+            self.send[block, rows, :] = joined.astype(BF)
+            self.copy(5 - i).start()
+
+    def total(self, own):
+        for i in range(2, 6):
+            self.copy(i).wait_recv()
+        return own + self.got[0].astype(F32) + self.got[1].astype(F32)
+
+    def finish(self):
+        for i in range(6):
+            self.copy(i).wait_send()
+
+
+def visiting(k):
+    return jnp.where(k == 0, 3, jnp.where(k == 3, 0, k))
+
+
 class Saver:
     def __init__(self, sems):
         self.sems, self.copies = sems, []
@@ -259,8 +338,8 @@
 
 FORWARD_OUTS = KEPT + ("res",)
 FORWARD_SCRATCH = (
-    "gt", "gate", "edge", "edge_gate", "send_kv", "send_gate", "got_gate", "far_gate", "wo_all", "o_all",
-    "part_send", "part_got", "own_part", "kv_ss", "kv_rs", "gate_ss", "gate_rs", "edge_ss", "edge_rs",
+    "gt", "gate", "edge", "edge_gate", "send_kv", "send_gate", "got_gate", "far_gate", "wo_all", "wo_high",
+    "pair_all", "single_all", "part_send", "part_got", "part_via", "own_part", "kv_ss", "kv_rs", "gate_ss", "gate_rs", "edge_ss", "edge_rs",
     "wo_ss", "wo_rs", "o_ss", "o_rs", "part_ss", "part_rs", "res_ss", "res_rs", "swap_ss", "swap_rs", "load", "saved",
 )
 
@@ -488,76 +567,104 @@
             cols = slice(h * LANES, (h + 1) * LANES)
             u = h * z.tiles + t
             arrived = rt[ARR, u]
-            query_tile = held.q[pl.ds(base, TILE), cols]
+            far = held.ckv[arrived]
             near = held.kvt[pl.ds(h * (z.tiles + 1) + t, 2)].reshape(2 * TILE, LANES)
-            far = held.ckv[arrived]
-            near_score = nt(query_tile, near) + s.gate[h * (z.tiles + 1) + t, 0:1, :]
-            far_score = nt(query_tile, jnp.concatenate([far, far], axis=0)) + s.far_gate[arrived][0:1]
+            keys = jnp.concatenate([near, far, far], axis=0)
+            gates = jnp.concatenate(
+                [s.gate[h * (z.tiles + 1) + t, 0:1, :], s.far_gate[arrived][0:1]], axis=1
+            )
             far_ok = (rt[POS, u] + lane >= begin) & (lane < TILE)
-            near_score = jnp.where(near_ok, near_score, MASKED)
-            far_score = jnp.where(far_ok, far_score, MASKED)
-            top = jnp.max(jnp.maximum(near_score, far_score), axis=-1, keepdims=True)
-            near_exp = jnp.exp(near_score - top)
-            far_exp = jnp.exp(far_score - top)
-            scale = 1.0 / jnp.sum(near_exp + far_exp, axis=-1, keepdims=True)
-            near_p = (near_exp * scale).astype(BF)
-            far_p = (far_exp * scale).astype(BF)
-            held.p[t * z.heads + h, :, 0:LANES] = near_p
-            held.p[t * z.heads + h, :, LANES:] = far_p
-            mixed.append(nn(near_p, near) + nn(far_p[:, :TILE], far))
+            score = jnp.where(
+                jnp.concatenate([near_ok, far_ok], axis=1),
+                nt(held.q[pl.ds(base, TILE), cols], keys) + gates,
+                MASKED,
+            )
+            raised = jnp.exp(score - jnp.max(score, axis=-1, keepdims=True))
+            p = (raised * (1.0 / jnp.sum(raised, axis=-1, keepdims=True))).astype(BF)
+            held.p[t * z.heads + h] = p
+            mixed.append(nn(p, keys))
         pair = jnp.where(lane < TILE, pltpu.roll(mixed[0], TILE, 1), mixed[1]).astype(BF)
-        single = pltpu.roll(mixed[2], TILE, 1).astype(BF)
+        single = pltpu.roll(mixed[2], TILE, 1)
         held.o[pl.ds(base, TILE), 0:LANES] = pair
-        held.o[pl.ds(base, TILE), LANES:] = single
-
-    def o_copy(step, b):
-        rows = pl.ds(b * z.block, z.block)
-        return remote(
-            held.o.at[rows, :],
-            s.o_all.at[me, rows, :],
-            s.o_ss.at[step * z.T + b],
-            s.o_rs.at[step * z.T + b],
-            to_tensor(step, me),
+        held.o[pl.ds(base, TILE), LANES:] = single.astype(BF)
+        s.pair_all[me, pl.ds(base, TILE), :] = pair
+        return single, mixed[2]
+
+    half_rows = z.block // 2
+
+    def pair_spread(b):
+        return Spread(
+            me,
+            lambda owner, half: s.pair_all.at[owner, pl.ds(b * z.block + half * half_rows, half_rows), :],
+            lambda i: s.o_ss.at[b * 12 + i],
+            lambda i: s.o_rs.at[b * 12 + i],
+        )
+
+    def single_spread(b):
+        return Spread(
+            me,
+            lambda owner, half: s.single_all.at[
+                owner, pl.ds(b * half_rows + half * (half_rows // 2), half_rows // 2), :
+            ],
+            lambda i: s.o_ss.at[b * 12 + 6 + i],
+            lambda i: s.o_rs.at[b * 12 + 6 + i],
         )
 
     def attend_block(b, _):
-        def pair(i, _):
-            attend(b * per_block + 2 * i)
-            attend(b * per_block + 2 * i + 1)
+        def two(i, _):
+            t = b * per_block + 2 * i
+            even, _ = attend(t)
+            _, odd = attend(t + 1)
+            s.single_all[me, pl.ds(pl.multiple_of(b * half_rows + i * TILE, TILE), TILE), :] = jnp.where(
+                lane < TILE, even, odd
+            ).astype(BF)
             return 0
 
-        lax.fori_loop(0, per_block // 2, pair, 0)
-        for step in range(1, z.T):
-            o_copy(step, b).start()
-        rows = pl.ds(b * z.block, z.block)
-        s.o_all[me, rows, :] = held.o[rows, :]
+        lax.fori_loop(0, per_block // 2, two, 0)
+        pair_spread(b).start()
+        single_spread(b).start()
+
+        @pl.when(b > 0)
+        def _():
+            pair_spread(b - 1).forward()
+            single_spread(b - 1).forward()
+
         return 0
 
     lax.fori_loop(0, z.T, attend_block, 0)
+    pair_spread(z.T - 1).forward()
+    single_spread(z.T - 1).forward()
     saver.save(held.p, outs["p"])
     saver.save(held.o, outs["o"])
     ready(4, 5)
     for step in range(1, z.T):
         wo_copy(step).wait()
-
-    def part_copy(step):
-        return remote(
-            s.part_send.at[step - 1],
-            s.part_got.at[step - 1],
-            s.part_ss.at[step - 1],
-            s.part_rs.at[step - 1],
-            to_tensor(step, me),
-        )
+    for t in range(z.T):
+        s.wo_high[t, 0:TILE, :] = jnp.zeros((TILE, z.width), BF)
+        s.wo_high[t, TILE:, :] = s.wo_all[t, LANES : LANES + TILE, :]
+    collect = Collect(
+        z, me, s.part_send, s.part_got, s.part_via, lambda i: s.part_ss.at[i], lambda i: s.part_rs.at[i]
+    )
 
     def feed(k, _):
-        step = (k + 1) % z.T
+        step = visiting(k)
         block = partner(me, step)
         rows = pl.ds(pl.multiple_of(block * z.block, z.block), z.block)
+        few = pl.ds(pl.multiple_of(block * half_rows, half_rows), half_rows)
         for other in range(1, z.T):
-            o_copy(other, block).wait_recv()
-        mixed = nn(s.o_all[0, rows, :], s.wo_all[0])
+            pair_spread(block).wait(other)
+            single_spread(block).wait(other)
+        mixed = nn(s.pair_all[0, rows, :], s.wo_all[0, 0:LANES, :])
+        even = nn(s.single_all[0, few, :], s.wo_all[0, LANES:, :])
+        odd = nn(s.single_all[0, few, :], s.wo_high[0])
         for other in range(1, z.T):
-            mixed += nn(s.o_all[other, rows, :], s.wo_all[other])
+            mixed += nn(s.pair_all[other, rows, :], s.wo_all[other, 0:LANES, :])
+            even += nn(s.single_all[other, few, :], s.wo_all[other, LANES:, :])
+            odd += nn(s.single_all[other, few, :], s.wo_high[other])
+        turns = []
+        for i in range(per_block // 2):
+            turns += [even[i * TILE : (i + 1) * TILE], odd[i * TILE : (i + 1) * TILE]]
+        mixed += jnp.concatenate(turns, axis=0)
         middle = r_ref[rows, :].astype(F32) + mixed + vec[3:4, :]
         held.mid[...] = middle
         y, _ = normed(middle)
@@ -569,38 +676,33 @@
         held.act[rows, :] = act
         s.own_part[...] = nn(act, used["wdn"][...])
 
-        @pl.when(step > 0)
-        def _():
-            s.part_send[step - 1] = s.own_part[...].astype(BF)
-            part_copy(step).start()
-
+        collect.put(step, lambda: s.own_part[...])
         return 0
 
     lax.fori_loop(0, z.T, feed, 0)
+    collect.join()
     for name in ("mid", "n2", "u", "act"):
         saver.save(getattr(held, name), outs[name])
-    total = held.mid[...] + s.own_part[...] + vec[7:8, :]
-    for step in range(1, z.T):
-        part_copy(step).wait_recv()
-        total += s.part_got[step - 1].astype(F32)
+    total = collect.total(held.mid[...] + s.own_part[...] + vec[7:8, :])
     own_rows = pl.ds(pl.multiple_of(me * z.block, z.block), z.block)
     held.res[own_rows, :] = total.astype(BF)
-
-    def res_copy(step):
-        return remote(
-            held.res.at[own_rows, :],
-            held.res.at[own_rows, :],
-            s.res_ss.at[step],
-            s.res_rs.at[step],
-            to_tensor(step, me),
-        )
-
-    for step in range(1, z.T):
-        res_copy(step).start()
-    for step in range(1, z.T):
-        part_copy(step).wait_send()
-        for b in range(z.T):
-            o_copy(step, b).wait_send()
+    spread = Spread(
+        me,
+        lambda owner, half: held.res.at[
+            pl.ds(pl.multiple_of(owner * z.block + half * half_rows, half_rows), half_rows), :
+        ],
+        lambda i: s.res_ss.at[i],
+        lambda i: s.res_rs.at[i],
+    )
+    spread.start()
+    collect.finish()
+
+    def finish_block(b, _):
+        pair_spread(b).finish()
+        single_spread(b).finish()
+        return 0
+
+    lax.fori_loop(0, z.T, finish_block, 0)
 
     def sent(d, _):
         for copy in tile_copies(d, at):
@@ -623,8 +725,10 @@
 
         for i in range(count):
             swap(i).wait_send()
+    spread.forward()
     for step in range(1, z.T):
-        res_copy(step).wait()
+        spread.wait(step)
+    spread.finish()
     saver.save(held.res, outs["res"])
     saver.finish()
 
@@ -670,9 +774,12 @@
             pltpu.VMEM((z.S, z.capg, LANES), F32),
             pltpu.VMEM((z.n, 8, LANES), F32),
             pltpu.VMEM((z.T, 2 * LANES, width), BF),
-            pltpu.VMEM((z.T, rows, 2 * LANES), BF),
+            pltpu.VMEM((z.T, LANES, width), BF),
+            pltpu.VMEM((z.T, rows, LANES), BF),
+            pltpu.VMEM((z.T, rows // 2, LANES), BF),
             pltpu.VMEM((z.T - 1, z.block, width), BF),
-            pltpu.VMEM((z.T - 1, z.block, width), BF),
+            pltpu.VMEM((2, z.block, width), BF),
+            pltpu.VMEM((2, z.block // 2, width), BF),
             pltpu.VMEM((z.block, width), F32),
             dma((z.S,)),
             dma((z.S,)),
@@ -682,12 +789,12 @@
             dma((heads + 1,)),
             dma((z.T,)),
             dma((z.T,)),
-            dma((z.T * z.T,)),
-            dma((z.T * z.T,)),
-            dma((z.T,)),
-            dma((z.T,)),
-            dma((z.T,)),
-            dma((z.T,)),
+            dma((z.T * 12,)),
+            dma((z.T * 12,)),
+            dma((6,)),
+            dma((6,)),
+            dma((6,)),
+            dma((6,)),
             dma((len(WEIGHTS),)),
             dma((len(WEIGHTS),)),
             dma((len(WEIGHTS),)),
@@ -703,10 +810,10 @@
 
 
 BACKWARD_SCRATCH = (
-    "du", "part_send", "part_got", "own_part", "dr2", "ob", "dout", "dqkv", "dkv", "dgate", "far", "far_gate",
+    "du", "part_send", "part_got", "part_via", "own_part", "dr2", "ob", "dout", "dqkv", "dkv", "dgate", "far", "far_gate",
     "send_kv", "send_gate", "got_kv", "got_gate", "got_gate_row", "edge_send", "edge_got", "edge_gate_got", "sum",
-    "gate_sum", "tile_gate", "ds", "stat", "stat_got", "grad",
-    "pa", "pb", "pc", "xa", "xb", "xc", "sa", "sb", "sc", "ta", "tb", "tc", "ha", "hb", "hc",
+    "gate_sum", "tile_gate", "ds", "stat", "stat_got", "grad", "bounce",
+    "pa", "pb", "pc", "pd", "xa", "xb", "xc", "xd", "sa", "sb", "sc", "sd", "ta", "tb", "tc", "td", "ha", "hb", "hc",
     "kv_ss", "kv_rs", "gate_ss", "gate_rs", "edge_ss", "edge_rs", "part_ss", "part_rs", "ob_ss", "ob_rs",
     "grad_ss", "grad_rs", "stat_ss", "stat_rs", "give_ss", "give_rs", "cross_ss", "cross_rs", "hand_ss", "hand_rs",
     "move_ss", "move_rs", "load", "saved",
@@ -780,42 +887,68 @@
     def keep(src, part):
         return pltpu.make_async_copy(src.at[part], both_out.at[core].at[part], s.saved.at[3])
 
+    def fetch(src, i):
+        return pltpu.make_async_copy(src, s.bounce.at[i], s.saved.at[1 + i])
+
     everything = pl.ds(0, z.rows)
+    stay, leave = s.bounce.at[0], s.bounce.at[1]
 
     @pl.when(core == 0)
     def _():
-        move(second_any, 0, everything).start()
-
-    if layer == 1:
-
-        @pl.when(core == 0)
-        def _():
-            keep(first_any, everything).start()
-
-        @pl.when(core == 1)
-        def _():
-            move(first_any, 0, everything).start()
-            keep(second_any, everything).start()
-
-    else:
-
-        @pl.when(core == 1)
-        def _():
-            keep(second_any, everything).start()
-
-    def part_copy(step, phase):
-        return remote(
-            s.part_send.at[phase, step - 1],
-            s.part_got.at[phase, step - 1],
-            s.part_ss.at[phase, step],
-            s.part_rs.at[phase, step],
-            to_tensor(step, me),
+        fetch(second_any, 1).start()
+        if layer == 1:
+            fetch(first_any, 0).start()
+
+    @pl.when(core == 1)
+    def _():
+        fetch(second_any, 0).start()
+        if layer == 1:
+            fetch(first_any, 1).start()
+
+    def forward_rows():
+        def leaving():
+            fetch(second_any, 1).wait()
+            move(leave, 0, everything).start()
+
+        def staying():
+            fetch(second_any, 0).wait()
+            keep(stay, everything).start()
+
+        if layer == 1:
+            leaving()
+            staying()
+        else:
+            pl.when(core == 0)(leaving)
+            pl.when(core == 1)(staying)
+
+    collects = [
+        Collect(
+            z,
+            me,
+            s.part_send.at[phase],
+            s.part_got.at[phase],
+            s.part_via.at[phase],
+            lambda i, phase=phase: s.part_ss.at[phase, i],
+            lambda i, phase=phase: s.part_rs.at[phase, i],
+        )
+        for phase in range(2)
+    ]
+    half_rows = z.block // 2
+
+    def rows_spread(ref, sends, recvs):
+        return Spread(
+            me,
+            lambda owner, half: ref.at[
+                pl.ds(pl.multiple_of(owner * z.block + half * half_rows, half_rows), half_rows), :
+            ],
+            lambda i: sends.at[i],
+            lambda i: recvs.at[i],
         )
 
     ready("c", "wdn", "u", "wup")
 
     def ff_back(i, _):
-        step = (i + 1) % z.T
+        step = visiting(i)
         rows = pl.ds(pl.multiple_of(partner(me, step) * z.block, z.block), z.block)
         u = k.u[rows, :].astype(F32)
         squared = u * u
@@ -827,22 +960,19 @@
         s.du[rows, :] = du
         s.own_part[...] = nt(du, used["wup"][...])
 
-        @pl.when(step > 0)
-        def _():
-            s.part_send[0, step - 1] = s.own_part[...].astype(BF)
-            part_copy(step, 0).start()
-
+        collects[0].put(step, lambda: s.own_part[...])
         return 0
 
     lax.fori_loop(0, z.T, ff_back, 0)
+    collects[0].join()
     ones = jnp.ones((16, z.rows), BF)
     s.stat[...] = jnp.zeros((24, W), F32)
 
-    mine = {0: s.pa, 1: s.pb, 2: s.pc}
-    theirs_part = {0: s.xa, 1: s.xb, 2: s.xc}
-    summed = {0: s.sa, 1: s.sb, 2: s.sc}
-    crossed = {0: s.ta, 1: s.tb, 2: s.tc}
-    handed = {0: s.ha, 1: s.hb, 2: s.hc}
+    mine = (s.pa, s.pb, s.pc, s.pd)
+    theirs_part = (s.xa, s.xb, s.xc, s.xd)
+    summed = (s.sa, s.sb, s.sc, s.sd)
+    crossed = (s.ta, s.tb, s.tc, s.td)
+    handed = (s.ha, s.hb, s.hc)
 
     def give(piece):
         return remote(
@@ -888,7 +1018,7 @@
 
         lax.fori_loop(0, W // span, chunk, 0)
 
-    offsets = (0, z.pieces[0], z.pieces[0] + z.pieces[1])
+    offsets = [sum(z.pieces[:piece]) for piece in range(len(z.pieces))]
 
     def reduce(piece):
         def wait(i, _):
@@ -907,8 +1037,9 @@
 
         @pl.when(core != layer)
         def _():
-            summed[piece][at] = total.astype(BF)
-            hand(piece).start()
+            if piece < len(handed):
+                summed[piece][at] = total.astype(BF)
+                hand(piece).start()
 
     def take(piece):
         cols = slice(offsets[piece], offsets[piece] + z.pieces[piece])
@@ -918,6 +1049,7 @@
             hand(piece).wait_recv()
             g_out[1 - core, :, cols] = handed[piece][...].astype(F32)[: z.share]
 
+    forward_rows()
     ready("act", "n2")
     s.pa[0] = tn(c_ref[...], k.act[...]).astype(BF)
     s.pa[1] = tn(k.n2[...], s.du[...]).astype(BF)
@@ -925,33 +1057,28 @@
     s.stat[8:9, :] = nn(ones, s.du[...])[0:1]
     s.stat[9:10, :] = nn(ones, c_ref[...])[0:1]
     ready("vec", "mid", "wo")
-    grad = s.own_part[...]
-    for step in range(1, z.T):
-        part_copy(step, 0).wait_recv()
-        grad += s.part_got[0, step - 1].astype(F32)
+    grad = collects[0].total(s.own_part[...])
     y, spread = normed(k.mid[...])
     dr2 = c_ref[own_rows, :].astype(F32) + norm_back(grad, vec[4:5, :], y, spread)
     s.dr2[...] = dr2
     s.ob[own_rows, :] = dr2.astype(BF)
 
-    def rows_copy(ref, sends, recvs, step):
-        return remote(
-            ref.at[own_rows, :], ref.at[own_rows, :], sends.at[step], recvs.at[step], to_tensor(step, me)
-        )
-
-    for step in range(1, z.T):
-        rows_copy(s.ob, s.ob_ss, s.ob_rs, step).start()
+    ob_spread = rows_spread(s.ob, s.ob_ss, s.ob_rs)
+    ob_spread.start()
     s.stat[0:1, :] = column_sum(dr2)
     s.stat[1:2, :] = column_sum(grad * y)
     s.stat[2:3, :] = column_sum(grad)
     s.dkv[...] = jnp.zeros((z.rows + TILE, z.pad), F32)
+    ob_spread.forward()
     add_up(0)
     lane_wide = grid_of((z.block, LANES), 1)
 
     def out_back(step, _):
-        @pl.when(step > 0)
-        def _():
-            rows_copy(s.ob, s.ob_ss, s.ob_rs, step).wait_recv()
+        for wanted in range(1, z.T):
+
+            @pl.when(step == wanted)
+            def _(wanted=wanted):
+                ob_spread.wait(wanted)
 
         rows = pl.ds(pl.multiple_of(partner(me, step) * z.block, z.block), z.block)
         dout = nt(s.ob[rows, :], used["wo"][...])
@@ -971,22 +1098,20 @@
             arrived = rt[ARR, u]
             near = k.kvt[pl.ds(h * (z.tiles + 1) + t, 2)].reshape(2 * TILE, LANES)
             far = k.ckv[arrived]
+            keys = jnp.concatenate([near, far, far], axis=0)
             query = k.q[pl.ds(base, TILE), cols]
             dout = s.dout[pl.ds(base, TILE), cols]
-            near_p = k.p[t * z.heads + h, :, 0:LANES]
-            far_p = k.p[t * z.heads + h, :, LANES : LANES + TILE]
-            near_pf, far_pf = near_p.astype(F32), far_p.astype(F32)
-            near_dp, far_dp = nt(dout, near), nt(dout, far)
-            total = jnp.sum(near_pf * near_dp, axis=-1, keepdims=True) + jnp.sum(
-                far_pf * far_dp, axis=-1, keepdims=True
-            )
-            near_dz = (near_pf * (near_dp - total)).astype(BF)
-            far_dz = (far_pf * (far_dp - total)).astype(BF)
-            s.dqkv[pl.ds(base, TILE), cols] = (nn(near_dz, near) + nn(far_dz, far)).astype(BF)
-            s.dkv[pl.ds(base, 2 * TILE), cols] += tn(near_dz, query) + tn(near_p, dout)
-            s.far[u] = (tn(far_dz, query) + tn(far_p, dout)).astype(BF)
-            s.dgate[t, h : h + 1, :] = column_sum(near_dz.astype(F32))
-            s.far_gate[u, 0:1, 0:TILE] = column_sum(far_dz.astype(F32))
+            p = k.p[t * z.heads + h]
+            weight = p.astype(F32)
+            dp = nt(dout, keys)
+            dz = (weight * (dp - jnp.sum(weight * dp, axis=-1, keepdims=True))).astype(BF)
+            s.dqkv[pl.ds(base, TILE), cols] = nn(dz, keys).astype(BF)
+            dkeys = tn(jnp.concatenate([dz, p], axis=0), jnp.concatenate([query, dout], axis=0))
+            s.dkv[pl.ds(base, 2 * TILE), cols] += dkeys[: 2 * TILE]
+            s.far[u] = dkeys[2 * TILE : 3 * TILE].astype(BF)
+            gates = column_sum(dz.astype(F32))
+            s.dgate[t, h : h + 1, :] = gates[:, :LANES]
+            s.far_gate[u, 0:1, :] = gates[:, LANES:]
 
     def attend_back_pair(i, _):
         attend_back(2 * i)
@@ -1100,20 +1225,17 @@
         s.ds[8:16, i * LANES : (i + 1) * LANES] = jnp.zeros((8, LANES), F32)
 
     def in_back(i, _):
-        step = (i + 1) % z.T
+        step = visiting(i)
         rows = pl.ds(pl.multiple_of(partner(me, step) * z.block, z.block), z.block)
         s.own_part[...] = nt(s.dqkv[rows, :], used["w1"][...]) + tn(
             s.ds[:, rows].astype(BF), used["swt"][...]
         )
 
-        @pl.when(step > 0)
-        def _():
-            s.part_send[1, step - 1] = s.own_part[...].astype(BF)
-            part_copy(step, 1).start()
-
+        collects[1].put(step, lambda: s.own_part[...])
         return 0
 
     lax.fori_loop(0, z.T, in_back, 0)
+    collects[1].join()
     s.pc[0] = tn(k.n1[...], s.dqkv[:, z.pad :]).astype(BF)
     queries = tn(k.n1[...], s.dqkv[:, : z.pad])
     lane_full = grid_of((W, LANES), 1)
@@ -1121,6 +1243,8 @@
         lane_full < TILE, queries[:, :LANES], pltpu.roll(queries[:, LANES : 2 * LANES], TILE, 1)
     ).astype(BF)
     s.pc[1, :, LANES : 2 * LANES] = queries[:, 2 * LANES :].astype(BF)
+    s.pc[1, :, 2 * LANES :] = jnp.zeros((W, z.pad - 2 * LANES), BF)
+    give(2).start()
     s.stat[10:13, :] = nn(s.ds[...].astype(BF), k.n1[...])[0:3]
     source, target = grid_of((W, W), 0), grid_of((W, W), 1)
     is_value = source >= z.pad
@@ -1133,15 +1257,12 @@
         (wanted == target) & filled, jnp.where(is_value, 1.0, TILE**-0.5), 0.0
     ).astype(BF)
     s.stat[13:14, :] = nn(nn(ones, s.dqkv[...]).astype(BF), spread_out)[0:1]
-    grad = s.own_part[...]
-    for step in range(1, z.T):
-        part_copy(step, 1).wait_recv()
-        grad += s.part_got[1, step - 1].astype(F32)
+    grad = collects[1].total(s.own_part[...])
     y, spread = normed(r_ref[...].astype(F32))
     dr = s.dr2[...] + norm_back(grad, vec[0:1, :], y, spread)
     s.grad[own_rows, :] = dr.astype(BF)
-    for step in range(1, z.T):
-        rows_copy(s.grad, s.grad_ss, s.grad_rs, step).start()
+    grad_spread = rows_spread(s.grad, s.grad_ss, s.grad_rs)
+    grad_spread.start()
     s.stat[3:4, :] = column_sum(grad * y)
     s.stat[4:5, :] = column_sum(grad)
 
@@ -1162,12 +1283,22 @@
         shared += s.stat_got[step - 1]
     stats = jnp.concatenate([shared, s.stat[8:16, :]], axis=0).astype(BF)
     unit = (grid_of((16, LANES), 0) == grid_of((16, LANES), 1)).astype(F32).astype(BF)
-    s.pc[1, :, 2 * LANES :] = tn(stats, unit).astype(BF)
-    give(2).start()
+    s.pd[core] = tn(stats, unit).astype(BF)
+    s.pd[1 - core] = s.pd[core]
+
+    @pl.when(core != layer)
+    def _():
+        give(3).start()
+
+    grad_spread.forward()
+    add_up(2)
+
+    @pl.when(core == layer)
+    def _():
+        add_up(3)
 
     reduce(0)
     reduce(1)
-    add_up(2)
     take(0)
     take(1)
 
@@ -1175,8 +1306,7 @@
         return pl.ds(pl.multiple_of(partner(me, step) * z.block, z.block), z.block)
 
     for step in range(z.T):
-        if step > 0:
-            rows_copy(s.grad, s.grad_ss, s.grad_rs, step).wait_recv()
+        grad_spread.wait(step)
         if layer == 0:
 
             @pl.when(core == 1)
@@ -1186,6 +1316,23 @@
     saver.save(s.grad, grad_out)
     reduce(2)
     take(2)
+
+    @pl.when(core == layer)
+    def _():
+        reduce(3)
+
+    def last_sent(i, _):
+        cross(3, (at + i) % z.S, at).wait_send()
+        return 0
+
+    @pl.when(core == layer)
+    def _():
+        lax.fori_loop(1, z.S, last_sent, 0)
+
+    @pl.when(core != layer)
+    def _():
+        give(3).wait_send()
+
     for piece in range(3):
         give(piece).wait_send()
 
@@ -1198,11 +1345,10 @@
             return 0
 
         lax.fori_loop(1, z.S, crossed_over, 0)
-    for step in range(1, z.T):
-        for phase in range(2):
-            part_copy(step, phase).wait_send()
-        rows_copy(s.ob, s.ob_ss, s.ob_rs, step).wait_send()
-        rows_copy(s.grad, s.grad_ss, s.grad_rs, step).wait_send()
+    for collect in collects:
+        collect.finish()
+    ob_spread.finish()
+    grad_spread.finish()
 
     def sent(d, _):
         for copy in tile_copies(d, at):
@@ -1217,20 +1363,20 @@
             copy.wait_send()
 
     if layer == 1:
-        move(first_any, 0, everything).wait()
-        keep(first_any, everything).wait()
+        move(leave, 0, everything).wait()
+        keep(stay, everything).wait()
     else:
 
         @pl.when(core == 0)
         def _():
             keep(s.grad, everything).start()
-            move(second_any, 0, everything).wait_send()
+            move(leave, 0, everything).wait_send()
             for step in range(z.T):
                 move(s.grad, step, block_of(step)).wait_recv()
 
         @pl.when(core == 1)
         def _():
-            move(second_any, 0, everything).wait_recv()
+            move(leave, 0, everything).wait_recv()
             for step in range(z.T):
                 move(s.grad, step, block_of(step)).wait_send()
 
@@ -1262,7 +1408,8 @@
             *(pltpu.VMEM(value.shape, value.dtype) for value in saved),
             pltpu.VMEM((rows, z.hidden), BF),
             pltpu.VMEM((2, z.T - 1, z.block, width), BF),
-            pltpu.VMEM((2, z.T - 1, z.block, width), BF),
+            pltpu.VMEM((2, 2, z.block, width), BF),
+            pltpu.VMEM((2, 2, z.block // 2, width), BF),
             pltpu.VMEM((z.block, width), F32),
             pltpu.VMEM((z.block, width), F32),
             pltpu.VMEM((rows, width), BF),
@@ -1287,29 +1434,30 @@
             pltpu.VMEM((24, width), F32),
             pltpu.VMEM((z.T - 1, 8, width), F32),
             pltpu.VMEM((rows, width), BF),
+            pltpu.VMEM((2, rows, width), BF),
             *(pltpu.VMEM((2, width, w), BF) for w in z.pieces),
             *(pltpu.VMEM((width, w), BF) for w in z.pieces),
             *(pltpu.VMEM((z.S, z.padded, w), BF) for w in z.pieces),
             *(pltpu.VMEM((z.S, z.padded, w), BF) for w in z.pieces),
-            *(pltpu.VMEM((z.padded, w), BF) for w in z.pieces),
+            *(pltpu.VMEM((z.padded, w), BF) for w in z.pieces[:3]),
             dma((z.S,)),
             dma((z.S,)),
             dma((z.S,)),
             dma((z.S,)),
             dma((2,)),
             dma((2,)),
-            dma((2, z.T)),
-            dma((2, z.T)),
+            dma((2, 6)),
+            dma((2, 6)),
+            dma((6,)),
+            dma((6,)),
+            dma((6,)),
+            dma((6,)),
             dma((z.T,)),
             dma((z.T,)),
-            dma((z.T,)),
-            dma((z.T,)),
-            dma((z.T,)),
-            dma((z.T,)),
-            dma((3,)),
-            dma((3,)),
-            dma((3, z.S)),
-            dma((3, z.S)),
+            dma((4,)),
+            dma((4,)),
+            dma((4, z.S)),
+            dma((4, z.S)),
             dma((3,)),
             dma((3,)),
             dma((z.T,)),
@@ -1390,7 +1538,7 @@
     total = jnp.where(core == 0, g0, g1)
     share = z.share
     c_o, c_i = hidden, hidden + LANES
-    pairs = total[0, :, c_i:].reshape(share, heads, LANES)
+    pairs = total[0, :, c_i : c_i + z.pad].reshape(share, heads, LANES)
     input_weight_grad = jnp.stack(
         [
             scale * total[1, :, c_i : c_i + inner],
@@ -1400,15 +1548,16 @@
         axis=1,
     )
     out_grad = jnp.concatenate([total[0, :, c_o:c_i], total[1, :, c_o:c_i]], axis=1)[:, :inner]
-    c_s = c_i + 2 * LANES
-    stats = total[1, :, c_s : c_s + 16].T
+    c_s = c_i + z.pad
+    kept_stats = jnp.where(core == 0, g0[0, :, c_s : c_s + 16], g1[1, :, c_s : c_s + 16])
+    stats = kept_stats.T
     each = inner // z.S
     return (
         layer_out[None],
         input_grad[None],
         input_weight_grad[None],
         jnp.stack([stats[13, :each], stats[13, each : 2 * each]])[None],
-        total[1, :, c_s + 10 : c_s + 10 + heads][None],
+        kept_stats[:, 10 : 10 + heads][None],
         out_grad.T[None],
         stats[0][None],
         total[1, :, :hidden][None],

time: 526 us -> 458 us (0.87)
  Pallas kernels: 482 us -> 415 us
    pallas_call x2, Pallas kernels: 280 us -> 243 us  [backward(): pl.pallas_call(functools.partial(backward_kernel, z, layer), out_shape=(j...]
    pallas_call x2, Pallas kernels: 198 us -> 169 us  [forward(): pl.pallas_call(functools.partial(forward_kernel, z, layer), out_shape=tup...]
where the time goes in v3:
time: 458 us; the launch traced here: 456 us
  Pallas kernels  415 us (91%)
  local copies, waits for them, and re-layouts  29.8 us (7%)
  other arithmetic  8.9 us (2%)
    pallas_call x2, Pallas kernels, backward(): pl.pallas_call(functools.partial(backward_kernel, z, layer), out_shape=(j...  243 us
    pallas_call x2, Pallas kernels, forward(): pl.pallas_call(functools.partial(forward_kernel, z, layer), out_shape=tup...  169 us
    unnamed x23, local copies, waits for them, and re-layouts  13.1 us
  transfers between devices with their start and end apart: 1, of which 0 were waited for; matrix products, arithmetic and copies ran while one was open for 2% of the time, Pallas kernels for 0%

profile of v3, /device:TPU:0, one launch (start us, length us, event | category | flops | bytes accessed | tf_op | source)
XLA Modules:
  0.0 456.3 jit_solution(14352504052544790037)
XLA Ops:
  0.6 0.0 copy-start
  0.7 0.8 reshape_squeeze.6
  1.4 0.1 reshape.49
  1.5 0.5 collective-permute-start
  2.0 0.6 fusion.7
  3.9 0.0 copy-start.6
  3.9 0.0 copy-start.5
  3.9 3.8 dynamic-slice_bitcast_fusion
  7.7 1.2 pad_add_fusion.ends_ref
  9.0 0.8 copy.56
  9.8 1.4 copy.55
  11.3 0.6 add_select_fusion.sel_ref
  11.8 3.4 prepare.1
  15.3 74.3 %forward0.1 = (bf16[1024,768]{1,0:T(8,128)(2,1)}, bf16[1024,384]{1,0:T(8,128)(2,1)}, bf16[51,64,128]{2,1,0:T(8,128)(2,1)}, f32[8,1024]{1,0:T(8,128)}, bf16[48,64...) custom-call(s32[8,128]{1,0:T(8,128)} %get-tuple-element.55.refs_0_, ...), custom_call_target="tpu_custom_call" | custom-call | tf_op jit(solution)/shard_map/forward0/pallas_call | solution.py:760
  89.5 94.5 %forward1.1 = (bf16[1024,768]{1,0:T(8,128)(2,1)}, bf16[1024,384]{1,0:T(8,128)(2,1)}, bf16[51,64,128]{2,1,0:T(8,128)(2,1)}, f32[8,1024]{1,0:T(8,128)}, bf16[48,64...) custom-call(s32[8,128]{1,0:T(8,128)} %get-tuple-element.54.refs_0_, ...), custom_call_target="tpu_custom_call" | custom-call | tf_op jit(solution)/shard_map/forward1/pallas_call | solution.py:760
  184.0 121.7 %backward1.1 = (bf16[1024,768]{1,0:T(8,128)(2,1)}, bf16[2,1024,768]{2,1,0:T(8,128)(2,1)}, f32[2,192,1408]{2,1,0:T(8,128)}) custom-call(s32[8,128]{1,0:T(8,128)} %get-tuple-element.54.refs_0_, bf16[1024,768]{1,0:T(8,128)(2,1)} %get-tuple-element.156.refs_1_, bf16[1024,768]{1,0:T(8,128)(2,1)} %get-tuple-element.60.refs_1_.refs_2_.refs_3_, ...), custom_call_target="tpu_custom_call" | custom-call | tf_op jit(solution)/shard_map/backward1/pallas_call | solution.py:1395
  305.8 121.2 %backward0.1 = (bf16[1024,768]{1,0:T(8,128)(2,1)}, bf16[2,1024,768]{2,1,0:T(8,128)(2,1)}, f32[2,192,1408]{2,1,0:T(8,128)}) custom-call(s32[8,128]{1,0:T(8,128)} %get-tuple-element.55.refs_0_, bf16[1024,768]{1,0:T(8,128)(2,1)} %get-tuple-element.80.refs_1_.refs_3_.refs_4_, bf16[1024,768]{1,0:T(8,128)(2,1)} %get-tuple-element.155.refs_1_.refs_2_, ...), custom_call_target="tpu_custom_call" | custom-call | tf_op jit(solution)/shard_map/backward0/pallas_call | solution.py:1395
  427.0 0.9 fusion.3
  427.9 1.8 broadcast_select_fusion
  429.8 0.7 fusion.1
  430.5 1.1 slice_bitcast_fusion
  431.6 0.1 fusion.6
  431.7 1.1 fusion.5
  432.8 0.1 slice_bitcast_fusion.3
  432.9 0.7 copy.67
  433.5 0.1 copy.61
  433.6 0.1 copy.62
  433.7 0.8 copy.68
  434.5 0.1 reshape_squeeze.7
  434.6 0.3 fusion.4
  434.9 0.8 copy.57
  435.7 1.9 copy.59
  437.6 0.8 copy.58
  438.4 1.0 copy.60
  439.5 1.0 copy.65
  440.4 1.0 copy.66
  441.4 1.0 copy.64
  442.4 1.0 copy.63
  443.4 1.5 copy.71
  444.9 1.5 copy.70
  446.5 1.5 copy.69
  448.0 0.6 maximum_bitcast_fusion.3
  448.6 0.6 maximum_bitcast_fusion.2
  449.2 0.6 maximum_bitcast_fusion.1
  449.7 1.9 maximum_bitcast_fusion
  451.6 1.7 copy.76
  453.3 1.4 copy-done.3
  454.6 1.7 copy.77
  (17 shorter events, 0.1 us)
Async XLA Ops:
  0.6 1.4 copy-start
  1.5 9.7 %collective-permute-start = (s32[4,48]{1,0:T(4,128)S(1)}, s32[4,48]{1,0:T(4,128)S(1)}, u32[]{:S(2)}, u32[]{:S(2)}) collective-permute-start(s32[4,48]{1,0:T(4,128)S(1)} %get-tuple-element.152), channel_id=1, source_target_pairs={{0,16},{16,0},{1,17},{17,1},{2,18},{18,2},{3,19},{19,3},{4,20},{20... | collective-permute-start | bytes 2312 | tf_op jit(solution)/shard_map/ppermute | solution.py:1476
  3.9 5.1 %copy-start.6 = (bf16[1,768,3]{1,2,0:T(4,128)(2,1)S(1)}, bf16[1,768,3]{1,2,0:T(4,128)(2,1)}, u32[]{:S(2)}) copy-start(bf16[1,768,3]{1,2,0:T(4,128)(2,1)} %param.21) | copy-start | bytes 13828
  3.9 5.9 %copy-start.5 = (bf16[1,768,3,192]{1,3,2,0:T(8,128)(2,1)S(1)}, bf16[1,768,3,192]{1,3,2,0:T(8,128)(2,1)}, u32[]{:S(2)}) copy-start(bf16[1,768,3,192]{1,3,2,0:T(8,128)(2,1)} %param.19) | copy-start | bytes 2654212
  305.8 121.2 %copy-start.4 = (f32[2,192,1408]{2,1,0:T(8,128)S(1)}, f32[2,192,1408]{2,1,0:T(8,128)}, u32[]{:S(2)}) copy-start(f32[2,192,1408]{2,1,0:T(8,128)} %get-tuple-element.94) | copy-start | bytes 6488068
  435.7 15.9 %copy-start.2 = (bf16[2,1024,768]{2,1,0:T(8,128)(2,1)S(1)}, bf16[2,1024,768]{2,1,0:T(8,128)(2,1)}, u32[]{:S(2)}) copy-start(bf16[2,1024,768]{2,1,0:T(8,128)(2,1)} %get-tuple-element.79) | copy-start | bytes 9437188
  451.6 3.0 copy-start.3
  454.6 1.7 copy-start.1

commit v4 on v3

--- a/solution.py
+++ b/solution.py
@@ -18,7 +18,7 @@
 F32 = jnp.float32
 GELU_A = 0.044715
 GELU_K = math.sqrt(2.0 / math.pi)
-LIMIT = 60 * 1024 * 1024
+LIMIT = 62 * 1024 * 1024
 
 
 class Sizes:
@@ -336,14 +336,6 @@
             copy.wait()
 
 
-FORWARD_OUTS = KEPT + ("res",)
-FORWARD_SCRATCH = (
-    "gt", "gate", "edge", "edge_gate", "send_kv", "send_gate", "got_gate", "far_gate", "wo_all", "wo_high",
-    "pair_all", "single_all", "part_send", "part_got", "part_via", "own_part", "kv_ss", "kv_rs", "gate_ss", "gate_rs", "edge_ss", "edge_rs",
-    "wo_ss", "wo_rs", "o_ss", "o_rs", "part_ss", "part_rs", "res_ss", "res_rs", "swap_ss", "swap_rs", "load", "saved",
-)
-
-
 class Refs:
     def __init__(self, names, refs):
         assert len(names) == len(refs), (len(names), len(refs))
@@ -351,74 +343,28 @@
             setattr(self, name, ref)
 
 
-def forward_kernel(z, layer, *refs):
-    count = len(WEIGHTS)
-    rt, r_ref = refs[:2]
-    own = dict(zip(WEIGHTS, refs[2 : 2 + count]))
-    refs = refs[2 + count :]
-    theirs = None
-    if layer == 1:
-        theirs, refs = dict(zip(WEIGHTS, refs[:count])), refs[count:]
-    outs, refs = dict(zip(FORWARD_OUTS, refs)), refs[len(FORWARD_OUTS) :]
-    if layer == 0:
-        theirs, refs = dict(zip(WEIGHTS, refs[:count])), refs[count:]
-    held, refs = Refs(FORWARD_OUTS, refs[: len(FORWARD_OUTS)]), refs[len(FORWARD_OUTS) :]
-    used, refs = dict(zip(WEIGHTS, refs[:count])), refs[count:]
-    s = Refs(FORWARD_SCRATCH, refs)
-    me, at, core = lax.axis_index("tensor"), lax.axis_index("seq"), lax.axis_index("section")
+def forward_part(z, layer, e):
+    rt, r_ref, res_ref = e.routes[layer], (e.rows, e.middle)[layer], (e.middle, e.rows)[layer]
+    used, s, me, at, core, load = e.used, e.s, e.me, e.at, e.core, e.load
+    held = e.held(layer)
     last = z.S - 1
     first_row = at * z.rows
-    vec = used["vec"]
-
-    def load(i, source):
-        name = WEIGHTS[i]
-        return pltpu.make_async_copy(source[name], used[name], s.load.at[i])
-
-    def swap(i):
-        name = WEIGHTS[i]
-        return remote(own[name], theirs[name], s.swap_ss.at[i], s.swap_rs.at[i], {"section": 1 - core})
-
-    @pl.when(core == layer)
-    def _():
-        for i in range(count):
-            load(i, own).start()
-
-    if layer == 1:
-
-        @pl.when(core != layer)
-        def _():
-            for i in range(count):
-                load(i, theirs).start()
+    vec = e.vec(layer)
+    edge_ss, edge_rs = s.edge_ss.at[layer], s.edge_rs.at[layer]
+    kv_ss, kv_rs, gate_ss, gate_rs = (
+        sems.at[layer] for sems in (s.kv_ss, s.kv_rs, s.gate_ss, s.gate_rs)
+    )
+    edge, edge_gate, got_gate = s.edge.at[layer], s.edge_gate.at[layer], s.got_gate.at[layer]
+    held.ckv[at * z.cap] = jnp.zeros((TILE, LANES), BF)
+    outs = e.store
 
     def ready(*wanted):
-        if layer == 0:
-
-            @pl.when(core != layer)
-            def _():
-                for i in wanted:
-                    swap(i).wait_recv()
-                    load(i, theirs).start()
-
         for i in wanted:
-            load(i, own).wait()
-
-    held.ckv[at * z.cap] = jnp.zeros((TILE, LANES), BF)
-    barrier = pltpu.get_barrier_semaphore()
-    for step in range(1, z.T):
-        signal(to_tensor(step, me), barrier)
+            e.weight_ready(layer, i)
+
     if layer == 0:
-        signal({"section": 1 - core}, barrier)
-
-    def greet(d, _):
-        signal({"seq": d}, barrier)
-        return 0
-
-    lax.fori_loop(0, at, greet, 0)
-    pl.semaphore_wait(barrier, z.T - 1 + last - at + (layer == 0))
-    if layer == 0:
-        for i in range(count):
-            swap(i).start()
-    saver = Saver(s.saved)
+        e.input_load.wait()
+    saver = Saver(s.saved) if layer == 0 else Unsaved()
     per_block = z.block // TILE
     ready(0)
 
@@ -461,18 +407,18 @@
         return [
             remote(
                 held.kvt.at[h * (z.tiles + 1) + z.tiles],
-                s.edge.at[h],
-                s.edge_ss.at[h],
-                s.edge_rs.at[h],
+                edge.at[h],
+                edge_ss.at[h],
+                edge_rs.at[h],
                 after,
             )
             for h in range(z.heads)
         ] + [
             remote(
                 s.gt.at[:, pl.ds(z.rows, LANES)],
-                s.edge_gate,
-                s.edge_ss.at[z.heads],
-                s.edge_rs.at[z.heads],
+                edge_gate,
+                edge_ss.at[z.heads],
+                edge_rs.at[z.heads],
                 after,
             )
         ]
@@ -487,12 +433,12 @@
             remote(
                 s.send_kv.at[d],
                 held.ckv.at[pl.ds(source * z.cap, z.cap)],
-                s.kv_ss.at[d],
-                s.kv_rs.at[source],
+                kv_ss.at[d],
+                kv_rs.at[source],
                 {"seq": d},
             ),
             remote(
-                s.send_gate.at[d], s.got_gate.at[source], s.gate_ss.at[d], s.gate_rs.at[source], {"seq": d}
+                s.send_gate.at[d], got_gate.at[source], gate_ss.at[d], gate_rs.at[source], {"seq": d}
             ),
         )
 
@@ -510,6 +456,7 @@
             copy.start()
         return 0
 
+    e.turn(layer, "pack")
     lax.fori_loop(0, last - at, pack, 0)
     ready(3)
 
@@ -528,7 +475,7 @@
         for copy in tile_copies(last, source):
             copy.wait_recv()
         for i in range(z.cap):
-            s.far_gate[source * z.cap + i, 0:1, :] = s.got_gate[source, i : i + 1, :]
+            s.far_gate[source * z.cap + i, 0:1, :] = got_gate[source, i : i + 1, :]
         return 0
 
     lax.fori_loop(0, at, landed, 0)
@@ -542,54 +489,64 @@
         for copy in edge_copies():
             copy.wait_recv()
         for h in range(z.heads):
-            held.kvt[h * (z.tiles + 1)] = s.edge[h]
+            held.kvt[h * (z.tiles + 1)] = edge[h]
             s.gate[h * (z.tiles + 1), 0:1, :] = jnp.where(
                 lane[0:1] < TILE,
-                pltpu.roll(s.edge_gate[...], TILE, 1)[h : h + 1],
+                pltpu.roll(edge_gate[...], TILE, 1)[h : h + 1],
                 s.gate[h * (z.tiles + 1), 0:1, :],
             )
 
     saver.save(held.kvt, outs["kvt"])
     saver.save(held.ckv, outs["ckv"])
 
-    def attend(t):
-        base = pl.multiple_of(t * TILE, TILE)
-        query = first_row + base + row
-        begin = jnp.where(
-            query >= rt[ENDS, 1],
-            rt[ENDS, 1],
-            jnp.where(query >= rt[ENDS, 0], rt[ENDS, 0], 0),
-        )
-        key = first_row + base - TILE + lane
-        near_ok = (key <= query) & (key > query - TILE) & (key >= begin)
-        mixed = []
-        for h in range(z.heads):
-            cols = slice(h * LANES, (h + 1) * LANES)
-            u = h * z.tiles + t
-            arrived = rt[ARR, u]
-            far = held.ckv[arrived]
-            near = held.kvt[pl.ds(h * (z.tiles + 1) + t, 2)].reshape(2 * TILE, LANES)
-            keys = jnp.concatenate([near, far, far], axis=0)
-            gates = jnp.concatenate(
-                [s.gate[h * (z.tiles + 1) + t, 0:1, :], s.far_gate[arrived][0:1]], axis=1
+    def attend(tiles):
+        units = [(g, h) for g in range(len(tiles)) for h in range(z.heads)]
+        keys, scores = {}, {}
+        for g, t in enumerate(tiles):
+            base = pl.multiple_of(t * TILE, TILE)
+            query = first_row + base + row
+            begin = jnp.where(
+                query >= rt[ENDS, 1],
+                rt[ENDS, 1],
+                jnp.where(query >= rt[ENDS, 0], rt[ENDS, 0], 0),
             )
-            far_ok = (rt[POS, u] + lane >= begin) & (lane < TILE)
-            score = jnp.where(
-                jnp.concatenate([near_ok, far_ok], axis=1),
-                nt(held.q[pl.ds(base, TILE), cols], keys) + gates,
-                MASKED,
-            )
-            raised = jnp.exp(score - jnp.max(score, axis=-1, keepdims=True))
-            p = (raised * (1.0 / jnp.sum(raised, axis=-1, keepdims=True))).astype(BF)
-            held.p[t * z.heads + h] = p
-            mixed.append(nn(p, keys))
-        pair = jnp.where(lane < TILE, pltpu.roll(mixed[0], TILE, 1), mixed[1]).astype(BF)
-        single = pltpu.roll(mixed[2], TILE, 1)
-        held.o[pl.ds(base, TILE), 0:LANES] = pair
-        held.o[pl.ds(base, TILE), LANES:] = single.astype(BF)
-        s.pair_all[me, pl.ds(base, TILE), :] = pair
-        return single, mixed[2]
-
+            key = first_row + base - TILE + lane
+            near_ok = (key <= query) & (key > query - TILE) & (key >= begin)
+            for h in range(z.heads):
+                u = h * z.tiles + t
+                arrived = rt[ARR, u]
+                far = held.ckv[arrived]
+                near = held.kvt[pl.ds(h * (z.tiles + 1) + t, 2)].reshape(2 * TILE, LANES)
+                keys[g, h] = jnp.concatenate([near, far, far], axis=0)
+                gates = jnp.concatenate(
+                    [s.gate[h * (z.tiles + 1) + t, 0:1, :], s.far_gate[arrived][0:1]], axis=1
+                )
+                far_ok = (rt[POS, u] + lane >= begin) & (lane < TILE)
+                query_tile = held.q[pl.ds(base, TILE), h * LANES : (h + 1) * LANES]
+                scores[g, h] = jnp.where(
+                    jnp.concatenate([near_ok, far_ok], axis=1), nt(query_tile, keys[g, h]) + gates, MASKED
+                )
+        tops = {u: jnp.max(scores[u], axis=-1, keepdims=True) for u in units}
+        raised = {u: jnp.exp(scores[u] - tops[u]) for u in units}
+        sums = {u: jnp.sum(raised[u], axis=-1, keepdims=True) for u in units}
+        probs = {u: (raised[u] * (1.0 / sums[u])).astype(BF) for u in units}
+        mixed = {u: nn(probs[u], keys[u]) for u in units}
+        for g, t in enumerate(tiles):
+            base = pl.multiple_of(t * TILE, TILE)
+            for h in range(z.heads):
+                held.p[t * z.heads + h] = probs[g, h]
+            pair = jnp.where(lane < TILE, pltpu.roll(mixed[g, 0], TILE, 1), mixed[g, 1]).astype(BF)
+            single = pltpu.roll(mixed[g, 2], TILE, 1)
+            held.o[pl.ds(base, TILE), 0:LANES] = pair
+            held.o[pl.ds(base, TILE), LANES:] = single.astype(BF)
+            s.pair_all[me, pl.ds(base, TILE), :] = pair
+            if g % 2 == 0:
+                even = single
+            else:
+                couple = pl.ds(pl.multiple_of((t - 1) * (TILE // 2), TILE), TILE)
+                s.single_all[me, couple, :] = jnp.where(lane < TILE, even, mixed[g, 2]).astype(BF)
+
+    e.turn(layer, "attend")
     half_rows = z.block // 2
 
     def pair_spread(b):
@@ -611,16 +568,7 @@
         )
 
     def attend_block(b, _):
-        def two(i, _):
-            t = b * per_block + 2 * i
-            even, _ = attend(t)
-            _, odd = attend(t + 1)
-            s.single_all[me, pl.ds(pl.multiple_of(b * half_rows + i * TILE, TILE), TILE), :] = jnp.where(
-                lane < TILE, even, odd
-            ).astype(BF)
-            return 0
-
-        lax.fori_loop(0, per_block // 2, two, 0)
+        attend([b * per_block + g for g in range(per_block)])
         pair_spread(b).start()
         single_spread(b).start()
 
@@ -642,9 +590,7 @@
     for t in range(z.T):
         s.wo_high[t, 0:TILE, :] = jnp.zeros((TILE, z.width), BF)
         s.wo_high[t, TILE:, :] = s.wo_all[t, LANES : LANES + TILE, :]
-    collect = Collect(
-        z, me, s.part_send, s.part_got, s.part_via, lambda i: s.part_ss.at[i], lambda i: s.part_rs.at[i]
-    )
+    collect = e.collect(0)
 
     def feed(k, _):
         step = visiting(k)
@@ -681,14 +627,17 @@
 
     lax.fori_loop(0, z.T, feed, 0)
     collect.join()
+    if layer == 0:
+        e.next_weights()
+    e.turn(layer, "feed")
     for name in ("mid", "n2", "u", "act"):
         saver.save(getattr(held, name), outs[name])
     total = collect.total(held.mid[...] + s.own_part[...] + vec[7:8, :])
     own_rows = pl.ds(pl.multiple_of(me * z.block, z.block), z.block)
-    held.res[own_rows, :] = total.astype(BF)
+    res_ref[own_rows, :] = total.astype(BF)
     spread = Spread(
         me,
-        lambda owner, half: held.res.at[
+        lambda owner, half: res_ref.at[
             pl.ds(pl.multiple_of(owner * z.block + half * half_rows, half_rows), half_rows), :
         ],
         lambda i: s.res_ss.at[i],
@@ -716,223 +665,41 @@
         for copy in edge_copies():
             copy.wait_send()
 
-    if layer == 0:
-
-        @pl.when(core == layer)
-        def _():
-            for i in range(count):
-                swap(i).wait_recv()
-
-        for i in range(count):
-            swap(i).wait_send()
     spread.forward()
     for step in range(1, z.T):
         spread.wait(step)
     spread.finish()
-    saver.save(held.res, outs["res"])
+    e.deliver(layer, res_ref, e.layer_out)
     saver.finish()
 
 
-def forward(z, layer, route, r, own, theirs):
-    rows, width, heads = z.rows, z.width, z.heads
-    shapes = dict(
-        n1=((rows, width), BF),
-        q=((rows, z.pad), BF),
-        kvt=((heads * (z.tiles + 1), TILE, LANES), BF),
-        st=((8, rows), F32),
-        p=((z.slots, TILE, 2 * LANES), BF),
-        ckv=((z.n, TILE, LANES), BF),
-        o=((rows, 2 * LANES), BF),
-        mid=((z.block, width), F32),
-        n2=((rows, width), BF),
-        u=((rows, z.hidden), BF),
-        act=((rows, z.hidden), BF),
-        res=((rows, width), BF),
-    )
-    dma = pltpu.SemaphoreType.DMA
-    shaped = [jax.ShapeDtypeStruct(*shapes[name]) for name in FORWARD_OUTS]
-    mine = [own[name] for name in WEIGHTS]
-    if layer == 0:
-        shaped += [jax.ShapeDtypeStruct(value.shape, value.dtype) for value in mine]
-        inputs = [route, r, *mine]
-    else:
-        inputs = [route, r, *mine, *(theirs[name] for name in WEIGHTS)]
-    outs = pl.pallas_call(
-        functools.partial(forward_kernel, z, layer),
-        out_shape=tuple(shaped),
-        in_specs=[smem(), vmem()] + [anywhere()] * (len(inputs) - 2),
-        out_specs=tuple(anywhere() for _ in shaped),
-        scratch_shapes=[
-            *(pltpu.VMEM(*shapes[name]) for name in FORWARD_OUTS),
-            *(pltpu.VMEM(value.shape, value.dtype) for value in mine),
-            pltpu.VMEM((8, rows + 2 * LANES), F32),
-            pltpu.VMEM((heads * (z.tiles + 1), 8, LANES), F32),
-            pltpu.VMEM((heads, TILE, LANES), BF),
-            pltpu.VMEM((8, LANES), F32),
-            pltpu.VMEM((z.S, z.cap, TILE, LANES), BF),
-            pltpu.VMEM((z.S, z.capg, LANES), F32),
-            pltpu.VMEM((z.S, z.capg, LANES), F32),
-            pltpu.VMEM((z.n, 8, LANES), F32),
-            pltpu.VMEM((z.T, 2 * LANES, width), BF),
-            pltpu.VMEM((z.T, LANES, width), BF),
-            pltpu.VMEM((z.T, rows, LANES), BF),
-            pltpu.VMEM((z.T, rows // 2, LANES), BF),
-            pltpu.VMEM((z.T - 1, z.block, width), BF),
-            pltpu.VMEM((2, z.block, width), BF),
-            pltpu.VMEM((2, z.block // 2, width), BF),
-            pltpu.VMEM((z.block, width), F32),
-            dma((z.S,)),
-            dma((z.S,)),
-            dma((z.S,)),
-            dma((z.S,)),
-            dma((heads + 1,)),
-            dma((heads + 1,)),
-            dma((z.T,)),
-            dma((z.T,)),
-            dma((z.T * 12,)),
-            dma((z.T * 12,)),
-            dma((6,)),
-            dma((6,)),
-            dma((6,)),
-            dma((6,)),
-            dma((len(WEIGHTS),)),
-            dma((len(WEIGHTS),)),
-            dma((len(WEIGHTS),)),
-            dma((len(FORWARD_OUTS),)),
-        ],
-        compiler_params=pltpu.CompilerParams(
-            collective_id=layer, has_side_effects=True, vmem_limit_bytes=LIMIT
-        ),
-        name=f"forward{layer}",
-    )(*inputs)
-    kept = dict(zip(FORWARD_OUTS, outs))
-    return (kept, dict(zip(WEIGHTS, outs[len(FORWARD_OUTS) :]))) if layer == 0 else (kept, theirs)
-
-
-BACKWARD_SCRATCH = (
-    "du", "part_send", "part_got", "part_via", "own_part", "dr2", "ob", "dout", "dqkv", "dkv", "dgate", "far", "far_gate",
-    "send_kv", "send_gate", "got_kv", "got_gate", "got_gate_row", "edge_send", "edge_got", "edge_gate_got", "sum",
-    "gate_sum", "tile_gate", "ds", "stat", "stat_got", "grad", "bounce",
-    "pa", "pb", "pc", "pd", "xa", "xb", "xc", "xd", "sa", "sb", "sc", "sd", "ta", "tb", "tc", "td", "ha", "hb", "hc",
-    "kv_ss", "kv_rs", "gate_ss", "gate_rs", "edge_ss", "edge_rs", "part_ss", "part_rs", "ob_ss", "ob_rs",
-    "grad_ss", "grad_rs", "stat_ss", "stat_rs", "give_ss", "give_rs", "cross_ss", "cross_rs", "hand_ss", "hand_rs",
-    "move_ss", "move_rs", "load", "saved",
-)
-
-
-def backward_kernel(z, layer, *refs):
-    count = len(WEIGHTS)
-    rt = refs[0]
-    c_any, r_any, first_any, second_any = refs[1:5]
-    refs = refs[5:]
-    own, refs = dict(zip(WEIGHTS, refs[:count])), refs[count:]
-    theirs, refs = dict(zip(WEIGHTS, refs[:count])), refs[count:]
-    kept, refs = dict(zip(KEPT, refs[: len(KEPT)])), refs[len(KEPT) :]
-    grad_out, both_out, g_out = refs[:3]
-    refs = refs[3:]
-    c_ref, r_ref, refs = refs[0], refs[1], refs[2:]
-    used, refs = dict(zip(WEIGHTS, refs[:count])), refs[count:]
-    k, refs = Refs(KEPT, refs[: len(KEPT)]), refs[len(KEPT) :]
-    s = Refs(BACKWARD_SCRATCH, refs)
-    me, at, core = lax.axis_index("tensor"), lax.axis_index("seq"), lax.axis_index("section")
+def backward_part(z, layer, e):
+    rt, used, s, me, at, core = e.routes[layer], e.used, e.s, e.me, e.at, e.core
+    c_ref, grad_ref = (e.grad, e.cotan) if layer == 0 else (e.cotan, e.grad)
+    k = e.held(layer)
     last = z.S - 1
-    vec = used["vec"]
+    vec = e.vec(layer)
     own_rows = pl.ds(pl.multiple_of(me * z.block, z.block), z.block)
     W = z.width
-    sources = {"c": (c_any, c_ref)}
-    sources |= {name: (kept[name], getattr(k, name)) for name in KEPT}
-    sources["r"] = (r_any.at[own_rows, :], r_ref)
-    order = ("c", "wdn", "u", "wup", "act", "n2", "vec", "mid", "wo", "p", "q", "kvt", "ckv", "o", "st", "w1", "swt", "n1", "r")
-
-    def loads(name, which):
-        i = order.index(name)
-        if name in WEIGHTS:
-            return pltpu.make_async_copy(which[name], used[name], s.load.at[i])
-        return pltpu.make_async_copy(*sources[name], s.load.at[i])
-
-    for name in order:
-        if name in WEIGHTS:
-
-            @pl.when(core == layer)
-            def _(name=name):
-                loads(name, own).start()
-
-            @pl.when(core != layer)
-            def _(name=name):
-                loads(name, theirs).start()
-        else:
-            loads(name, None).start()
+    g_out = e.g_out
+    across = {"section": 1 - core}
 
     def ready(*names):
         for name in names:
-            loads(name, own).wait()
-
-    barrier = pltpu.get_barrier_semaphore()
-    for step in range(1, z.T):
-        signal(to_tensor(step, me), barrier)
-    signal({"section": 1 - core}, barrier)
-
-    def greet(i, _):
-        signal({"seq": (at + i) % z.S}, barrier)
-        return 0
-
-    lax.fori_loop(1, z.S, greet, 0)
-    pl.semaphore_wait(barrier, z.T - 1 + 1 + last)
-    saver = Saver(s.saved)
-    across = {"section": 1 - core}
-
-    def move(src, i, part):
-        return remote(src.at[part], both_out.at[core].at[part], s.move_ss.at[i], s.move_rs.at[i], across)
-
-    def keep(src, part):
-        return pltpu.make_async_copy(src.at[part], both_out.at[core].at[part], s.saved.at[3])
-
-    def fetch(src, i):
-        return pltpu.make_async_copy(src, s.bounce.at[i], s.saved.at[1 + i])
-
-    everything = pl.ds(0, z.rows)
-    stay, leave = s.bounce.at[0], s.bounce.at[1]
-
-    @pl.when(core == 0)
-    def _():
-        fetch(second_any, 1).start()
+            if name in WEIGHTS:
+                e.weight_ready(layer, WEIGHTS.index(name))
+            else:
+                e.kept_ready(layer, name)
+
+    def done(*names):
         if layer == 1:
-            fetch(first_any, 0).start()
-
-    @pl.when(core == 1)
-    def _():
-        fetch(second_any, 0).start()
-        if layer == 1:
-            fetch(first_any, 1).start()
-
-    def forward_rows():
-        def leaving():
-            fetch(second_any, 1).wait()
-            move(leave, 0, everything).start()
-
-        def staying():
-            fetch(second_any, 0).wait()
-            keep(stay, everything).start()
-
-        if layer == 1:
-            leaving()
-            staying()
-        else:
-            pl.when(core == 0)(leaving)
-            pl.when(core == 1)(staying)
-
-    collects = [
-        Collect(
-            z,
-            me,
-            s.part_send.at[phase],
-            s.part_got.at[phase],
-            s.part_via.at[phase],
-            lambda i, phase=phase: s.part_ss.at[phase, i],
-            lambda i, phase=phase: s.part_rs.at[phase, i],
-        )
-        for phase in range(2)
-    ]
+            for name in names:
+                if name in WEIGHTS:
+                    e.weight_again(WEIGHTS.index(name))
+                else:
+                    e.kept_again(name)
+
+    collects = (e.collect(0), e.collect(1))
     half_rows = z.block // 2
 
     def rows_spread(ref, sends, recvs):
@@ -945,7 +712,9 @@
             lambda i: recvs.at[i],
         )
 
-    ready("c", "wdn", "u", "wup")
+    if layer == 1:
+        e.cotan_load.wait()
+    ready("wdn", "u", "wup")
 
     def ff_back(i, _):
         step = visiting(i)
@@ -964,7 +733,6 @@
         return 0
 
     lax.fori_loop(0, z.T, ff_back, 0)
-    collects[0].join()
     ones = jnp.ones((16, z.rows), BF)
     s.stat[...] = jnp.zeros((24, W), F32)
 
@@ -976,7 +744,7 @@
 
     def give(piece):
         return remote(
-            mine[piece].at[1 - core], theirs_part[piece], s.give_ss.at[piece], s.give_rs.at[piece], across
+            mine[piece].at[1 - core if piece < 3 else 0], theirs_part[piece], s.give_ss.at[piece], s.give_rs.at[piece], across
         )
 
     def cross(piece, d, source):
@@ -1000,7 +768,7 @@
 
         def chunk(i, _):
             rows = pl.ds(pl.multiple_of(i * span, span), span)
-            value = mine[piece][core, rows, :].astype(F32) + theirs_part[piece][rows, :].astype(F32)
+            value = mine[piece][core if piece < 3 else 0, rows, :].astype(F32) + theirs_part[piece][rows, :].astype(F32)
             for j in range(span // z.share):
                 d = i * (span // z.share) + j
                 rows_of = value[j * z.share : (j + 1) * z.share]
@@ -1033,7 +801,10 @@
 
         total = lax.fori_loop(1, z.S, add, summed[piece][at].astype(F32))
         cols = slice(offsets[piece], offsets[piece] + z.pieces[piece])
-        g_out[core, :, cols] = total[: z.share]
+
+        @pl.when(core == layer)
+        def _():
+            g_out[core, :, cols] = total[: z.share]
 
         @pl.when(core != layer)
         def _():
@@ -1049,28 +820,38 @@
             hand(piece).wait_recv()
             g_out[1 - core, :, cols] = handed[piece][...].astype(F32)[: z.share]
 
-    forward_rows()
     ready("act", "n2")
-    s.pa[0] = tn(c_ref[...], k.act[...]).astype(BF)
-    s.pa[1] = tn(k.n2[...], s.du[...]).astype(BF)
+    wide = z.hidden // 2
+    for cols in (slice(0, wide), slice(wide, z.hidden)):
+        s.pa[0, :, cols] = tn(c_ref[...], k.act[:, cols]).astype(BF)
+    collects[0].join()
+    for cols in (slice(0, wide), slice(wide, z.hidden)):
+        s.pa[1, :, cols] = tn(k.n2[...], s.du[:, cols]).astype(BF)
     give(0).start()
+    done("wdn", "wup", "u", "act", "n2")
     s.stat[8:9, :] = nn(ones, s.du[...])[0:1]
     s.stat[9:10, :] = nn(ones, c_ref[...])[0:1]
-    ready("vec", "mid", "wo")
+    ready("mid", "wo")
+    add_up(0)
     grad = collects[0].total(s.own_part[...])
     y, spread = normed(k.mid[...])
     dr2 = c_ref[own_rows, :].astype(F32) + norm_back(grad, vec[4:5, :], y, spread)
     s.dr2[...] = dr2
-    s.ob[own_rows, :] = dr2.astype(BF)
-
-    ob_spread = rows_spread(s.ob, s.ob_ss, s.ob_rs)
+    s.wo_all[me] = dr2.astype(BF)
+
+    ob_spread = Spread(
+        me,
+        lambda owner, half: s.wo_all.at[owner, pl.ds(half * half_rows, half_rows), :],
+        lambda i: s.ob_ss.at[i],
+        lambda i: s.ob_rs.at[i],
+    )
     ob_spread.start()
+    done("mid")
     s.stat[0:1, :] = column_sum(dr2)
     s.stat[1:2, :] = column_sum(grad * y)
     s.stat[2:3, :] = column_sum(grad)
     s.dkv[...] = jnp.zeros((z.rows + TILE, z.pad), F32)
     ob_spread.forward()
-    add_up(0)
     lane_wide = grid_of((z.block, LANES), 1)
 
     def out_back(step, _):
@@ -1081,51 +862,63 @@
                 ob_spread.wait(wanted)
 
         rows = pl.ds(pl.multiple_of(partner(me, step) * z.block, z.block), z.block)
-        dout = nt(s.ob[rows, :], used["wo"][...])
+        dout = nt(s.wo_all[partner(me, step)], used["wo"][...])
         pair, single = dout[:, :LANES], dout[:, LANES:]
         for h, value in enumerate((pltpu.roll(pair, TILE, 1), pair, pltpu.roll(single, TILE, 1))):
-            s.dout[rows, h * LANES : (h + 1) * LANES] = jnp.where(lane_wide < TILE, 0.0, value).astype(BF)
+            s.pair_all[h, rows, :] = jnp.where(lane_wide < TILE, 0.0, value).astype(BF)
         return 0
 
     lax.fori_loop(0, z.T, out_back, 0)
+    done("wo")
+    collects[0].finish()
     ready("p", "q", "kvt", "ckv")
 
-    def attend_back(t):
-        base = pl.multiple_of(t * TILE, TILE)
-        for h in range(z.heads):
-            cols = slice(h * LANES, (h + 1) * LANES)
-            u = h * z.tiles + t
-            arrived = rt[ARR, u]
-            near = k.kvt[pl.ds(h * (z.tiles + 1) + t, 2)].reshape(2 * TILE, LANES)
-            far = k.ckv[arrived]
-            keys = jnp.concatenate([near, far, far], axis=0)
-            query = k.q[pl.ds(base, TILE), cols]
-            dout = s.dout[pl.ds(base, TILE), cols]
-            p = k.p[t * z.heads + h]
-            weight = p.astype(F32)
-            dp = nt(dout, keys)
-            dz = (weight * (dp - jnp.sum(weight * dp, axis=-1, keepdims=True))).astype(BF)
-            s.dqkv[pl.ds(base, TILE), cols] = nn(dz, keys).astype(BF)
-            dkeys = tn(jnp.concatenate([dz, p], axis=0), jnp.concatenate([query, dout], axis=0))
-            s.dkv[pl.ds(base, 2 * TILE), cols] += dkeys[: 2 * TILE]
-            s.far[u] = dkeys[2 * TILE : 3 * TILE].astype(BF)
-            gates = column_sum(dz.astype(F32))
-            s.dgate[t, h : h + 1, :] = gates[:, :LANES]
-            s.far_gate[u, 0:1, :] = gates[:, LANES:]
-
-    def attend_back_pair(i, _):
-        attend_back(2 * i)
-        attend_back(2 * i + 1)
-        return 0
-
-    lax.fori_loop(0, z.tiles // 2, attend_back_pair, 0)
+    ones_row = jnp.ones((16, TILE), BF)
+
+    def attend_back(i, _):
+        tiles = [i * group + g for g in range(group)]
+        units = [(g, h) for g in range(group) for h in range(z.heads)]
+        keys, query, dout, prob, dprob = {}, {}, {}, {}, {}
+        for g, t in enumerate(tiles):
+            base = pl.multiple_of(t * TILE, TILE)
+            for h in range(z.heads):
+                cols = slice(h * LANES, (h + 1) * LANES)
+                far = k.ckv[rt[ARR, h * z.tiles + t]]
+                near = k.kvt[pl.ds(h * (z.tiles + 1) + t, 2)].reshape(2 * TILE, LANES)
+                keys[g, h] = jnp.concatenate([near, far, far], axis=0)
+                query[g, h] = k.q[pl.ds(base, TILE), cols]
+                dout[g, h] = s.pair_all[h, pl.ds(base, TILE), :]
+                prob[g, h] = k.p[t * z.heads + h]
+                dprob[g, h] = nt(dout[g, h], keys[g, h])
+        totals = {u: jnp.sum(prob[u].astype(F32) * dprob[u], axis=-1, keepdims=True) for u in units}
+        dz = {u: (prob[u].astype(F32) * (dprob[u] - totals[u])).astype(BF) for u in units}
+        for g, t in enumerate(tiles):
+            base = pl.multiple_of(t * TILE, TILE)
+            for h in range(z.heads):
+                cols = slice(h * LANES, (h + 1) * LANES)
+                u = h * z.tiles + t
+                s.dqkv[pl.ds(base, TILE), cols] = nn(dz[g, h], keys[g, h]).astype(BF)
+                dkeys = tn(
+                    jnp.concatenate([dz[g, h], prob[g, h]], axis=0),
+                    jnp.concatenate([query[g, h], dout[g, h]], axis=0),
+                )
+                s.dkv[pl.ds(base, 2 * TILE), cols] += dkeys[: 2 * TILE]
+                s.far[u] = dkeys[2 * TILE : 3 * TILE].astype(BF)
+                gates = nn(ones_row, dz[g, h])[0:1]
+                s.dgate[t, h : h + 1, :] = gates[:, :LANES]
+                s.far_gate[u, 0:1, :] = gates[:, LANES:]
+        return 0
+
+    group = 4
+    lax.fori_loop(0, z.tiles // group, attend_back, 0)
+    done("p", "q", "kvt", "ckv")
     s.dgate[z.tiles] = jnp.zeros((8, LANES), F32)
 
     def edge_copies():
         behind = {"seq": jnp.maximum(at - 1, 0)}
         return (
-            remote(s.edge_send, s.edge_got, s.edge_ss.at[0], s.edge_rs.at[0], behind),
-            remote(s.dgate.at[0], s.edge_gate_got, s.edge_ss.at[1], s.edge_rs.at[1], behind),
+            remote(s.edge_send, s.edge_got, s.back_edge_ss.at[0], s.back_edge_rs.at[0], behind),
+            remote(s.dgate.at[0], s.edge_gate_got, s.back_edge_ss.at[1], s.back_edge_rs.at[1], behind),
         )
 
     @pl.when(at > 0)
@@ -1139,12 +932,12 @@
             remote(
                 s.send_kv.at[d],
                 s.got_kv.at[pl.ds(source * z.cap, z.cap)],
-                s.kv_ss.at[d],
-                s.kv_rs.at[source],
+                s.back_kv_ss.at[d],
+                s.back_kv_rs.at[source],
                 {"seq": d},
             ),
             remote(
-                s.send_gate.at[d], s.got_gate.at[source], s.gate_ss.at[d], s.gate_rs.at[source], {"seq": d}
+                s.back_send_gate.at[d], s.back_got_gate.at[source], s.back_gate_ss.at[d], s.back_gate_rs.at[source], {"seq": d}
             ),
         )
 
@@ -1152,7 +945,7 @@
         def slot(i, _):
             u = rt[INV, d * z.cap + i]
             s.send_kv[d, i] = s.far[u]
-            s.send_gate[d, pl.ds(i, 1), :] = s.far_gate[u][0:1]
+            s.back_send_gate[d, pl.ds(i, 1), :] = s.far_gate[u][0:1]
             return 0
 
         lax.fori_loop(0, z.cap, slot, 0)
@@ -1162,14 +955,14 @@
 
     lax.fori_loop(0, at, pack, 0)
     ready("o")
-    out_grad = tn(s.ob[...], k.o[...]).astype(BF)
+    out_grad = tn(s.wo_all[...].reshape(z.rows, W), k.o[...]).astype(BF)
+    done("o")
     s.pb[0] = out_grad[:, :LANES]
     s.pb[1] = out_grad[:, LANES:]
     give(1).start()
     s.sum[z.n] = jnp.zeros((TILE, LANES), F32)
     s.gate_sum[z.n] = jnp.zeros((8, LANES), F32)
-    ready("st", "w1", "swt", "n1", "r")
-    add_up(1)
+    ready("st", "w1", "swt", "n1")
 
     @pl.when(at < last)
     def _():
@@ -1182,7 +975,7 @@
         for copy in tile_copies(0, source):
             copy.wait_recv()
         for i in range(z.cap):
-            s.got_gate_row[source * z.cap + i, 0:1, :] = s.got_gate[source, i : i + 1, :]
+            s.got_gate_row[source * z.cap + i, 0:1, :] = s.back_got_gate[source, i : i + 1, :]
         return 0
 
     lax.fori_loop(at + 1, z.S, landed, 0)
@@ -1235,6 +1028,7 @@
         return 0
 
     lax.fori_loop(0, z.T, in_back, 0)
+    done("st", "w1", "swt")
     collects[1].join()
     s.pc[0] = tn(k.n1[...], s.dqkv[:, z.pad :]).astype(BF)
     queries = tn(k.n1[...], s.dqkv[:, : z.pad])
@@ -1246,23 +1040,30 @@
     s.pc[1, :, 2 * LANES :] = jnp.zeros((W, z.pad - 2 * LANES), BF)
     give(2).start()
     s.stat[10:13, :] = nn(s.ds[...].astype(BF), k.n1[...])[0:3]
-    source, target = grid_of((W, W), 0), grid_of((W, W), 1)
+    done("n1")
+    source, target = grid_of((W, 1), 0), grid_of((1, W), 1)
     is_value = source >= z.pad
     index = jnp.where(is_value, source - z.pad, source)
     index = index // LANES * TILE + index % TILE
     each = z.heads * TILE // z.S
     wanted = index // each * z.share + index % each + jnp.where(is_value, each, 0)
     filled = (source % LANES >= TILE) == is_value
-    spread_out = jnp.where(
-        (wanted == target) & filled, jnp.where(is_value, 1.0, TILE**-0.5), 0.0
-    ).astype(BF)
+    wanted = jnp.where(filled, wanted, -1)
+    spread_out = jnp.where(wanted == target, jnp.where(is_value, 1.0, TILE**-0.5), 0.0).astype(BF)
     s.stat[13:14, :] = nn(nn(ones, s.dqkv[...]).astype(BF), spread_out)[0:1]
+    reduce(0)
+    add_up(1)
+    add_up(2)
     grad = collects[1].total(s.own_part[...])
-    y, spread = normed(r_ref[...].astype(F32))
+    if layer == 1:
+        entry = e.middle[own_rows, :]
+    else:
+        e.entry_load.wait()
+        entry = s.entry[...]
+    y, spread = normed(entry.astype(F32))
     dr = s.dr2[...] + norm_back(grad, vec[0:1, :], y, spread)
-    s.grad[own_rows, :] = dr.astype(BF)
-    grad_spread = rows_spread(s.grad, s.grad_ss, s.grad_rs)
-    grad_spread.start()
+    grad_ref[own_rows, :] = dr.astype(BF)
+    grad_spread = rows_spread(grad_ref, s.grad_ss, s.grad_rs)
     s.stat[3:4, :] = column_sum(grad * y)
     s.stat[4:5, :] = column_sum(grad)
 
@@ -1277,43 +1078,36 @@
 
     for step in range(1, z.T):
         stat_copy(step).start()
+    grad_spread.start()
     shared = s.stat[0:8, :]
     for step in range(1, z.T):
         stat_copy(step).wait()
         shared += s.stat_got[step - 1]
     stats = jnp.concatenate([shared, s.stat[8:16, :]], axis=0).astype(BF)
     unit = (grid_of((16, LANES), 0) == grid_of((16, LANES), 1)).astype(F32).astype(BF)
-    s.pd[core] = tn(stats, unit).astype(BF)
-    s.pd[1 - core] = s.pd[core]
+    s.pd[0] = tn(stats, unit).astype(BF)
 
     @pl.when(core != layer)
     def _():
         give(3).start()
 
     grad_spread.forward()
-    add_up(2)
 
     @pl.when(core == layer)
     def _():
         add_up(3)
 
-    reduce(0)
     reduce(1)
     take(0)
     take(1)
 
-    def block_of(step):
-        return pl.ds(pl.multiple_of(partner(me, step) * z.block, z.block), z.block)
-
     for step in range(z.T):
         grad_spread.wait(step)
         if layer == 0:
-
-            @pl.when(core == 1)
-            def _(step=step):
-                move(s.grad, step, block_of(step)).start()
-
-    saver.save(s.grad, grad_out)
+            e.deliver_block(grad_ref, step)
+
+    if layer == 1:
+        e.deliver(1, grad_ref, e.input_grad)
     reduce(2)
     take(2)
 
@@ -1345,8 +1139,7 @@
             return 0
 
         lax.fori_loop(1, z.S, crossed_over, 0)
-    for collect in collects:
-        collect.finish()
+    collects[1].finish()
     ob_spread.finish()
     grad_spread.finish()
 
@@ -1362,114 +1155,340 @@
         for copy in edge_copies():
             copy.wait_send()
 
-    if layer == 1:
-        move(leave, 0, everything).wait()
-        keep(stay, everything).wait()
-    else:
-
+
+class Unsaved:
+    def save(self, src, dst):
+        pass
+
+    def finish(self):
+        pass
+
+
+class Env:
+    pass
+
+
+def layers_kernel(z, names, *refs):
+    count = len(WEIGHTS)
+    e = Env()
+    e.routes, refs = refs[:2], refs[2:]
+    tokens, cotangent, refs = refs[0], refs[1], refs[2:]
+    own, refs = dict(zip(WEIGHTS, refs[:count])), refs[count:]
+    e.layer_out, e.input_grad, e.g_out, refs = refs[0], refs[1], refs[2], refs[3:]
+    theirs, refs = dict(zip(WEIGHTS, refs[:count])), refs[count:]
+    e.store, refs = dict(zip(KEPT, refs[: len(KEPT)])), refs[len(KEPT) :]
+    e.used, refs = dict(zip(WEIGHTS, refs[:count])), refs[count:]
+    held, refs = dict(zip(KEPT, refs[: len(KEPT)])), refs[len(KEPT) :]
+    s = e.s = Refs(names, refs)
+    e.rows, e.middle, e.cotan, e.grad = s.rows, s.middle, s.cotan, s.grad
+    me, at, core = e.me, e.at, e.core = lax.axis_index("tensor"), lax.axis_index("seq"), lax.axis_index("section")
+    across = {"section": 1 - core}
+    own_rows = pl.ds(pl.multiple_of(me * z.block, z.block), z.block)
+    e.input_load = pltpu.make_async_copy(tokens, s.rows, s.load.at[0])
+    e.cotan_load = pltpu.make_async_copy(cotangent, s.cotan, s.load.at[1])
+    e.entry_load = pltpu.make_async_copy(tokens.at[own_rows, :], s.entry, s.load.at[2])
+    e.input_load.start()
+
+    def vec(layer):
+        return e.used["vec"].at[layer]
+
+    def chosen_keys(layer):
+        return s.ckv_next if layer == 1 else held["ckv"]
+
+    def held_in(layer):
+        return Refs(KEPT, [chosen_keys(layer) if name == "ckv" else held[name] for name in KEPT])
+
+    e.vec, e.held = vec, held_in
+
+    def load(layer, i, source):
+        name = WEIGHTS[i]
+        target = e.used[name].at[layer] if name == "vec" else e.used[name]
+        return pltpu.make_async_copy(source[name], target, s.weight_load.at[i])
+
+    e.load = load
+
+    def swap(i):
+        name = WEIGHTS[i]
+        return remote(own[name], theirs[name], s.swap_ss.at[i], s.swap_rs.at[i], across)
+
+    def start_weight(layer, i):
+        @pl.when(core == layer)
+        def _():
+            load(layer, i, own).start()
+
+        @pl.when(core != layer)
+        def _():
+            load(layer, i, theirs).start()
+
+    loaded = {0: set(), 1: set()}
+    pending = {}
+
+    def weight_ready(layer, i):
+        if layer == 0 and i not in loaded[0]:
+
+            @pl.when(core != layer)
+            def _():
+                swap(i).wait_recv()
+                load(layer, i, theirs).start()
+
+            loaded[0].add(i)
+            load(layer, i, own).wait()
+        elif pending.pop((layer, i), False):
+            load(layer, i, own).wait()
+
+    def next_weights():
         @pl.when(core == 0)
         def _():
-            keep(s.grad, everything).start()
-            move(leave, 0, everything).wait_send()
-            for step in range(z.T):
-                move(s.grad, step, block_of(step)).wait_recv()
+            for i in range(count):
+                swap(i).wait_recv()
+
+        for i in range(count):
+            start_weight(1, i)
+            pending[1, i] = True
+
+    def weight_again(i):
+        if WEIGHTS[i] != "vec":
+            start_weight(0, i)
+            pending[0, i] = True
+
+    e.weight_ready, e.next_weights, e.weight_again = weight_ready, next_weights, weight_again
+    kept_pending = {}
+
+    def kept_load(name):
+        return pltpu.make_async_copy(e.store[name], held[name], s.kept_load.at[KEPT.index(name)])
+
+    def kept_again(name):
+        if name != "ckv":
+            kept_load(name).start()
+            kept_pending[name] = True
+
+    def kept_ready(layer, name):
+        if kept_pending.pop(name, False):
+            kept_load(name).wait()
+
+    e.kept_again, e.kept_ready = kept_again, kept_ready
+
+    def collect(phase):
+        return Collect(
+            z,
+            me,
+            s.part_send,
+            s.part_got,
+            s.part_via,
+            lambda i: s.part_ss.at[phase, i],
+            lambda i: s.part_rs.at[phase, i],
+        )
+
+    e.collect = collect
+    delivered = []
+
+    def rows_to(ref, target, slot, part):
+        local = pltpu.make_async_copy(ref.at[part, :], target.at[core].at[part, :], s.keep.at[slot])
+        return local, remote(
+            ref.at[part, :], target.at[core].at[part, :], s.move_ss.at[slot], s.move_rs.at[slot], across
+        )
+
+    everything = pl.ds(0, z.rows)
+
+    def deliver(layer, ref, target):
+        slot = len(delivered)
+        local, away = rows_to(ref, target, slot, everything)
+
+        @pl.when(core == layer)
+        def _():
+            local.start()
+
+        @pl.when(core != layer)
+        def _():
+            away.start()
+
+        delivered.append((layer, local, away))
+
+    def deliver_block(ref, step):
+        slot = len(delivered)
+        part = pl.ds(pl.multiple_of(partner(me, step) * z.block, z.block), z.block)
+        local, away = rows_to(ref, target=e.input_grad, slot=slot, part=part)
+
+        @pl.when(core == 0)
+        def _():
+            local.start()
 
         @pl.when(core == 1)
         def _():
-            move(leave, 0, everything).wait_recv()
-            for step in range(z.T):
-                move(s.grad, step, block_of(step)).wait_send()
-
-        keep(s.grad, everything).wait()
-    saver.finish()
-
-
-def backward(z, layer, route, c, r, first, second, own, theirs, kept):
-    rows, width = z.rows, z.width
-    dma = pltpu.SemaphoreType.DMA
-    wide = sum(z.pieces)
+            away.start()
+
+        delivered.append((0, local, away))
+
+    e.deliver, e.deliver_block = deliver, deliver_block
+
+    def turn(layer, where):
+        if (layer, where) == TURN_FROM:
+
+            @pl.when(core == 0)
+            def _():
+                pl.semaphore_signal(s.turn, inc=1, device_id=across, device_id_type=MESH)
+
+        if (layer, where) == TURN_TO:
+
+            @pl.when(core == 1)
+            def _():
+                pl.semaphore_wait(s.turn, 1)
+
+    e.turn = turn
+
+    @pl.when(core == 0)
+    def _():
+        for i in range(count):
+            load(0, i, own).start()
+
+    barrier = pltpu.get_barrier_semaphore()
+    for step in range(1, z.T):
+        signal(to_tensor(step, me), barrier)
+    signal(across, barrier)
+
+    def greet(i, _):
+        signal({"seq": (at + i) % z.S}, barrier)
+        return 0
+
+    lax.fori_loop(1, z.S, greet, 0)
+    pl.semaphore_wait(barrier, z.T - 1 + 1 + z.S - 1)
+    for i in range(count):
+        swap(i).start()
+    e.cotan_load.start()
+    e.entry_load.start()
+    forward_part(z, 0, e)
+    forward_part(z, 1, e)
+    backward_part(z, 1, e)
+    backward_part(z, 0, e)
+    for i in range(count):
+        swap(i).wait_send()
+    for layer, local, away in delivered:
+
+        @pl.when(core == layer)
+        def _(local=local, away=away):
+            local.wait()
+            away.wait_recv()
+
+        @pl.when(core != layer)
+        def _(away=away):
+            away.wait_send()
+
+
+TURN_FROM, TURN_TO = (0, "attend"), (0, "pack")
+
+
+def layers(z, routes, tokens, cotangent, own):
+    rows, width, heads = z.rows, z.width, z.heads
+    half = z.block // 2
+    kept = dict(
+        n1=((rows, width), BF),
+        q=((rows, z.pad), BF),
+        kvt=((heads * (z.tiles + 1), TILE, LANES), BF),
+        st=((8, rows), F32),
+        p=((z.slots, TILE, 2 * LANES), BF),
+        ckv=((z.n, TILE, LANES), BF),
+        o=((rows, 2 * LANES), BF),
+        mid=((z.block, width), F32),
+        n2=((rows, width), BF),
+        u=((rows, z.hidden), BF),
+        act=((rows, z.hidden), BF),
+    )
     weights = [own[name] for name in WEIGHTS]
-    saved = [kept[name] for name in KEPT]
-    inputs = [route, c, r, first, second, *weights, *(theirs[name] for name in WEIGHTS), *saved]
-    parts = [(w,) for w in z.pieces]
-    return pl.pallas_call(
-        functools.partial(backward_kernel, z, layer),
-        out_shape=(
-            jax.ShapeDtypeStruct((rows, width), BF),
-            jax.ShapeDtypeStruct((2, rows, width), BF),
-            jax.ShapeDtypeStruct((2, z.share, wide), F32),
-        ),
-        in_specs=[smem()] + [anywhere()] * (len(inputs) - 1),
-        out_specs=(anywhere(), anywhere(), vmem()),
+    vmem_of, dma = pltpu.VMEM, pltpu.SemaphoreType.DMA
+    scratch = dict(
+        rows=vmem_of((rows, width), BF),
+        middle=vmem_of((rows, width), BF),
+        cotan=vmem_of((rows, width), BF),
+        grad=vmem_of((rows, width), BF),
+        entry=vmem_of((z.block, width), BF),
+        ckv_next=vmem_of((z.n, TILE, LANES), BF),
+        gt=vmem_of((8, rows + 2 * LANES), F32),
+        gate=vmem_of((heads * (z.tiles + 1), 8, LANES), F32),
+        edge=vmem_of((2, heads, TILE, LANES), BF),
+        edge_gate=vmem_of((2, 8, LANES), F32),
+        send_kv=vmem_of((z.S, z.cap, TILE, LANES), BF),
+        send_gate=vmem_of((z.S, z.capg, LANES), F32),
+        got_gate=vmem_of((2, z.S, z.capg, LANES), F32),
+        far_gate=vmem_of((max(z.n, z.slots), 8, LANES), F32),
+        wo_all=vmem_of((z.T, max(2 * LANES, z.block), width), BF),
+        wo_high=vmem_of((z.T, LANES, width), BF),
+        pair_all=vmem_of((z.T, rows, LANES), BF),
+        single_all=vmem_of((z.T, rows // 2, LANES), BF),
+        part_send=vmem_of((z.T - 1, z.block, width), BF),
+        part_got=vmem_of((2, z.block, width), BF),
+        part_via=vmem_of((2, half, width), BF),
+        own_part=vmem_of((z.block, width), F32),
+        du=vmem_of((rows, z.hidden), BF),
+        dr2=vmem_of((z.block, width), F32),
+        dqkv=vmem_of((rows, 2 * z.pad), BF),
+        dkv=vmem_of((rows + TILE, z.pad), F32),
+        dgate=vmem_of((z.tiles + 1, 8, LANES), F32),
+        far=vmem_of((z.slots, TILE, LANES), BF),
+        back_send_gate=vmem_of((z.S, z.capg, LANES), F32),
+        got_kv=vmem_of((z.n, TILE, LANES), BF),
+        back_got_gate=vmem_of((z.S, z.capg, LANES), F32),
+        got_gate_row=vmem_of((z.n, 8, LANES), F32),
+        edge_send=vmem_of((TILE, z.pad), BF),
+        edge_got=vmem_of((TILE, z.pad), BF),
+        edge_gate_got=vmem_of((8, LANES), F32),
+        sum=vmem_of((z.n + 1, TILE, LANES), F32),
+        gate_sum=vmem_of((z.n + 1, 8, LANES), F32),
+        tile_gate=vmem_of((z.tiles, 8, LANES), F32),
+        ds=vmem_of((16, rows), F32),
+        stat=vmem_of((24, width), F32),
+        stat_got=vmem_of((z.T - 1, 8, width), F32),
+    )
+    for name, w in zip("abcd", z.pieces):
+        scratch["p" + name] = vmem_of((1 if name == "d" else 2, width, w), BF)
+        scratch["x" + name] = vmem_of((width, w), BF)
+        scratch["s" + name] = vmem_of((z.S, z.padded, w), BF)
+        scratch["t" + name] = vmem_of((z.S, z.padded, w), BF)
+        if name != "d":
+            scratch["h" + name] = vmem_of((z.padded, w), BF)
+    pairs = dict(
+        kv=(2, z.S), gate=(2, z.S), edge=(2, heads + 1), wo=(z.T,), o=(z.T * 12,), part=(2, 6), res=(6,),
+        swap=(len(WEIGHTS),), move=(3 + z.T,), back_kv=(z.S,), back_gate=(z.S,), back_edge=(2,), ob=(6,),
+        grad=(6,), stat=(z.T,), give=(4,), cross=(4, z.S), hand=(3,),
+    )
+    for name, shape in pairs.items():
+        scratch[name + "_ss"] = dma(shape)
+        scratch[name + "_rs"] = dma(shape)
+    scratch |= dict(
+        load=dma((3,)),
+        weight_load=dma((len(WEIGHTS),)),
+        kept_load=dma((len(KEPT),)),
+        saved=dma((len(KEPT),)),
+        keep=dma((3 + z.T,)),
+        turn=pltpu.SemaphoreType.REGULAR,
+    )
+    doubled = {"vec"}
+
+    def room(name, shape, kind):
+        return vmem_of((2, *shape) if name in doubled else shape, kind)
+
+    shaped = (
+        jax.ShapeDtypeStruct((2, rows, width), BF),
+        jax.ShapeDtypeStruct((2, rows, width), BF),
+        jax.ShapeDtypeStruct((2, z.share, sum(z.pieces)), F32),
+        *(jax.ShapeDtypeStruct(value.shape, value.dtype) for value in weights),
+        *(jax.ShapeDtypeStruct(*kept[name]) for name in KEPT),
+    )
+    outs = pl.pallas_call(
+        functools.partial(layers_kernel, z, tuple(scratch)),
+        out_shape=shaped,
+        in_specs=[smem(), smem()] + [anywhere()] * (2 + len(weights)),
+        out_specs=tuple(vmem() if i == 2 else anywhere() for i in range(len(shaped))),
         scratch_shapes=[
-            pltpu.VMEM((rows, width), BF),
-            pltpu.VMEM((z.block, width), BF),
-            *(pltpu.VMEM(value.shape, value.dtype) for value in weights),
-            *(pltpu.VMEM(value.shape, value.dtype) for value in saved),
-            pltpu.VMEM((rows, z.hidden), BF),
-            pltpu.VMEM((2, z.T - 1, z.block, width), BF),
-            pltpu.VMEM((2, 2, z.block, width), BF),
-            pltpu.VMEM((2, 2, z.block // 2, width), BF),
-            pltpu.VMEM((z.block, width), F32),
-            pltpu.VMEM((z.block, width), F32),
-            pltpu.VMEM((rows, width), BF),
-            pltpu.VMEM((rows, z.pad), BF),
-            pltpu.VMEM((rows, 2 * z.pad), BF),
-            pltpu.VMEM((rows + TILE, z.pad), F32),
-            pltpu.VMEM((z.tiles + 1, 8, LANES), F32),
-            pltpu.VMEM((z.slots, TILE, LANES), BF),
-            pltpu.VMEM((z.slots, 8, LANES), F32),
-            pltpu.VMEM((z.S, z.cap, TILE, LANES), BF),
-            pltpu.VMEM((z.S, z.capg, LANES), F32),
-            pltpu.VMEM((z.n, TILE, LANES), BF),
-            pltpu.VMEM((z.S, z.capg, LANES), F32),
-            pltpu.VMEM((z.n, 8, LANES), F32),
-            pltpu.VMEM((TILE, z.pad), BF),
-            pltpu.VMEM((TILE, z.pad), BF),
-            pltpu.VMEM((8, LANES), F32),
-            pltpu.VMEM((z.n + 1, TILE, LANES), F32),
-            pltpu.VMEM((z.n + 1, 8, LANES), F32),
-            pltpu.VMEM((z.tiles, 8, LANES), F32),
-            pltpu.VMEM((16, rows), F32),
-            pltpu.VMEM((24, width), F32),
-            pltpu.VMEM((z.T - 1, 8, width), F32),
-            pltpu.VMEM((rows, width), BF),
-            pltpu.VMEM((2, rows, width), BF),
-            *(pltpu.VMEM((2, width, w), BF) for w in z.pieces),
-            *(pltpu.VMEM((width, w), BF) for w in z.pieces),
-            *(pltpu.VMEM((z.S, z.padded, w), BF) for w in z.pieces),
-            *(pltpu.VMEM((z.S, z.padded, w), BF) for w in z.pieces),
-            *(pltpu.VMEM((z.padded, w), BF) for w in z.pieces[:3]),
-            dma((z.S,)),
-            dma((z.S,)),
-            dma((z.S,)),
-            dma((z.S,)),
-            dma((2,)),
-            dma((2,)),
-            dma((2, 6)),
-            dma((2, 6)),
-            dma((6,)),
-            dma((6,)),
-            dma((6,)),
-            dma((6,)),
-            dma((z.T,)),
-            dma((z.T,)),
-            dma((4,)),
-            dma((4,)),
-            dma((4, z.S)),
-            dma((4, z.S)),
-            dma((3,)),
-            dma((3,)),
-            dma((z.T,)),
-            dma((z.T,)),
-            dma((2 + len(WEIGHTS) + len(KEPT),)),
-            dma((4,)),
+            *(room(name, value.shape, value.dtype) for name, value in zip(WEIGHTS, weights)),
+            *(room(name, *kept[name]) for name in KEPT),
+            *scratch.values(),
         ],
         compiler_params=pltpu.CompilerParams(
-            collective_id=2 + layer, has_side_effects=True, vmem_limit_bytes=LIMIT
+            collective_id=0, has_side_effects=True, vmem_limit_bytes=LIMIT
         ),
-        name=f"backward{layer}",
-    )(*inputs)
+        name="layers",
+    )(*routes, tokens, cotangent, *weights)
+    return outs[:3]
 
 
 def swapped(value):
@@ -1527,15 +1546,7 @@
     own |= dict(wup=up_weight[0], wdn=down_weight[0])
     first = lax.dynamic_index_in_dim(tokens, core, 0, keepdims=False)
     cotan = lax.dynamic_index_in_dim(cotangent, core, 0, keepdims=False)
-    zero, theirs = forward(z, 0, routes[0], first, own, None)
-    one, _ = forward(z, 1, routes[1], zero["res"], own, theirs)
-    grad1, layer_out, g1 = backward(
-        z, 1, routes[1], cotan, zero["res"], zero["res"], one["res"], own, theirs, one
-    )
-    grad0, input_grad, g0 = backward(
-        z, 0, routes[0], grad1, first, grad1, grad1, own, theirs, zero
-    )
-    total = jnp.where(core == 0, g0, g1)
+    layer_out, input_grad, total = layers(z, routes, first, cotan, own)
     share = z.share
     c_o, c_i = hidden, hidden + LANES
     pairs = total[0, :, c_i : c_i + z.pad].reshape(share, heads, LANES)
@@ -1549,7 +1560,7 @@
     )
     out_grad = jnp.concatenate([total[0, :, c_o:c_i], total[1, :, c_o:c_i]], axis=1)[:, :inner]
     c_s = c_i + z.pad
-    kept_stats = jnp.where(core == 0, g0[0, :, c_s : c_s + 16], g1[1, :, c_s : c_s + 16])
+    kept_stats = lax.dynamic_index_in_dim(total, core, 0, keepdims=False)[:, c_s : c_s + 16]
     stats = kept_stats.T
     each = inner // z.S
     return (

time: 458 us -> 401 us (0.88)
  Pallas kernels: 415 us -> 349 us
  local copies, waits for them, and re-layouts: 29.8 us -> 36.8 us
    pallas_call x4 -> x1, Pallas kernels: 412 us -> 346 us  [layers(): pl.pallas_call(functools.partial(layers_kernel, z, tuple(scratch)), out_s...]
    unnamed x23 -> x21, local copies, waits for them, and re-layouts: 13.1 us -> 14 us
where the time goes in v4:
time: 401 us; the launch traced here: 396 us
  Pallas kernels  349 us (87%)
  local copies, waits for them, and re-layouts  36.8 us (9%)
  other arithmetic  7.11 us (2%)
    pallas_call x1, Pallas kernels, layers(): pl.pallas_call(functools.partial(layers_kernel, z, tuple(scratch)), out_s...  346 us
    unnamed x21, local copies, waits for them, and re-layouts  14 us
  transfers between devices with their start and end apart: 1, of which 0 were waited for; matrix products, arithmetic and copies ran while one was open for 2% of the time, Pallas kernels for 0%

profile of v4, /device:TPU:0, one launch (start us, length us, event | category | flops | bytes accessed | tf_op | source)
XLA Modules:
  0.0 395.6 jit_solution(6900745224495016020)
XLA Ops:
  0.6 0.0 copy-start
  0.7 0.8 reshape_squeeze.6
  1.4 0.1 reshape.47
  1.5 0.5 collective-permute-start
  2.0 0.6 fusion.4
  3.9 0.0 copy-start.5
  3.9 0.0 copy-start.4
  3.9 3.8 dynamic-slice_bitcast_fusion
  7.7 1.2 pad_add_fusion.ends_ref
  9.0 0.8 copy.49
  9.8 0.0 copy-done.4
  9.8 1.4 copy.48
  11.3 0.0 collective-permute-done
  11.3 0.6 add_select_fusion.sel_ref
  11.9 3.4 prepare.1
  15.3 345.8 %layers.1 = (bf16[2,1024,768]{2,1,0:T(8,128)(2,1)}, bf16[2,1024,768]{2,1,0:T(8,128)(2,1)}, f32[2,192,1408]{2,1,0:T(8,128)}, f32[8,768]{1,0:T(8,128)}, bf16[768,7...) custom-call(s32[8,128]{1,0:T(8,128)} %get-tuple-element.22.refs_0_, ...), custom_call_target="tpu_custom_call" | custom-call | tf_op jit(solution)/shard_map/layers/pallas_call | solution.py:1476
  361.1 1.6 multiply_bitcast_fusion
  362.7 1.1 slice_bitcast_fusion.4
  363.8 1.0 slice.76
  364.8 1.3 dynamic-slice_bitcast_fusion.2
  366.1 1.1 slice_bitcast_fusion
  367.2 0.7 slice_bitcast_fusion.1
  368.0 0.7 fusion.3
  368.7 1.1 fusion.2
  369.8 0.8 copy.61
  370.6 0.1 reshape_squeeze.7
  370.7 0.3 fusion.1
  371.0 0.8 copy.50
  371.8 1.9 copy.52
  373.7 0.8 copy.51
  374.5 1.0 copy.53
  375.6 1.6 copy.60
  377.1 0.8 copy.54
  377.9 0.8 copy.55
  378.7 1.0 copy.58
  379.7 1.0 copy.59
  380.7 1.0 copy.57
  381.7 1.0 copy.56
  382.6 1.5 copy.64
  384.2 1.5 copy.63
  385.7 1.5 copy.62
  387.3 0.6 maximum_bitcast_fusion.3
  387.8 0.6 maximum_bitcast_fusion.2
  388.4 0.6 maximum_bitcast_fusion.1
  389.0 1.9 maximum_bitcast_fusion
  390.9 1.7 copy.69
  392.6 1.4 copy-done.2
  393.9 1.7 copy.70
  (12 shorter events, 0.1 us)
Async XLA Ops:
  0.6 1.4 copy-start
  1.5 9.7 %collective-permute-start = (s32[4,48]{1,0:T(4,128)S(1)}, s32[4,48]{1,0:T(4,128)S(1)}, u32[]{:S(2)}, u32[]{:S(2)}) collective-permute-start(s32[4,48]{1,0:T(4,128)S(1)} %get-tuple-element.86), channel_id=1, source_target_pairs={{0,16},{16,0},{1,17},{17,1},{2,18},{18,2},{3,19},{19,3},{4,20},{20... | collective-permute-start | bytes 2312 | tf_op jit(solution)/shard_map/ppermute | solution.py:1495
  3.9 5.1 %copy-start.5 = (bf16[1,768,3]{1,2,0:T(4,128)(2,1)S(1)}, bf16[1,768,3]{1,2,0:T(4,128)(2,1)}, u32[]{:S(2)}) copy-start(bf16[1,768,3]{1,2,0:T(4,128)(2,1)} %param.21) | copy-start | bytes 13828
  3.9 5.9 %copy-start.4 = (bf16[1,768,3,192]{1,3,2,0:T(8,128)(2,1)S(1)}, bf16[1,768,3,192]{1,3,2,0:T(8,128)(2,1)}, u32[]{:S(2)}) copy-start(bf16[1,768,3,192]{1,3,2,0:T(8,128)(2,1)} %param.19) | copy-start | bytes 2654212
  362.7 3.4 copy-start.1
  371.8 19.1 %copy-start.3 = (bf16[2,1024,768]{2,1,0:T(8,128)(2,1)S(1)}, bf16[2,1024,768]{2,1,0:T(8,128)(2,1)}, u32[]{:S(2)}) copy-start(bf16[2,1024,768]{2,1,0:T(8,128)(2,1)} %get-tuple-element.28) | copy-start | bytes 9437188
  390.9 3.0 copy-start.2

commit v5 on v4

--- a/solution.py
+++ b/solution.py
@@ -95,8 +95,9 @@
 
 def prepare_kernel(
     z,
-    ends_ref,
-    sel_ref,
+    length_ref,
+    kept_ref,
+    got_ref,
     win_ref,
     bin_ref,
     sw_ref,
@@ -136,8 +137,10 @@
     wo_ref[0:inner, :] = wout_ref[...]
     wo_ref[inner:, :] = jnp.zeros((2 * LANES - inner, z.width), BF)
 
-    at = lax.axis_index("seq")
+    at, core = lax.axis_index("seq"), lax.axis_index("section")
     n, slots, cap = z.n, z.slots, z.cap
+    first_end = length_ref[core, 0]
+    second_end = first_end + length_ref[core, 1]
     shift = z.tiles.bit_length() - 1
     near = 1e-3
 
@@ -149,7 +152,7 @@
 
     for layer, rt in enumerate((rt0_ref, rt1_ref)):
         rt[...] = jnp.zeros((8, LANES), jnp.int32)
-        chosen = sel_ref[layer]
+        chosen = jnp.where(core == layer, kept_ref[...], got_ref[...])
         owner = lax.shift_right_arithmetic(chosen, shift)
         sub, lan = grid_of((slots, n), 0), grid_of((slots, n), 1)
         wide = jnp.zeros((slots, n), jnp.int32)
@@ -207,10 +210,10 @@
         upto = jnp.sum((key_col <= tile).astype(F32), axis=0, keepdims=True)
         has = jnp.sum((key_col == tile).astype(F32), axis=0, keepdims=True)
         rt[LAST : LAST + 1, :slots] = whole(jnp.where(has > 0.5, upto - 1.0, n * 1.0))
-        rt[ENDS : ENDS + 1, :] = jnp.where(grid_of((1, LANES), 1) == 0, ends_ref[0], ends_ref[1])
-
-
-def prepare(z, ends, sel, win, bin_, sw, wout, bout, bup, bdn, gain, shift):
+        rt[ENDS : ENDS + 1, :] = jnp.where(grid_of((1, LANES), 1) == 0, first_end, second_end)
+
+
+def prepare(z, lengths, kept, got, win, bin_, sw, wout, bout, bup, bdn, gain, shift):
     table = jax.ShapeDtypeStruct((8, LANES), jnp.int32)
     outs = pl.pallas_call(
         functools.partial(prepare_kernel, z),
@@ -222,10 +225,10 @@
             table,
             table,
         ),
-        in_specs=[smem()] + [vmem()] * 10,
+        in_specs=[smem()] + [vmem()] * 11,
         out_specs=tuple(vmem() for _ in range(6)),
         name="prepare",
-    )(ends, sel, win, bin_, sw, wout, bout, bup, bdn, gain, shift)
+    )(lengths, kept, got, win, bin_, sw, wout, bout, bup, bdn, gain, shift)
     return dict(zip(WEIGHTS[:4], outs)), outs[4:]
 
 
@@ -368,18 +371,13 @@
     per_block = z.block // TILE
     ready(0)
 
-    def norm_in(b, _):
-        rows = pl.ds(b * z.block, z.block)
+    def norm_in(b):
+        rows = pl.ds(pl.multiple_of(b * z.block, z.block), z.block)
         y, _ = normed(r_ref[rows, :].astype(F32))
         held.n1[rows, :] = (y * vec[0:1, :] + vec[1:2, :]).astype(BF)
-        return 0
-
-    lax.fori_loop(0, z.T, norm_in, 0)
-    saver.save(held.n1, outs["n1"])
-    ready(1, 2)
-
-    def project(b, _):
-        rows = pl.ds(b * z.block, z.block)
+
+    def project(b):
+        rows = pl.ds(pl.multiple_of(b * z.block, z.block), z.block)
         qkv = (nn(held.n1[rows, :], used["w1"][...]) + vec[2:3, :]).astype(BF)
         held.q[rows, :] = qkv[:, : z.pad]
         for h in range(z.heads):
@@ -387,9 +385,38 @@
             held.kvt[pl.ds(h * (z.tiles + 1) + 1 + b * per_block, per_block)] = pairs.reshape(
                 per_block, TILE, LANES
             )
-        return 0
-
-    lax.fori_loop(0, z.T, project, 0)
+
+    def each_norm(b, _):
+        norm_in(b)
+        return 0
+
+    def each_project(b, _):
+        project(b)
+        return 0
+
+    def arrived_block(step, _):
+        for wanted in range(1, z.T):
+
+            @pl.when(step == wanted)
+            def _(wanted=wanted):
+                e.arriving.wait(wanted)
+
+        norm_in(partner(me, step))
+        project(partner(me, step))
+        return 0
+
+    if layer == 0:
+        lax.fori_loop(0, z.T, each_norm, 0)
+        saver.save(held.n1, outs["n1"])
+        ready(1, 2)
+        lax.fori_loop(0, z.T, each_project, 0)
+    else:
+        ready(1, 2)
+        arrived_block(0, 0)
+        e.arriving.forward()
+        lax.fori_loop(1, z.T, arrived_block, 0)
+        e.arriving.finish()
+        e.deliver(0, r_ref, e.layer_out)
     score = nt(used["swt"][...], held.n1[...])[0:8]
     held.st[...] = score
     gate = jnp.minimum(score, 0.0) - jnp.log1p(jnp.exp(-jnp.abs(score)))
@@ -600,13 +627,18 @@
         for other in range(1, z.T):
             pair_spread(block).wait(other)
             single_spread(block).wait(other)
-        mixed = nn(s.pair_all[0, rows, :], s.wo_all[0, 0:LANES, :])
-        even = nn(s.single_all[0, few, :], s.wo_all[0, LANES:, :])
-        odd = nn(s.single_all[0, few, :], s.wo_high[0])
-        for other in range(1, z.T):
-            mixed += nn(s.pair_all[other, rows, :], s.wo_all[other, 0:LANES, :])
-            even += nn(s.single_all[other, few, :], s.wo_all[other, LANES:, :])
-            odd += nn(s.single_all[other, few, :], s.wo_high[other])
+        def joined(value, weight):
+            return sum(
+                nn(
+                    jnp.concatenate([value(t), value(t + 1)], axis=1),
+                    jnp.concatenate([weight(t), weight(t + 1)], axis=0),
+                )
+                for t in range(0, z.T, 2)
+            )
+
+        mixed = joined(lambda t: s.pair_all[t, rows, :], lambda t: s.wo_all[t, 0:LANES, :])
+        even = joined(lambda t: s.single_all[t, few, :], lambda t: s.wo_all[t, LANES : 2 * LANES, :])
+        odd = joined(lambda t: s.single_all[t, few, :], lambda t: s.wo_high[t])
         turns = []
         for i in range(per_block // 2):
             turns += [even[i * TILE : (i + 1) * TILE], odd[i * TILE : (i + 1) * TILE]]
@@ -643,7 +675,9 @@
         lambda i: s.res_ss.at[i],
         lambda i: s.res_rs.at[i],
     )
-    spread.start()
+    e.arriving = spread
+    if layer == 0:
+        spread.start()
     collect.finish()
 
     def finish_block(b, _):
@@ -665,11 +699,6 @@
         for copy in edge_copies():
             copy.wait_send()
 
-    spread.forward()
-    for step in range(1, z.T):
-        spread.wait(step)
-    spread.finish()
-    e.deliver(layer, res_ref, e.layer_out)
     saver.finish()
 
 
@@ -699,7 +728,7 @@
                 else:
                     e.kept_again(name)
 
-    collects = (e.collect(0), e.collect(1))
+    collects = (e.collect(1), e.collect(2))
     half_rows = z.block // 2
 
     def rows_spread(ref, sends, recvs):
@@ -871,6 +900,8 @@
     lax.fori_loop(0, z.T, out_back, 0)
     done("wo")
     collects[0].finish()
+    if layer == 1:
+        e.arriving.start()
     ready("p", "q", "kvt", "ckv")
 
     ones_row = jnp.ones((16, TILE), BF)
@@ -954,6 +985,8 @@
         return 0
 
     lax.fori_loop(0, at, pack, 0)
+    if layer == 1:
+        e.arriving.forward()
     ready("o")
     out_grad = tn(s.wo_all[...].reshape(z.rows, W), k.o[...]).astype(BF)
     done("o")
@@ -1005,6 +1038,11 @@
         return 0
 
     lax.fori_loop(0, z.tiles, settle, 0)
+    if layer == 1:
+        for step in range(1, z.T):
+            e.arriving.wait(step)
+        e.arriving.finish()
+        e.deliver(1, e.rows, e.layer_out)
     lane = grid_of((8, LANES), 1)
     head_row = grid_of((8, LANES), 0)
     for i in range(z.tiles // 2):
@@ -1184,9 +1222,9 @@
     me, at, core = e.me, e.at, e.core = lax.axis_index("tensor"), lax.axis_index("seq"), lax.axis_index("section")
     across = {"section": 1 - core}
     own_rows = pl.ds(pl.multiple_of(me * z.block, z.block), z.block)
-    e.input_load = pltpu.make_async_copy(tokens, s.rows, s.load.at[0])
-    e.cotan_load = pltpu.make_async_copy(cotangent, s.cotan, s.load.at[1])
-    e.entry_load = pltpu.make_async_copy(tokens.at[own_rows, :], s.entry, s.load.at[2])
+    e.input_load = pltpu.make_async_copy(tokens.at[core], s.rows, s.load.at[0])
+    e.cotan_load = pltpu.make_async_copy(cotangent.at[core], s.cotan, s.load.at[1])
+    e.entry_load = pltpu.make_async_copy(tokens.at[core].at[own_rows, :], s.entry, s.load.at[2])
     e.input_load.start()
 
     def vec(layer):
@@ -1273,8 +1311,8 @@
             z,
             me,
             s.part_send,
-            s.part_got,
-            s.part_via,
+            s.part_got.at[phase % 2],
+            s.part_via.at[phase % 2],
             lambda i: s.part_ss.at[phase, i],
             lambda i: s.part_rs.at[phase, i],
         )
@@ -1415,8 +1453,8 @@
         pair_all=vmem_of((z.T, rows, LANES), BF),
         single_all=vmem_of((z.T, rows // 2, LANES), BF),
         part_send=vmem_of((z.T - 1, z.block, width), BF),
-        part_got=vmem_of((2, z.block, width), BF),
-        part_via=vmem_of((2, half, width), BF),
+        part_got=vmem_of((2, 2, z.block, width), BF),
+        part_via=vmem_of((2, 2, half, width), BF),
         own_part=vmem_of((z.block, width), F32),
         du=vmem_of((rows, z.hidden), BF),
         dr2=vmem_of((z.block, width), F32),
@@ -1446,7 +1484,7 @@
         if name != "d":
             scratch["h" + name] = vmem_of((z.padded, w), BF)
     pairs = dict(
-        kv=(2, z.S), gate=(2, z.S), edge=(2, heads + 1), wo=(z.T,), o=(z.T * 12,), part=(2, 6), res=(6,),
+        kv=(2, z.S), gate=(2, z.S), edge=(2, heads + 1), wo=(z.T,), o=(z.T * 12,), part=(3, 6), res=(6,),
         swap=(len(WEIGHTS),), move=(3 + z.T,), back_kv=(z.S,), back_gate=(z.S,), back_edge=(2,), ob=(6,),
         grad=(6,), stat=(z.T,), give=(4,), cross=(4, z.S), hand=(3,),
     )
@@ -1489,6 +1527,62 @@
         name="layers",
     )(*routes, tokens, cotangent, *weights)
     return outs[:3]
+
+
+UNPACKED = (
+    "input_weight", "input_bias", "score", "out", "out_bias", "up", "up_bias", "down", "down_bias", "gain", "shift",
+)
+
+
+def unpack_kernel(z, head, total_ref, *refs):
+    out = Refs(UNPACKED, refs)
+    core = lax.axis_index("section")
+    inner, hidden, share = z.heads * head, z.hidden, z.share
+    c_o, c_i = hidden, hidden + LANES
+    c_s = c_i + z.pad
+    out.up[...] = total_ref[1, :, :hidden]
+    out.down[...] = total_ref[0, :, :hidden].T
+    first, second = total_ref[0, :, c_o:c_i].T, total_ref[1, :, c_o:c_i].T
+    out.out[0:LANES, :] = first
+    out.out[LANES:inner, :] = second[: inner - LANES]
+    out.input_weight[0] = head**-0.5 * total_ref[1, :, c_i : c_i + inner]
+    lane = grid_of((share, LANES), 1)
+    pairs = [total_ref[0, :, c_i + h * LANES : c_i + (h + 1) * LANES] for h in range(z.heads)]
+    turned = [pltpu.roll(pair, LANES // 2, 1) for pair in pairs]
+    out.input_weight[1, :, 0:LANES] = jnp.where(lane < head, pairs[0], turned[1])
+    out.input_weight[1, :, LANES:inner] = pairs[2][:, :head]
+    out.input_weight[2, :, 0:LANES] = jnp.where(lane < head, turned[0], pairs[1])
+    out.input_weight[2, :, LANES:inner] = turned[2][:, :head]
+    stats = total_ref[core, :, c_s : c_s + LANES]
+    rows = stats.T
+    out.score[...] = pltpu.roll(stats, LANES - 10, 1)[:, : z.heads]
+    each = inner // z.S
+    out.input_bias[0:1, :] = rows[13:14, :each]
+    out.input_bias[1:2, :] = pltpu.roll(rows[8:16], share - each, 1)[5:6, :each]
+    out.out_bias[...] = rows[0:1]
+    out.up_bias[...] = rows[8:9]
+    out.down_bias[...] = rows[9:10]
+    out.gain[0:1, :] = rows[3:4]
+    out.gain[1:2, :] = rows[1:2]
+    out.shift[0:1, :] = rows[4:5]
+    out.shift[1:2, :] = rows[2:3]
+
+
+def unpack(z, head, total):
+    inner, hidden, share = z.heads * head, z.hidden, z.share
+    shapes = (
+        (3, share, inner), (2, inner // z.S), (share, z.heads), (inner, share), (1, share), (share, hidden), (1, share),
+        (hidden, share), (1, share), (2, share), (2, share),
+    )
+    outs = pl.pallas_call(
+        functools.partial(unpack_kernel, z, head),
+        out_shape=tuple(jax.ShapeDtypeStruct(shape, F32) for shape in shapes),
+        in_specs=[vmem()],
+        out_specs=tuple(vmem() for _ in shapes),
+        compiler_params=pltpu.CompilerParams(vmem_limit_bytes=LIMIT // 2),
+        name="unpack",
+    )(total)
+    return dict(zip(UNPACKED, outs))
 
 
 def swapped(value):
@@ -1524,15 +1618,11 @@
     )
     kept_choice = lax.dynamic_index_in_dim(grouped, core, 0, keepdims=False)
     got_choice = swapped(lax.dynamic_index_in_dim(grouped, 1 - core, 0, keepdims=False))
-    choice = jnp.where(
-        core == 0, jnp.stack([kept_choice, got_choice]), jnp.stack([got_choice, kept_choice])
-    )
-    length = lax.dynamic_index_in_dim(lengths, core, 0, keepdims=False)
-    ends = jnp.stack([length[0], length[0] + length[1]])
     own, routes = prepare(
         z,
-        ends,
-        choice,
+        lengths,
+        kept_choice,
+        got_choice,
         input_weight[0].transpose(1, 0, 2),
         input_bias[0],
         score_weight[0],
@@ -1544,40 +1634,22 @@
         norm_bias[0],
     )
     own |= dict(wup=up_weight[0], wdn=down_weight[0])
-    first = lax.dynamic_index_in_dim(tokens, core, 0, keepdims=False)
-    cotan = lax.dynamic_index_in_dim(cotangent, core, 0, keepdims=False)
-    layer_out, input_grad, total = layers(z, routes, first, cotan, own)
-    share = z.share
-    c_o, c_i = hidden, hidden + LANES
-    pairs = total[0, :, c_i : c_i + z.pad].reshape(share, heads, LANES)
-    input_weight_grad = jnp.stack(
-        [
-            scale * total[1, :, c_i : c_i + inner],
-            pairs[:, :, :head].reshape(share, inner),
-            pairs[:, :, head:].reshape(share, inner),
-        ],
-        axis=1,
-    )
-    out_grad = jnp.concatenate([total[0, :, c_o:c_i], total[1, :, c_o:c_i]], axis=1)[:, :inner]
-    c_s = c_i + z.pad
-    kept_stats = lax.dynamic_index_in_dim(total, core, 0, keepdims=False)[:, c_s : c_s + 16]
-    stats = kept_stats.T
-    each = inner // z.S
-    return (
-        layer_out[None],
-        input_grad[None],
-        input_weight_grad[None],
-        jnp.stack([stats[13, :each], stats[13, each : 2 * each]])[None],
-        kept_stats[:, 10 : 10 + heads][None],
-        out_grad.T[None],
-        stats[0][None],
-        total[1, :, :hidden][None],
-        stats[8][None],
-        total[0, :, :hidden].T[None],
-        stats[9][None],
-        jnp.stack([stats[3], stats[1]])[None],
-        jnp.stack([stats[4], stats[2]])[None],
-    )
+    layer_out, input_grad, total = layers(z, routes, tokens, cotangent, own)
+    parts = unpack(z, head, total)
+    parts["input_weight"] = parts["input_weight"].transpose(1, 0, 2)
+    return (layer_out[None], input_grad[None], *(part.reshape(1, *shape) for part, shape in (
+        (parts["input_weight"], (z.share, 3, inner)),
+        (parts["input_bias"], (2, inner // z.S)),
+        (parts["score"], (z.share, heads)),
+        (parts["out"], (inner, z.share)),
+        (parts["out_bias"], (z.share,)),
+        (parts["up"], (z.share, hidden)),
+        (parts["up_bias"], (z.share,)),
+        (parts["down"], (hidden, z.share)),
+        (parts["down_bias"], (z.share,)),
+        (parts["gain"], (2, z.share)),
+        (parts["shift"], (2, z.share)),
+    )))
 
 
 def solution(mesh):

time: 401 us -> 353 us (0.88)
  local copies, waits for them, and re-layouts: 36.8 us -> 14.8 us
  Pallas kernels: 349 us -> 333 us
  other arithmetic: 7.11 us -> 0 us
    pallas_call x1, Pallas kernels: 346 us -> 328 us  [layers(): pl.pallas_call(functools.partial(layers_kernel, z, tuple(scratch)), out_s...]
    slice x13 -> x0, local copies, waits for them, and re-layouts: 10.8 us -> none  [the longest x2 2.05 us: body(): stats[4]]
    squeeze x3 -> x1, local copies, waits for them, and re-layouts: 6.25 us -> 0.59 us  [body(): lax.dynamic_index_in_dim(grouped, 1 - core, 0, keepdims=False)]
    unnamed x21 -> x12, local copies, waits for them, and re-layouts: 14 us -> 13.3 us
  transfers between devices with their start and end apart: 1 -> 1, of which waited for: 0 -> 0; matrix products, arithmetic and copies ran while one was open for 2% -> 1% of each run, Pallas kernels for 0% -> 0%
where the time goes in v5:
time: 353 us; the launch traced here: 349 us
  Pallas kernels  333 us (94%)
  local copies, waits for them, and re-layouts  14.8 us (4%)
    pallas_call x1, Pallas kernels, layers(): pl.pallas_call(functools.partial(layers_kernel, z, tuple(scratch)), out_s...  328 us
    unnamed x12, local copies, waits for them, and re-layouts  13.3 us
  transfers between devices with their start and end apart: 1, of which 0 were waited for; matrix products, arithmetic and copies ran while one was open for 1% of the time, Pallas kernels for 0%

profile of v5, /device:TPU:0, one launch (start us, length us, event | category | flops | bytes accessed | tf_op | source)
XLA Modules:
  0.0 349.1 jit_solution(15210003093242052773)
XLA Ops:
  0.6 0.8 reshape_squeeze.3
  1.4 0.1 reshape.53
  1.5 0.6 dynamic-slice_bitcast_fusion
  2.1 0.5 collective-permute-start
  2.6 1.5 copy.35
  4.1 2.3 copy.34
  6.4 0.0 collective-permute-done.got_ref
  6.4 0.0 copy-start.2
  6.4 0.6 copy-done.2
  7.0 3.4 prepare.1
  10.4 328.3 %layers.1 = (bf16[2,1024,768]{2,1,0:T(8,128)(2,1)}, bf16[2,1024,768]{2,1,0:T(8,128)(2,1)}, f32[2,192,1408]{2,1,0:T(8,128)}, f32[8,768]{1,0:T(8,128)}, bf16[768,7...) custom-call(s32[8,128]{1,0:T(8,128)} %get-tuple-element.33.refs_0_, ...), custom_call_target="tpu_custom_call" | custom-call | tf_op jit(solution)/shard_map/layers/pallas_call | solution.py:1514
  338.7 0.0 copy-start
  338.7 1.6 copy-done
  340.3 1.5 unpack.1
  341.8 0.7 copy.36
  342.5 1.1 copy.37
  343.5 0.0 copy-start.1
  343.5 3.9 %copy.42 = bf16[1,2,1024,768]{3,2,1,0:T(8,128)(2,1)} copy(bf16[1,2,1024,768]{3,2,1,0:T(8,128)(2,1)} %bitcast.35) | data formatting | bytes 6291456
  347.5 0.0 copy-done.1
  347.5 1.7 copy.43
  (1 shorter events, 0.0 us)
Async XLA Ops:
  2.1 4.3 %collective-permute-start = (s32[4,48]{1,0:T(4,128)S(1)}, s32[4,48]{1,0:T(4,128)S(1)}, u32[]{:S(2)}, u32[]{:S(2)}) collective-permute-start(s32[4,48]{1,0:T(4,128)S(1)} %get-tuple-element.79), channel_id=1, source_target_pairs={{0,16},{16,0},{1,17},{17,1},{2,18},{18,2},{3,19},{19,3},{4,20},{20... | collective-permute-start | bytes 2312 | tf_op jit(solution)/shard_map/ppermute | solution.py:1589
  6.4 0.6 copy-start.2
  338.7 1.6 copy-start
  343.5 3.9 %copy-start.1 = (bf16[2,1024,768]{2,1,0:T(8,128)(2,1)S(1)}, bf16[2,1024,768]{2,1,0:T(8,128)(2,1)}, u32[]{:S(2)}) copy-start(bf16[2,1024,768]{2,1,0:T(8,128)(2,1)} %get-tuple-element.40) | copy-start | bytes 9437188

commit v6 on v5

--- a/solution.py
+++ b/solution.py
@@ -785,6 +785,27 @@
             {"seq": d},
         )
 
+    stepwise = z.S == 4
+    near_by, far_off = at + 1 - 2 * (at % 2), (at + 2) % z.S
+
+    def hop(piece, i):
+        block, target = ((near_by, near_by), ((near_by + 2) % z.S, near_by), (far_off, far_off))[i]
+        return remote(
+            summed[piece].at[block],
+            crossed[piece].at[i],
+            s.cross_ss.at[piece, i],
+            s.cross_rs.at[piece, i],
+            {"seq": target},
+        )
+
+    def relay(piece):
+        if stepwise:
+            hop(piece, 1).wait_recv()
+            summed[piece][far_off] = (
+                summed[piece][far_off].astype(F32) + crossed[piece][1].astype(F32)
+            ).astype(BF)
+            hop(piece, 2).start()
+
     def hand(piece):
         return remote(
             summed[piece].at[at], handed[piece], s.hand_ss.at[piece], s.hand_rs.at[piece], across
@@ -807,13 +828,18 @@
                     )
                 summed[piece][d] = rows_of.astype(BF)
 
-                @pl.when(d != at)
-                def _():
-                    cross(piece, d, at).start()
+                if not stepwise:
+
+                    @pl.when(d != at)
+                    def _():
+                        cross(piece, d, at).start()
 
             return 0
 
         lax.fori_loop(0, W // span, chunk, 0)
+        if stepwise:
+            hop(piece, 0).start()
+            hop(piece, 1).start()
 
     offsets = [sum(z.pieces[:piece]) for piece in range(len(z.pieces))]
 
@@ -823,12 +849,18 @@
             cross(piece, d, d).wait_recv()
             return 0
 
-        lax.fori_loop(1, z.S, wait, 0)
-
         def add(i, running):
             return running + crossed[piece][(at + i) % z.S].astype(F32)
 
-        total = lax.fori_loop(1, z.S, add, summed[piece][at].astype(F32))
+        if stepwise:
+            hop(piece, 0).wait_recv()
+            hop(piece, 2).wait_recv()
+            total = (
+                summed[piece][at].astype(F32) + crossed[piece][0].astype(F32) + crossed[piece][2].astype(F32)
+            )
+        else:
+            lax.fori_loop(1, z.S, wait, 0)
+            total = lax.fori_loop(1, z.S, add, summed[piece][at].astype(F32))
         cols = slice(offsets[piece], offsets[piece] + z.pieces[piece])
 
         @pl.when(core == layer)
@@ -840,6 +872,17 @@
             if piece < len(handed):
                 summed[piece][at] = total.astype(BF)
                 hand(piece).start()
+
+    def crossed_over(piece):
+        def one(i, _):
+            cross(piece, (at + i) % z.S, at).wait_send()
+            return 0
+
+        if stepwise:
+            for i in range(3):
+                hop(piece, i).wait_send()
+        else:
+            lax.fori_loop(1, z.S, one, 0)
 
     def take(piece):
         cols = slice(offsets[piece], offsets[piece] + z.pieces[piece])
@@ -861,6 +904,8 @@
     s.stat[8:9, :] = nn(ones, s.du[...])[0:1]
     s.stat[9:10, :] = nn(ones, c_ref[...])[0:1]
     ready("mid", "wo")
+    if layer == 0:
+        e.leftover()
     add_up(0)
     grad = collects[0].total(s.own_part[...])
     y, spread = normed(k.mid[...])
@@ -881,6 +926,7 @@
     s.stat[2:3, :] = column_sum(grad)
     s.dkv[...] = jnp.zeros((z.rows + TILE, z.pad), F32)
     ob_spread.forward()
+    relay(0)
     lane_wide = grid_of((z.block, LANES), 1)
 
     def out_back(step, _):
@@ -1067,8 +1113,8 @@
 
     lax.fori_loop(0, z.T, in_back, 0)
     done("st", "w1", "swt")
+    s.pc[0] = tn(k.n1[...], s.dqkv[:, z.pad :]).astype(BF)
     collects[1].join()
-    s.pc[0] = tn(k.n1[...], s.dqkv[:, z.pad :]).astype(BF)
     queries = tn(k.n1[...], s.dqkv[:, : z.pad])
     lane_full = grid_of((W, LANES), 1)
     s.pc[1, :, :LANES] = jnp.where(
@@ -1130,14 +1176,12 @@
         give(3).start()
 
     grad_spread.forward()
+    relay(1)
+    relay(2)
 
     @pl.when(core == layer)
     def _():
         add_up(3)
-
-    reduce(1)
-    take(0)
-    take(1)
 
     for step in range(z.T):
         grad_spread.wait(step)
@@ -1146,37 +1190,38 @@
 
     if layer == 1:
         e.deliver(1, grad_ref, e.input_grad)
-    reduce(2)
-    take(2)
-
-    @pl.when(core == layer)
-    def _():
-        reduce(3)
-
-    def last_sent(i, _):
-        cross(3, (at + i) % z.S, at).wait_send()
-        return 0
-
-    @pl.when(core == layer)
-    def _():
-        lax.fori_loop(1, z.S, last_sent, 0)
-
-    @pl.when(core != layer)
-    def _():
-        give(3).wait_send()
+    def settle_sums():
+        reduce(1)
+        take(0)
+        take(1)
+
+        @pl.when(core == layer)
+        def _():
+            relay(3)
+
+        reduce(2)
+        take(2)
+
+        @pl.when(core == layer)
+        def _():
+            reduce(3)
+            crossed_over(3)
+
+        @pl.when(core != layer)
+        def _():
+            give(3).wait_send()
+            for piece in range(3):
+                hand(piece).wait_send()
+
+        for piece in range(3):
+            crossed_over(piece)
 
     for piece in range(3):
         give(piece).wait_send()
-
-        @pl.when(core != layer)
-        def _(piece=piece):
-            hand(piece).wait_send()
-
-        def crossed_over(i, _, piece=piece):
-            cross(piece, (at + i) % z.S, at).wait_send()
-            return 0
-
-        lax.fori_loop(1, z.S, crossed_over, 0)
+    if layer == 1:
+        e.leftover = settle_sums
+    else:
+        settle_sums()
     collects[1].finish()
     ob_spread.finish()
     grad_spread.finish()

time: 353 us -> 337 us (0.955); the launches traced: 349 us -> 337 us
  Pallas kernels: 333 us -> 321 us
    pallas_call x1, Pallas kernels: 328 us -> 316 us  [layers(): pl.pallas_call(functools.partial(layers_kernel, z, tuple(scratch)), out_s...]
where the time goes in v6:
time: 337 us
  Pallas kernels  321 us (95%)
  local copies, waits for them, and re-layouts  14.8 us (4%)
    pallas_call x1, Pallas kernels, layers(): pl.pallas_call(functools.partial(layers_kernel, z, tuple(scratch)), out_s...  316 us
    unnamed x12, local copies, waits for them, and re-layouts  13.3 us
  transfers between devices with their start and end apart: 1, of which 0 were waited for; matrix products, arithmetic and copies ran while one was open for 1% of the time, Pallas kernels for 0%

profile of v6, /device:TPU:0, one launch (start us, length us, event | category | flops | bytes accessed | tf_op | source)
XLA Modules:
  0.0 336.9 jit_solution(12216008961020397526)
XLA Ops:
  0.6 0.8 reshape_squeeze.3
  1.4 0.1 reshape.53
  1.5 0.6 dynamic-slice_bitcast_fusion
  2.1 0.5 collective-permute-start
  2.6 1.5 copy.35
  4.1 2.3 copy.34
  6.4 0.0 collective-permute-done.got_ref
  6.4 0.0 copy-start.2
  6.4 0.6 copy-done.2
  7.0 3.4 %prepare.1 = (f32[8,768]{1,0:T(8,128)}, bf16[768,768]{1,0:T(8,128)(2,1)}, bf16[16,768]{1,0:T(8,128)(2,1)}, bf16[256,768]{1,0:T(8,128)(2,1)}, s32[8,128]{1,0:T(8,128)}, /*index=5*/s32[8,128]{1,0:T(8,128)}) custom-call(s32[2,3]{1,0:T(2,128)} %length_ref.1, s32[4,48]{1,0:T(4,128)} %get-tuple-element.80.kept_ref, s32[4,48]{1,0:T(4,128)} %copy-done.2, ...), custom_call_target="tpu_custom_call" | custom-call | tf_op jit(solution)/shard_map/prepare/pallas_call | solution.py:218
  10.4 316.1 %layers.1 = (bf16[2,1024,768]{2,1,0:T(8,128)(2,1)}, bf16[2,1024,768]{2,1,0:T(8,128)(2,1)}, f32[2,192,1408]{2,1,0:T(8,128)}, f32[8,768]{1,0:T(8,128)}, bf16[768,7...) custom-call(s32[8,128]{1,0:T(8,128)} %get-tuple-element.33.refs_0_, ...), custom_call_target="tpu_custom_call" | custom-call | tf_op jit(solution)/shard_map/layers/pallas_call | solution.py:1559
  326.5 0.0 copy-start
  326.5 1.6 copy-done
  328.1 1.5 unpack.1
  329.6 0.7 copy.36
  330.3 1.1 copy.37
  331.4 0.0 copy-start.1
  331.4 3.9 %copy.42 = bf16[1,2,1024,768]{3,2,1,0:T(8,128)(2,1)} copy(bf16[1,2,1024,768]{3,2,1,0:T(8,128)(2,1)} %bitcast.35) | data formatting | bytes 6291456
  335.3 0.0 copy-done.1
  335.3 1.7 copy.43
  (1 shorter events, 0.0 us)
Async XLA Ops:
  2.1 4.3 %collective-permute-start = (s32[4,48]{1,0:T(4,128)S(1)}, s32[4,48]{1,0:T(4,128)S(1)}, u32[]{:S(2)}, u32[]{:S(2)}) collective-permute-start(s32[4,48]{1,0:T(4,128)S(1)} %get-tuple-element.79), channel_id=1, source_target_pairs={{0,16},{16,0},{1,17},{17,1},{2,18},{18,2},{3,19},{19,3},{4,20},{20... | collective-permute-start | bytes 2312 | tf_op jit(solution)/shard_map/ppermute | solution.py:1634
  6.4 0.6 copy-start.2
  326.5 1.6 copy-start
  331.4 3.9 %copy-start.1 = (bf16[2,1024,768]{2,1,0:T(8,128)(2,1)S(1)}, bf16[2,1024,768]{2,1,0:T(8,128)(2,1)}, u32[]{:S(2)}) copy-start(bf16[2,1024,768]{2,1,0:T(8,128)(2,1)} %get-tuple-element.40) | copy-start | bytes 9437188

commit v7 on v6

--- a/solution.py
+++ b/solution.py
@@ -133,7 +133,7 @@
     vec_ref[6:7, :] = bup_ref[...].astype(F32)
     vec_ref[7:8, :] = bdn_ref[...].astype(F32)
     unit = (grid_of((16, z.heads), 0) == grid_of((16, z.heads), 1)).astype(F32).astype(BF)
-    swt_ref[...] = nt(unit, sw_ref[...]).astype(BF)
+    swt_ref[...] = nn(unit, sw_ref[...]).astype(BF)
     wo_ref[0:inner, :] = wout_ref[...]
     wo_ref[inner:, :] = jnp.zeros((2 * LANES - inner, z.width), BF)
 
@@ -1579,14 +1579,26 @@
 )
 
 
-def unpack_kernel(z, head, total_ref, *refs):
-    out = Refs(UNPACKED, refs)
+def unpack_kernel(z, head, total_ref, out_any, grad_any, *refs):
+    count = len(UNPACKED)
+    out, rows_out, buffers, sems = Refs(UNPACKED, refs[:count]), refs[count : count + 2], refs[count + 2 : count + 4], refs[-1]
+    loads = [
+        pltpu.make_async_copy(src, buffer, sems.at[i]) for i, (src, buffer) in enumerate(zip((out_any, grad_any), buffers))
+    ]
+    stores = [
+        pltpu.make_async_copy(buffer, dst, sems.at[2 + i]) for i, (buffer, dst) in enumerate(zip(buffers, rows_out))
+    ]
+    for load in loads:
+        load.start()
+    for load, store in zip(loads, stores):
+        load.wait()
+        store.start()
     core = lax.axis_index("section")
     inner, hidden, share = z.heads * head, z.hidden, z.share
     c_o, c_i = hidden, hidden + LANES
     c_s = c_i + z.pad
     out.up[...] = total_ref[1, :, :hidden]
-    out.down[...] = total_ref[0, :, :hidden].T
+    out.down[...] = total_ref[0, :, :hidden]
     first, second = total_ref[0, :, c_o:c_i].T, total_ref[1, :, c_o:c_i].T
     out.out[0:LANES, :] = first
     out.out[LANES:inner, :] = second[: inner - LANES]
@@ -1600,7 +1612,7 @@
     out.input_weight[2, :, LANES:inner] = turned[2][:, :head]
     stats = total_ref[core, :, c_s : c_s + LANES]
     rows = stats.T
-    out.score[...] = pltpu.roll(stats, LANES - 10, 1)[:, : z.heads]
+    out.score[...] = rows[10 : 10 + z.heads]
     each = inner // z.S
     out.input_bias[0:1, :] = rows[13:14, :each]
     out.input_bias[1:2, :] = pltpu.roll(rows[8:16], share - each, 1)[5:6, :each]
@@ -1611,23 +1623,34 @@
     out.gain[1:2, :] = rows[1:2]
     out.shift[0:1, :] = rows[4:5]
     out.shift[1:2, :] = rows[2:3]
-
-
-def unpack(z, head, total):
+    for store in stores:
+        store.wait()
+
+
+def unpack(z, head, total, layer_out, input_grad):
     inner, hidden, share = z.heads * head, z.hidden, z.share
     shapes = (
-        (3, share, inner), (2, inner // z.S), (share, z.heads), (inner, share), (1, share), (share, hidden), (1, share),
-        (hidden, share), (1, share), (2, share), (2, share),
+        (3, share, inner), (2, inner // z.S), (z.heads, share), (inner, share), (1, share), (share, hidden), (1, share),
+        (share, hidden), (1, share), (2, share), (2, share),
     )
     outs = pl.pallas_call(
         functools.partial(unpack_kernel, z, head),
-        out_shape=tuple(jax.ShapeDtypeStruct(shape, F32) for shape in shapes),
-        in_specs=[vmem()],
-        out_specs=tuple(vmem() for _ in shapes),
-        compiler_params=pltpu.CompilerParams(vmem_limit_bytes=LIMIT // 2),
+        out_shape=(
+            *(jax.ShapeDtypeStruct(shape, F32) for shape in shapes),
+            jax.ShapeDtypeStruct(layer_out.shape, BF),
+            jax.ShapeDtypeStruct(input_grad.shape, BF),
+        ),
+        in_specs=[vmem(), anywhere(), anywhere()],
+        out_specs=(*(vmem() for _ in shapes), anywhere(), anywhere()),
+        scratch_shapes=[
+            pltpu.VMEM(layer_out.shape, BF),
+            pltpu.VMEM(input_grad.shape, BF),
+            pltpu.SemaphoreType.DMA((4,)),
+        ],
+        compiler_params=pltpu.CompilerParams(vmem_limit_bytes=LIMIT),
         name="unpack",
-    )(total)
-    return dict(zip(UNPACKED, outs))
+    )(total, layer_out, input_grad)
+    return dict(zip(UNPACKED, outs)), outs[-2], outs[-1]
 
 
 def swapped(value):
@@ -1670,7 +1693,7 @@
         got_choice,
         input_weight[0].transpose(1, 0, 2),
         input_bias[0],
-        score_weight[0],
+        score_weight[0].T,
         output_weight[0],
         output_bias,
         up_bias,
@@ -1680,7 +1703,8 @@
     )
     own |= dict(wup=up_weight[0], wdn=down_weight[0])
     layer_out, input_grad, total = layers(z, routes, tokens, cotangent, own)
-    parts = unpack(z, head, total)
+    parts, layer_out, input_grad = unpack(z, head, total, layer_out, input_grad)
+    parts["down"], parts["score"] = parts["down"].T, parts["score"].T
     parts["input_weight"] = parts["input_weight"].transpose(1, 0, 2)
     return (layer_out[None], input_grad[None], *(part.reshape(1, *shape) for part, shape in (
         (parts["input_weight"], (z.share, 3, inner)),

time: 337 us -> 330 us (0.979)
  local copies, waits for them, and re-layouts: 14.8 us -> 5.6 us
    unnamed x12 -> x4, local copies, waits for them, and re-layouts: 13.3 us -> 4.15 us
    pallas_call x1, Pallas kernels: 1.53 us -> 7.52 us  [unpack(): pl.pallas_call(functools.partial(unpack_kernel, z, head), out_shape=(*(ja...]
    pallas_call x1, Pallas kernels: 316 us -> 313 us  [layers(): pl.pallas_call(functools.partial(layers_kernel, z, tuple(scratch)), out_s...]
where the time goes in v7:
time: 330 us
  Pallas kernels  324 us (98%)
  local copies, waits for them, and re-layouts  5.6 us (2%)
    pallas_call x1, Pallas kernels, layers(): pl.pallas_call(functools.partial(layers_kernel, z, tuple(scratch)), out_s...  313 us
    pallas_call x1, Pallas kernels, unpack(): pl.pallas_call(functools.partial(unpack_kernel, z, head), out_shape=(*(ja...  7.52 us
  transfers between devices with their start and end apart: 1, of which 0 were waited for; matrix products, arithmetic and copies ran while one was open for 1% of the time, Pallas kernels for 0%

profile of v7, /device:TPU:0, one launch (start us, length us, event | category | flops | bytes accessed | tf_op | source)
XLA Modules:
  0.0 330.3 jit_solution(11394913130719293153)
XLA Ops:
  0.6 0.8 reshape_squeeze.3
  1.4 0.1 reshape.53
  1.5 0.6 dynamic-slice_bitcast_fusion
  2.1 0.5 collective-permute-start
  2.6 2.3 copy.32
  4.9 0.0 collective-permute-done.got_ref
  4.9 0.0 copy-start
  4.9 0.6 copy-done
  5.5 3.4 %prepare.1 = (f32[8,768]{1,0:T(8,128)}, bf16[768,768]{1,0:T(8,128)(2,1)}, bf16[16,768]{1,0:T(8,128)(2,1)}, bf16[256,768]{1,0:T(8,128)(2,1)}, s32[8,128]{1,0:T(8,128)}, /*index=5*/s32[8,128]{1,0:T(8,128)}) custom-call(s32[2,3]{1,0:T(2,128)} %length_ref.1, s32[4,48]{1,0:T(4,128)} %get-tuple-element.84.kept_ref, s32[4,48]{1,0:T(4,128)} %copy-done, ...), custom_call_target="tpu_custom_call" | custom-call | tf_op jit(solution)/shard_map/prepare/pallas_call | solution.py:218
  8.9 312.6 %layers.1 = (bf16[2,1024,768]{2,1,0:T(8,128)(2,1)}, bf16[2,1024,768]{2,1,0:T(8,128)(2,1)}, f32[2,192,1408]{2,1,0:T(8,128)}, f32[8,768]{1,0:T(8,128)}, bf16[768,7...) custom-call(s32[8,128]{1,0:T(8,128)} %get-tuple-element.35.refs_0_, ...), custom_call_target="tpu_custom_call" | custom-call | tf_op jit(solution)/shard_map/layers/pallas_call | solution.py:1559
  321.5 7.5 %unpack.1 = (f32[3,192,192]{2,1,0:T(8,128)}, f32[2,48]{1,0:T(2,128)}, f32[3,192]{1,0:T(4,128)}, f32[192,192]{1,0:T(8,128)}, f32[1,192]{1,0:T(1,128)}, /*index=5*...) custom-call(f32[2,192,1408]{2,1,0:T(8,128)} %get-tuple-element.41.to, ...), custom_call_target="tpu_custom_call" | custom-call | tf_op jit(solution)/shard_map/unpack/pallas_call | solution.py:1636
  329.0 1.3 copy.33
  (1 shorter events, 0.0 us)
Async XLA Ops:
  2.1 2.8 collective-permute-start
  4.9 0.6 copy-start

commit v8 on v7

--- a/solution.py
+++ b/solution.py
@@ -1042,6 +1042,14 @@
     s.sum[z.n] = jnp.zeros((TILE, LANES), F32)
     s.gate_sum[z.n] = jnp.zeros((8, LANES), F32)
     ready("st", "w1", "swt", "n1")
+    queries = tn(k.n1[...], s.dqkv[:, : z.pad])
+    lane_full = grid_of((W, LANES), 1)
+    s.pc[1, :, :LANES] = jnp.where(
+        lane_full < TILE, queries[:, :LANES], pltpu.roll(queries[:, LANES : 2 * LANES], TILE, 1)
+    ).astype(BF)
+    s.pc[1, :, LANES : 2 * LANES] = queries[:, 2 * LANES :].astype(BF)
+    s.pc[1, :, 2 * LANES :] = jnp.zeros((W, z.pad - 2 * LANES), BF)
+    reduce(0)
 
     @pl.when(at < last)
     def _():
@@ -1115,16 +1123,11 @@
     done("st", "w1", "swt")
     s.pc[0] = tn(k.n1[...], s.dqkv[:, z.pad :]).astype(BF)
     collects[1].join()
-    queries = tn(k.n1[...], s.dqkv[:, : z.pad])
-    lane_full = grid_of((W, LANES), 1)
-    s.pc[1, :, :LANES] = jnp.where(
-        lane_full < TILE, queries[:, :LANES], pltpu.roll(queries[:, LANES : 2 * LANES], TILE, 1)
-    ).astype(BF)
-    s.pc[1, :, LANES : 2 * LANES] = queries[:, 2 * LANES :].astype(BF)
-    s.pc[1, :, 2 * LANES :] = jnp.zeros((W, z.pad - 2 * LANES), BF)
     give(2).start()
     s.stat[10:13, :] = nn(s.ds[...].astype(BF), k.n1[...])[0:3]
     done("n1")
+    add_up(1)
+    add_up(2)
     source, target = grid_of((W, 1), 0), grid_of((1, W), 1)
     is_value = source >= z.pad
     index = jnp.where(is_value, source - z.pad, source)
@@ -1135,9 +1138,6 @@
     wanted = jnp.where(filled, wanted, -1)
     spread_out = jnp.where(wanted == target, jnp.where(is_value, 1.0, TILE**-0.5), 0.0).astype(BF)
     s.stat[13:14, :] = nn(nn(ones, s.dqkv[...]).astype(BF), spread_out)[0:1]
-    reduce(0)
-    add_up(1)
-    add_up(2)
     grad = collects[1].total(s.own_part[...])
     if layer == 1:
         entry = e.middle[own_rows, :]

time: 330 us -> 331 us (level)
  no operation moved by 1% of the time
where the time goes in v8:
time: 331 us; the launch traced here: 329 us
  Pallas kernels  322 us (97%)
  local copies, waits for them, and re-layouts  5.6 us (2%)
    pallas_call x1, Pallas kernels, layers(): pl.pallas_call(functools.partial(layers_kernel, z, tuple(scratch)), out_s...  311 us
    pallas_call x1, Pallas kernels, unpack(): pl.pallas_call(functools.partial(unpack_kernel, z, head), out_shape=(*(ja...  7.52 us
  transfers between devices with their start and end apart: 1, of which 0 were waited for; matrix products, arithmetic and copies ran while one was open for 1% of the time, Pallas kernels for 0%

profile of v8, /device:TPU:0, one launch (start us, length us, event | category | flops | bytes accessed | tf_op | source)
XLA Modules:
  0.0 328.6 jit_solution(11608371895621967808)
XLA Ops:
  0.6 0.8 reshape_squeeze.3
  1.4 0.1 reshape.53
  1.5 0.6 dynamic-slice_bitcast_fusion
  2.1 0.5 collective-permute-start
  2.6 2.3 copy.32
  4.9 0.0 collective-permute-done.got_ref
  4.9 0.0 copy-start
  4.9 0.6 copy-done
  5.5 3.4 %prepare.1 = (f32[8,768]{1,0:T(8,128)}, bf16[768,768]{1,0:T(8,128)(2,1)}, bf16[16,768]{1,0:T(8,128)(2,1)}, bf16[256,768]{1,0:T(8,128)(2,1)}, s32[8,128]{1,0:T(8,128)}, /*index=5*/s32[8,128]{1,0:T(8,128)}) custom-call(s32[2,3]{1,0:T(2,128)} %length_ref.1, s32[4,48]{1,0:T(4,128)} %get-tuple-element.84.kept_ref, s32[4,48]{1,0:T(4,128)} %copy-done, ...), custom_call_target="tpu_custom_call" | custom-call | tf_op jit(solution)/shard_map/prepare/pallas_call | solution.py:218
  8.9 310.9 %layers.1 = (bf16[2,1024,768]{2,1,0:T(8,128)(2,1)}, bf16[2,1024,768]{2,1,0:T(8,128)(2,1)}, f32[2,192,1408]{2,1,0:T(8,128)}, f32[8,768]{1,0:T(8,128)}, bf16[768,7...) custom-call(s32[8,128]{1,0:T(8,128)} %get-tuple-element.35.refs_0_, ...), custom_call_target="tpu_custom_call" | custom-call | tf_op jit(solution)/shard_map/layers/pallas_call | solution.py:1559
  319.8 7.5 %unpack.1 = (f32[3,192,192]{2,1,0:T(8,128)}, f32[2,48]{1,0:T(2,128)}, f32[3,192]{1,0:T(4,128)}, f32[192,192]{1,0:T(8,128)}, f32[1,192]{1,0:T(1,128)}, /*index=5*...) custom-call(f32[2,192,1408]{2,1,0:T(8,128)} %get-tuple-element.41.to, ...), custom_call_target="tpu_custom_call" | custom-call | tf_op jit(solution)/shard_map/unpack/pallas_call | solution.py:1636
  327.3 1.3 copy.33
  (1 shorter events, 0.0 us)
Async XLA Ops:
  2.1 2.8 collective-permute-start
  4.9 0.6 copy-start
